TPU v7x, 32 devices: a whole 2x2x4 slice. The times are simulated.
32 devices in a mesh: aux: 8 (over y, x, core), pair: 4 (over z).
Axes of the slice: x: 2, y: 2, z: 4, core: 2. Of those that a mesh axis runs over, the one named last changes fastest.
Arguments:
- b_slab: bfloat16 [8192, 8, 4096], P(('aux', 'pair')), may hold values from -6 to 6
- b_rows: bfloat16 [64, 8, 4096], P('aux', 'pair'), may hold values from -0.03125 to 0.03125
- g_occ: bfloat16 [512, 512], P(('aux', 'pair')), may hold values from -0.375 to 0.375
- g_virt: bfloat16 [512, 512], P(('aux', 'pair')), may hold values from -0.375 to 0.375
- pair_index: int32 [2, 8], replicated, may hold values from 0 to 7, as said below
Outputs:
- polar: float32 [8192, 64], P(('aux', 'pair'))
Inputs may be any that keep to these rules, and one draw needn't show every extreme that they name: `pair_index`: no pair block repeats; every block index 0 to 7 is the first block of exactly 1 pair blocks.
All inputs are finite; a program needn't handle non-finite values.
Results may differ from a plain program's by a relative error of at most 0.004.
Values may be sent and summed in bfloat16 or wider, within the bound.
No kernel may reach another device: no remote copies, remote signals or barrier semaphores. Data moves between devices by JAX's collectives and lax.ppermute only.
A program may use at most 192 MiB of HBM per device.

v0:
```python
import jax
import jax.numpy as jnp
from jax import lax
from jax.sharding import PartitionSpec as P

BLK = 64
NB = 8


def block_tables(g_occ, g_virt, pair_index):
    first_block = pair_index[0]
    second_block = pair_index[1]
    occupied = g_occ.reshape(NB, BLK, NB, BLK)[first_block][:, :, first_block]
    virtual = g_virt.reshape(NB, BLK, NB, BLK)[second_block][:, :, second_block]
    return (jnp.transpose(occupied, (0, 2, 1, 3)), jnp.transpose(virtual, (0, 2, 1, 3)))


def project_slab(slab_rows, occ_tables, virt_tables):
    count = slab_rows.shape[0]
    pairs = slab_rows.shape[1]
    slab_tiles = slab_rows.reshape(count, pairs, BLK, BLK)

    def one_target(inputs):
        occ_row, virt_row = inputs
        half_step = jnp.einsum(
            "lac,qlcd->qlad", occ_row, slab_tiles, preferred_element_type=jnp.float32
        ).astype(jnp.bfloat16)
        summed = jnp.einsum(
            "qlad,lbd->qab", half_step, virt_row, preferred_element_type=jnp.float32
        )
        return summed.astype(jnp.bfloat16)

    stacked = lax.map(one_target, (occ_tables, virt_tables))
    return jnp.moveaxis(stacked, 0, 1).reshape(count, pairs * BLK * BLK)


def on_device(b_slab, b_rows, g_occ, g_virt, pair_index):
    occ_full, virt_full = (
        lax.all_gather(g_occ, ("aux", "pair"), axis=0, tiled=True),
        lax.all_gather(g_virt, ("aux", "pair"), axis=0, tiled=True),
    )
    occ_tables, virt_tables = block_tables(occ_full, virt_full, pair_index)
    weighted = project_slab(b_slab, occ_tables, virt_tables)
    pairs = b_slab.shape[1]
    tile_size = b_slab.shape[2]
    across_pairs = lax.all_gather(b_rows, "pair", axis=1, tiled=True)
    shard_rows = lax.all_gather(across_pairs, "aux", axis=0, tiled=True)
    flattened = shard_rows.reshape(shard_rows.shape[0], pairs * tile_size)
    return jnp.einsum("qx,px->qp", weighted, flattened, preferred_element_type=jnp.float32)


def solution(mesh):
    placed = (
        P(("aux", "pair"), None, None),
        P("aux", "pair", None),
        P(("aux", "pair"), None),
        P(("aux", "pair"), None),
        P(),
    )
    return jax.shard_map(
        on_device, mesh=mesh, in_specs=placed, out_specs=P(("aux", "pair"), None), check_vma=False
    )
```

profile of v0, /device:TPU:0, one launch (start us, length us, event | category | flops | bytes accessed | tf_op | source)
XLA Modules:
  0.0 456.5 jit_solution(3287583230631359413)
XLA Ops:
  7.5 17.4 %all_gather.14 = bf16[8,8,4096]{2,0,1:T(8,128)(2,1)S(1)} all-gather(bf16[8,2,4096]{2,0,1:T(8,128)(2,1)S(1)} %copy.24), channel_id=1, replica_groups=mesh['aux'=8,'pair'=4] {'pair'}, dimensions={1}, use_global_device_ids=true | all-gather | bytes 655360 | tf_op jit(solution)/shard_map/all_gather | solution.py:46
  26.8 70.7 %all_gather.12 = bf16[512,512]{1,0:T(8,128)(2,1)S(1)} all-gather(bf16[16,512]{1,0:T(8,128)(2,1)} %param.9), channel_id=1, replica_groups=mesh['aux'=8,'pair'=4] {'aux','pair'}, dimensions={0}, use_global_device_ids=true | all-gather | bytes 540672 | tf_op jit(solution)/shard_map/all_gather | solution.py:39
  99.8 68.2 %all_gather.13 = bf16[512,512]{1,0:T(8,128)(2,1)S(1)} all-gather(bf16[16,512]{1,0:T(8,128)(2,1)} %param.10), channel_id=1, replica_groups=mesh['aux'=8,'pair'=4] {'aux','pair'}, dimensions={0}, use_global_device_ids=true | all-gather | bytes 540672 | tf_op jit(solution)/shard_map/all_gather | solution.py:40
  170.4 22.4 %copy.19 = bf16[256,8,4096]{0,2,1:T(8,128)(2,1)} copy(bf16[256,8,4096]{2,1,0:T(8,128)(2,1)} %param.7) | data formatting | bytes 33554432 | tf_op args[0]
  192.7 17.8 %copy.22 = bf16[256,8,64,64]{0,2,3,1:T(8,128)(2,1)} copy(bf16[256,8,64,64]{0,3,2,1:T(8,128)(2,1)} %bitcast.54) | data formatting | bytes 33554432 | tf_op jit(solution)/shard_map/while | solution.py:33
  210.6 225.2 %while.10 = (s32[]{:T(128)}, bf16[8,256,64,64]{1,3,2,0:T(8,128)(2,1)}, bf16[8,8,64,64]{3,2,0,1:T(8,128)(2,1)S(1)}, bf16[256,8,64,64]{0,2,3,1:T(8,128)(2,1)}, bf16[8,8,64,64]{3,2,0,1:T(8,128)(2,1)S(1)}, /*index=5*/s32[]{:T(128)}) while((s32[]{:T(128)}, bf16[8,256,64,64]{1,3,2,0:T(8,128)(2,1)}, bf16[8,8,64,64]{3,2,0,1:T(8,128)(2,1)S(1)}, ...), condition=%wide.region_1.2_spmd, body=%wide.region_0.1_spmd.sunk | while | flops 2156920832 | bytes 52692040 | solution.py:33
  210.6 11.4 %convert_bitcast_fusion.2 = bf16[256,8,64,64]{0,2,3,1:T(8,128)(2,1)} fusion(bf16[256,8,64,64]{0,2,3,1:T(8,128)(2,1)} %get-tuple-element.106, bf16[8,8,64,64]{3,2,0,1:T(8,128)(2,1)S(1)} %get-tuple-element.105, s32[]{:T(128)} %get-tuple-element.97), kind=kOutput, calls=%fused_computation.6.clone.1 | convolution fusion | flops 1082130432 | bytes 33685508 | tf_op jit(solution)/shard_map/while/body/eval_jaxpr/lac,qlcd->qlad/dot_general | solution.py:25
  222.0 16.7 %bitcast_dynamic-update-slice_fusion.2 = bf16[8,256,64,64]{1,3,2,0:T(8,128)(2,1)} fusion(bf16[8,256,64,64]{1,3,2,0:T(8,128)(2,1)} %get-tuple-element.98, s32[]{:T(128)} %get-tuple-element.97, bf16[256,8,64,64]{0,2,3,1:T(8,128)(2,1)} %convert_bitcast_fusion.2, bf16[8,8,64,64]{3,2,0,1:T(8,128)(2,1)S(1)} %get-tuple-element.107), kind=kOutput, calls=%fused_computation.8.clone.1 | convolution fusion | flops 1074790400 | bytes 19006464 | tf_op jit(solution)/shard_map/while/body/eval_jaxpr/qlad,lbd->qab/dot_general | solution.py:28
  238.7 11.4 %convert_bitcast_fusion.2 = bf16[256,8,64,64]{0,2,3,1:T(8,128)(2,1)} fusion(bf16[256,8,64,64]{0,2,3,1:T(8,128)(2,1)} %get-tuple-element.106, bf16[8,8,64,64]{3,2,0,1:T(8,128)(2,1)S(1)} %get-tuple-element.105, s32[]{:T(128)} %get-tuple-element.97), kind=kOutput, calls=%fused_computation.6.clone.1 | convolution fusion | flops 1082130432 | bytes 33685508 | tf_op jit(solution)/shard_map/while/body/eval_jaxpr/lac,qlcd->qlad/dot_general | solution.py:25
  250.1 16.7 %bitcast_dynamic-update-slice_fusion.2 = bf16[8,256,64,64]{1,3,2,0:T(8,128)(2,1)} fusion(bf16[8,256,64,64]{1,3,2,0:T(8,128)(2,1)} %get-tuple-element.98, s32[]{:T(128)} %get-tuple-element.97, bf16[256,8,64,64]{0,2,3,1:T(8,128)(2,1)} %convert_bitcast_fusion.2, bf16[8,8,64,64]{3,2,0,1:T(8,128)(2,1)S(1)} %get-tuple-element.107), kind=kOutput, calls=%fused_computation.8.clone.1 | convolution fusion | flops 1074790400 | bytes 19006464 | tf_op jit(solution)/shard_map/while/body/eval_jaxpr/qlad,lbd->qab/dot_general | solution.py:28
  266.8 11.4 %convert_bitcast_fusion.2 = bf16[256,8,64,64]{0,2,3,1:T(8,128)(2,1)} fusion(bf16[256,8,64,64]{0,2,3,1:T(8,128)(2,1)} %get-tuple-element.106, bf16[8,8,64,64]{3,2,0,1:T(8,128)(2,1)S(1)} %get-tuple-element.105, s32[]{:T(128)} %get-tuple-element.97), kind=kOutput, calls=%fused_computation.6.clone.1 | convolution fusion | flops 1082130432 | bytes 33685508 | tf_op jit(solution)/shard_map/while/body/eval_jaxpr/lac,qlcd->qlad/dot_general | solution.py:25
  278.3 16.7 %bitcast_dynamic-update-slice_fusion.2 = bf16[8,256,64,64]{1,3,2,0:T(8,128)(2,1)} fusion(bf16[8,256,64,64]{1,3,2,0:T(8,128)(2,1)} %get-tuple-element.98, s32[]{:T(128)} %get-tuple-element.97, bf16[256,8,64,64]{0,2,3,1:T(8,128)(2,1)} %convert_bitcast_fusion.2, bf16[8,8,64,64]{3,2,0,1:T(8,128)(2,1)S(1)} %get-tuple-element.107), kind=kOutput, calls=%fused_computation.8.clone.1 | convolution fusion | flops 1074790400 | bytes 19006464 | tf_op jit(solution)/shard_map/while/body/eval_jaxpr/qlad,lbd->qab/dot_general | solution.py:28
  295.0 11.4 %convert_bitcast_fusion.2 = bf16[256,8,64,64]{0,2,3,1:T(8,128)(2,1)} fusion(bf16[256,8,64,64]{0,2,3,1:T(8,128)(2,1)} %get-tuple-element.106, bf16[8,8,64,64]{3,2,0,1:T(8,128)(2,1)S(1)} %get-tuple-element.105, s32[]{:T(128)} %get-tuple-element.97), kind=kOutput, calls=%fused_computation.6.clone.1 | convolution fusion | flops 1082130432 | bytes 33685508 | tf_op jit(solution)/shard_map/while/body/eval_jaxpr/lac,qlcd->qlad/dot_general | solution.py:25
  306.4 16.7 %bitcast_dynamic-update-slice_fusion.2 = bf16[8,256,64,64]{1,3,2,0:T(8,128)(2,1)} fusion(bf16[8,256,64,64]{1,3,2,0:T(8,128)(2,1)} %get-tuple-element.98, s32[]{:T(128)} %get-tuple-element.97, bf16[256,8,64,64]{0,2,3,1:T(8,128)(2,1)} %convert_bitcast_fusion.2, bf16[8,8,64,64]{3,2,0,1:T(8,128)(2,1)S(1)} %get-tuple-element.107), kind=kOutput, calls=%fused_computation.8.clone.1 | convolution fusion | flops 1074790400 | bytes 19006464 | tf_op jit(solution)/shard_map/while/body/eval_jaxpr/qlad,lbd->qab/dot_general | solution.py:28
  323.2 11.4 %convert_bitcast_fusion.2 = bf16[256,8,64,64]{0,2,3,1:T(8,128)(2,1)} fusion(bf16[256,8,64,64]{0,2,3,1:T(8,128)(2,1)} %get-tuple-element.106, bf16[8,8,64,64]{3,2,0,1:T(8,128)(2,1)S(1)} %get-tuple-element.105, s32[]{:T(128)} %get-tuple-element.97), kind=kOutput, calls=%fused_computation.6.clone.1 | convolution fusion | flops 1082130432 | bytes 33685508 | tf_op jit(solution)/shard_map/while/body/eval_jaxpr/lac,qlcd->qlad/dot_general | solution.py:25
  334.6 16.8 %bitcast_dynamic-update-slice_fusion.2 = bf16[8,256,64,64]{1,3,2,0:T(8,128)(2,1)} fusion(bf16[8,256,64,64]{1,3,2,0:T(8,128)(2,1)} %get-tuple-element.98, s32[]{:T(128)} %get-tuple-element.97, bf16[256,8,64,64]{0,2,3,1:T(8,128)(2,1)} %convert_bitcast_fusion.2, bf16[8,8,64,64]{3,2,0,1:T(8,128)(2,1)S(1)} %get-tuple-element.107), kind=kOutput, calls=%fused_computation.8.clone.1 | convolution fusion | flops 1074790400 | bytes 19006464 | tf_op jit(solution)/shard_map/while/body/eval_jaxpr/qlad,lbd->qab/dot_general | solution.py:28
  351.4 11.4 %convert_bitcast_fusion.2 = bf16[256,8,64,64]{0,2,3,1:T(8,128)(2,1)} fusion(bf16[256,8,64,64]{0,2,3,1:T(8,128)(2,1)} %get-tuple-element.106, bf16[8,8,64,64]{3,2,0,1:T(8,128)(2,1)S(1)} %get-tuple-element.105, s32[]{:T(128)} %get-tuple-element.97), kind=kOutput, calls=%fused_computation.6.clone.1 | convolution fusion | flops 1082130432 | bytes 33685508 | tf_op jit(solution)/shard_map/while/body/eval_jaxpr/lac,qlcd->qlad/dot_general | solution.py:25
  362.8 16.7 %bitcast_dynamic-update-slice_fusion.2 = bf16[8,256,64,64]{1,3,2,0:T(8,128)(2,1)} fusion(bf16[8,256,64,64]{1,3,2,0:T(8,128)(2,1)} %get-tuple-element.98, s32[]{:T(128)} %get-tuple-element.97, bf16[256,8,64,64]{0,2,3,1:T(8,128)(2,1)} %convert_bitcast_fusion.2, bf16[8,8,64,64]{3,2,0,1:T(8,128)(2,1)S(1)} %get-tuple-element.107), kind=kOutput, calls=%fused_computation.8.clone.1 | convolution fusion | flops 1074790400 | bytes 19006464 | tf_op jit(solution)/shard_map/while/body/eval_jaxpr/qlad,lbd->qab/dot_general | solution.py:28
  379.5 11.4 %convert_bitcast_fusion.2 = bf16[256,8,64,64]{0,2,3,1:T(8,128)(2,1)} fusion(bf16[256,8,64,64]{0,2,3,1:T(8,128)(2,1)} %get-tuple-element.106, bf16[8,8,64,64]{3,2,0,1:T(8,128)(2,1)S(1)} %get-tuple-element.105, s32[]{:T(128)} %get-tuple-element.97), kind=kOutput, calls=%fused_computation.6.clone.1 | convolution fusion | flops 1082130432 | bytes 33685508 | tf_op jit(solution)/shard_map/while/body/eval_jaxpr/lac,qlcd->qlad/dot_general | solution.py:25
  390.9 16.8 %bitcast_dynamic-update-slice_fusion.2 = bf16[8,256,64,64]{1,3,2,0:T(8,128)(2,1)} fusion(bf16[8,256,64,64]{1,3,2,0:T(8,128)(2,1)} %get-tuple-element.98, s32[]{:T(128)} %get-tuple-element.97, bf16[256,8,64,64]{0,2,3,1:T(8,128)(2,1)} %convert_bitcast_fusion.2, bf16[8,8,64,64]{3,2,0,1:T(8,128)(2,1)S(1)} %get-tuple-element.107), kind=kOutput, calls=%fused_computation.8.clone.1 | convolution fusion | flops 1074790400 | bytes 19006464 | tf_op jit(solution)/shard_map/while/body/eval_jaxpr/qlad,lbd->qab/dot_general | solution.py:28
  407.7 11.4 %convert_bitcast_fusion.2 = bf16[256,8,64,64]{0,2,3,1:T(8,128)(2,1)} fusion(bf16[256,8,64,64]{0,2,3,1:T(8,128)(2,1)} %get-tuple-element.106, bf16[8,8,64,64]{3,2,0,1:T(8,128)(2,1)S(1)} %get-tuple-element.105, s32[]{:T(128)} %get-tuple-element.97), kind=kOutput, calls=%fused_computation.6.clone.1 | convolution fusion | flops 1082130432 | bytes 33685508 | tf_op jit(solution)/shard_map/while/body/eval_jaxpr/lac,qlcd->qlad/dot_general | solution.py:25
  419.1 16.7 %bitcast_dynamic-update-slice_fusion.2 = bf16[8,256,64,64]{1,3,2,0:T(8,128)(2,1)} fusion(bf16[8,256,64,64]{1,3,2,0:T(8,128)(2,1)} %get-tuple-element.98, s32[]{:T(128)} %get-tuple-element.97, bf16[256,8,64,64]{0,2,3,1:T(8,128)(2,1)} %convert_bitcast_fusion.2, bf16[8,8,64,64]{3,2,0,1:T(8,128)(2,1)S(1)} %get-tuple-element.107), kind=kOutput, calls=%fused_computation.8.clone.1 | convolution fusion | flops 1074790400 | bytes 19006464 | tf_op jit(solution)/shard_map/while/body/eval_jaxpr/qlad,lbd->qab/dot_general | solution.py:28
  435.8 4.6 copy.30
  440.4 9.3 %fusion.14 = f32[256,64]{0,1:T(8,128)} fusion(bf16[64,32768]{1,0:T(8,128)(2,1)S(1)} %bitcast.56, bf16[256,32768]{0,1:T(8,128)(2,1)} %bitcast.55), kind=kOutput, calls=%fused_computation.21 | convolution fusion | flops 1073741824 | bytes 21037056 | tf_op jit(solution)/shard_map/qx,px->qp/dot_general | solution.py:49
  (17 shorter events, 7.5 us)
Async XLA Ops:
  6.5 429.3 %all-gather.2.cloned.1.call-start = ((), (), s32[]{:S(2)}) async-start(), calls=%async_computation | async-start | bytes 4718592 | tf_op jit(solution)/shard_map/all_gather | solution.py:47
Sparse Core Ops, SparseCore 0:
  26.1 38.9 all-gather.1
where the time goes:
time: 458 us; the launch traced here: 456 us
  matrix products  234 us (51%)
  blocking collectives  156 us (34%)
  local copies, waits for them, and re-layouts  51.4 us (11%)
  between operations  13.5 us (3%)
    dot_general x8, matrix products, one_target(): jnp.einsum('qlad,lbd->qab', half_step, virt_row, preferred_element_type=j...  134 us
    dot_general x8, matrix products, one_target(): jnp.einsum('lac,qlcd->qlad', occ_row, slab_tiles, preferred_element_type=...  91.3 us
    all_gather x1, blocking collectives, on_device(): lax.all_gather(g_occ, ('aux', 'pair'), axis=0, tiled=True)  70.7 us
    all_gather x1, blocking collectives, on_device(): lax.all_gather(g_virt, ('aux', 'pair'), axis=0, tiled=True)  68.2 us
    unnamed x3, local copies, waits for them, and re-layouts  27.9 us
    while x1, local copies, waits for them, and re-layouts, project_slab(): stacked = lax.map(one_target, (occ_tables, virt_tables))  17.8 us
    all_gather x1, blocking collectives, on_device(): across_pairs = lax.all_gather(b_rows, 'pair', axis=1, tiled=True)  17.4 us
    dot_general x1, matrix products, on_device(): jnp.einsum('qx,px->qp', weighted, flattened, preferred_element_type=jnp.f...  9.25 us
  transfers between devices with their start and end apart: 1, of which 0 were waited for; matrix products, arithmetic and copies ran while one was open for 59% of the time, Pallas kernels for 0%

commit v1 on v0

v1 whole, which is shorter than its diff:
```python
import functools

import jax
import jax.numpy as jnp
from jax import lax
from jax.experimental import pallas as pl
from jax.experimental.pallas import tpu as pltpu
from jax.sharding import PartitionSpec as P

BLK = 64
LANES = 128
PAIRS_HI = BLK * BLK // LANES
F32 = jnp.float32
BF16 = jnp.bfloat16
VMEM_LIMIT = 56 * 1024 * 1024


def swap(value, axis, size, offset):
    return lax.ppermute(value, axis, [(i, i ^ offset) for i in range(size)])


def dot(a, b, dims=(((1,), (0,)), ((), ())), precision=None):
    return lax.dot_general(a, b, dims, preferred_element_type=F32, precision=precision)


NT = (((1,), (1,)), ((), ()))


def tables_kernel(blocks, nz, *refs):
    g_refs = refs[: len(blocks)]
    row_id, occ_row, occ_col, virt_row, virt_col, occ_out, virt_out, occ_g, virt_g = refs[len(blocks) :]
    place = 0
    strip = g_refs[0].shape[2] // 8
    for ref in g_refs:
        for d in range(ref.shape[0]):
            for z in range(ref.shape[1]):
                for group in range(4):
                    base = group * 2 * strip
                    lanes = slice(group * LANES, (group + 1) * LANES)
                    occ_g[place : place + strip, lanes] = ref[d, z, base : base + strip, :]
                    virt_g[place : place + strip, lanes] = ref[d, z, base + strip : base + 2 * strip, :]
                place += strip
    rid = row_id[...]
    one = lambda hit: jnp.where(hit, 1.0, 0.0).astype(BF16)
    nao = occ_g.shape[1]
    picked = dot(one(occ_row[...] == rid), occ_g[...]).astype(BF16)
    col_rows = one(occ_col[...] == lax.broadcasted_iota(jnp.int32, (occ_col.shape[0], nao), 1))
    table = dot(col_rows, picked, NT).astype(BF16)
    half = table.shape[1] // 2
    for l in range(occ_out.shape[0]):
        for a_lo in range(2):
            occ_out[l, a_lo * BLK : (a_lo + 1) * BLK, :] = table[l * BLK : (l + 1) * BLK, a_lo * half : (a_lo + 1) * half]
    cols = one(lax.broadcasted_iota(jnp.int32, (nao, virt_col.shape[1]), 0) == virt_col[...])
    step = 4 * LANES
    for start in range(0, virt_row.shape[0], step):
        picked = dot(one(virt_row[start : start + step, :] == rid), virt_g[...]).astype(BF16)
        full = dot(picked, cols)
        same = (lax.broadcasted_iota(jnp.int32, full.shape, 0) // BLK) % 2 == (
            lax.broadcasted_iota(jnp.int32, full.shape, 1) // BLK
        ) % 2
        virt_out[start : start + step, :] = jnp.where(same, full, 0.0).astype(BF16)


def make_tables(g_blocks, row_id, m_rows, n_rows, m_cols, n_cols):
    nk, nl = m_rows.shape[0], m_cols.shape[0]
    nao = row_id.shape[0]
    ids = lambda *shape: lax.broadcasted_iota(jnp.int32, shape, len(shape) - 1)
    hi = jnp.arange(PAIRS_HI, dtype=jnp.int32) * 2
    lo = jnp.arange(2, dtype=jnp.int32)
    inner = jnp.arange(BLK, dtype=jnp.int32)
    occ_row = (m_rows[None, :, None] * BLK + hi[None, None, :] + lo[:, None, None]).reshape(-1, 1)
    occ_col = (m_cols[:, None, None] * BLK + hi[None, None, :] + lo[None, :, None]).reshape(-1, 1)
    virt_row = (n_rows[:, None, None] * BLK + 0 * lo[None, :, None] + inner[None, None, :]).reshape(-1, 1)
    virt_col = (n_cols[:, None, None] * BLK + 0 * lo[None, :, None] + inner[None, None, :]).reshape(1, -1)
    return pl.pallas_call(
        functools.partial(tables_kernel, g_blocks, None),
        out_shape=(
            jax.ShapeDtypeStruct((nl, 2 * BLK, nk * PAIRS_HI), BF16),
            jax.ShapeDtypeStruct((nk * LANES, nl * LANES), BF16),
        ),
        scratch_shapes=[pltpu.VMEM((nao, nao), BF16), pltpu.VMEM((nao, nao), BF16)],
        compiler_params=pltpu.CompilerParams(vmem_limit_bytes=VMEM_LIMIT),
        name="tables",
    )(*g_blocks, row_id.reshape(1, -1), occ_row, occ_col, virt_row, virt_col)


def transform_kernel(count, *refs):
    b_refs = refs[:count]
    virt, occ, out, x_buf, z_buf = refs[count:]
    nk = b_refs[0].shape[0]
    group = occ.shape[0]
    rows = b_refs[0].shape[1]
    per = rows // PAIRS_HI
    for k in range(nk):
        weights = virt[k * LANES : (k + 1) * LANES, :]
        for e in range(count):
            x = dot(b_refs[e][k], weights).astype(BF16)
            for l in range(group):
                for p in range(per):
                    x_buf[l, k * PAIRS_HI : (k + 1) * PAIRS_HI, (e * per + p) * LANES : (e * per + p + 1) * LANES] = x[
                        p * PAIRS_HI : (p + 1) * PAIRS_HI, l * LANES : (l + 1) * LANES
                    ]
    low = lax.broadcasted_iota(jnp.int32, (PAIRS_HI, LANES), 1) < BLK
    for l in range(group):
        y = dot(occ[l], x_buf[l])
        for p in range(count * per):
            part = y[:, p * LANES : (p + 1) * LANES]
            t0, t2, t1, t3 = (part[i * PAIRS_HI : (i + 1) * PAIRS_HI] for i in range(4))
            z_buf[p, :, :] = jnp.where(low, t0, t3) + pltpu.roll(jnp.where(low, t2, t1), BLK, 1)
        for c in range(PAIRS_HI):
            out[l, :, c * LANES : (c + 1) * LANES] = z_buf[:, c, :].astype(BF16)


def transform(b_blocks, occ, virt):
    nl, nk = occ.shape[0], b_blocks[0].shape[0]
    count = len(b_blocks)
    rows = b_blocks[0].shape[1]
    ps = count * rows // PAIRS_HI
    group = 4
    whole = pl.BlockSpec((nk, rows, LANES), lambda i: (0, 0, 0))
    return pl.pallas_call(
        functools.partial(transform_kernel, count),
        grid=(nl // group,),
        in_specs=[whole] * count
        + [
            pl.BlockSpec((nk * LANES, group * LANES), lambda i: (0, i)),
            pl.BlockSpec((group, 2 * BLK, nk * PAIRS_HI), lambda i: (i, 0, 0)),
        ],
        out_specs=pl.BlockSpec((group, ps, BLK * BLK), lambda i: (i, 0, 0)),
        out_shape=jax.ShapeDtypeStruct((nl, ps, BLK * BLK), BF16),
        scratch_shapes=[
            pltpu.VMEM((group, nk * PAIRS_HI, ps * LANES), BF16),
            pltpu.VMEM((ps, PAIRS_HI, LANES), F32),
        ],
        compiler_params=pltpu.CompilerParams(vmem_limit_bytes=VMEM_LIMIT),
        name="transform",
    )(*b_blocks, virt, occ)


def contract_kernel(pieces, nl, *refs):
    w_refs = refs[:pieces]
    slab, place, out, weights = refs[pieces:]

    @pl.when(pl.program_id(0) == 0)
    def _():
        for i, ref in enumerate(w_refs):
            n = ref.shape[0]
            weights[i * n : (i + 1) * n, :] = ref[...]

    full = dot(slab[...], weights[...], NT)
    per = w_refs[0].shape[0] // nl
    own = (lax.broadcasted_iota(jnp.int32, full.shape, 1) // per) % nl == lax.broadcasted_iota(
        jnp.int32, full.shape, 0
    ) % nl
    kept = jnp.where(own, full, 0.0).reshape(full.shape[0] // nl, nl, full.shape[1])
    summed = jnp.sum(kept, axis=1)
    out[...] = dot(summed, place[...], precision=lax.Precision.HIGHEST)


def contract(slab, w_pieces, place):
    count, nl, tile = slab.shape
    pieces = [w.reshape(-1, tile) for w in w_pieces]
    total = sum(w.shape[0] for w in pieces)
    rows = min(512, count * nl)
    fixed = lambda shape: pl.BlockSpec(shape, lambda i: (0, 0))
    return pl.pallas_call(
        functools.partial(contract_kernel, len(pieces), nl),
        grid=(count * nl // rows,),
        in_specs=[fixed(w.shape) for w in pieces]
        + [pl.BlockSpec((rows, tile), lambda i: (i, 0)), fixed(place.shape)],
        out_specs=pl.BlockSpec((rows // nl, place.shape[1]), lambda i: (i, 0)),
        out_shape=jax.ShapeDtypeStruct((count, place.shape[1]), F32),
        scratch_shapes=[pltpu.VMEM((total, tile), BF16)],
        compiler_params=pltpu.CompilerParams(vmem_limit_bytes=VMEM_LIMIT),
        name="contract",
    )(*pieces, slab.reshape(count * nl, tile), place)


def on_device(na, nz, b_slab, b_rows, g_occ, g_virt, pair_index):
    per, k_local, tile = b_rows.shape
    strip = g_occ.shape[0]
    nl = b_slab.shape[1]
    me_a, me_z = lax.axis_index("aux"), lax.axis_index("pair")
    outer = list(range(0, na, 2))

    b_own = jnp.transpose(b_rows.reshape(per, k_local, PAIRS_HI, LANES), (1, 0, 2, 3)).reshape(-1, LANES)
    g_own = jnp.concatenate([g_occ, g_virt], axis=0)
    g_own = jnp.concatenate([g_own[:, i * LANES : (i + 1) * LANES] for i in range(g_own.shape[1] // LANES)], axis=0)
    packed = jnp.concatenate([b_own, g_own], axis=0)
    column = [packed] + [swap(packed, "pair", nz, d) for d in range(1, nz)]
    b_z = jnp.concatenate([c[: b_own.shape[0]].reshape(k_local, per * PAIRS_HI, LANES) for c in column], axis=0)
    g_z = jnp.stack([c[b_own.shape[0] :] for c in column])

    g_half = jnp.stack([g_z] + [swap(g_z, "aux", na, e) for e in outer[1:]])
    g_other = swap(g_half, "aux", na, 1)
    b_blocks = [b_z]
    if len(outer) == 4:
        b_x, b_y = swap(b_z, "aux", na, 2), swap(b_z, "aux", na, 4)
        mid = b_z.shape[1] // 2
        diagonal = jnp.concatenate(
            [swap(b_x[:, :mid], "aux", na, 4), swap(b_y[:, mid:], "aux", na, 2)], axis=1
        )
        b_blocks += [b_x, b_y, diagonal]
    else:
        b_blocks += [swap(b_z, "aux", na, e) for e in outer[1:]]

    z_of = me_z ^ jnp.arange(nz, dtype=jnp.int32)
    aux_of = me_a ^ jnp.concatenate([jnp.asarray(outer, jnp.int32), jnp.asarray(outer, jnp.int32) + 1])
    row_id = ((aux_of[:, None] * nz + z_of[None, :])[:, :, None] * strip + jnp.arange(strip, dtype=jnp.int32)).reshape(-1)
    k_ids = (z_of[:, None] * k_local + jnp.arange(k_local, dtype=jnp.int32)).reshape(-1)
    first, second = pair_index[0], pair_index[1]
    occ, virt = make_tables([g_half, g_other], row_id, first[k_ids], second[k_ids], first, second)

    pieces = [transform(b_blocks[i : i + 2], occ, virt) for i in range(0, len(outer), 2)]
    others = [swap(w, "aux", na, 1) for w in pieces]

    core = jnp.arange(2, dtype=jnp.int32)[:, None, None, None, None]
    piece = jnp.arange(len(pieces), dtype=jnp.int32)[None, :, None, None, None]
    which = jnp.arange(2, dtype=jnp.int32)[None, None, None, :, None]
    row = jnp.arange(per, dtype=jnp.int32)
    target = (me_a ^ (piece * 4 + which * 2 + core)) * per + row
    target = jnp.broadcast_to(target, (2, len(pieces), nl, 2, per)).reshape(-1, 1)
    place = (target == jnp.arange(na * per, dtype=jnp.int32)).astype(F32)
    return contract(b_slab, pieces + others, place)


def solution(mesh):
    placed = (
        P(("aux", "pair"), None, None),
        P("aux", "pair", None),
        P(("aux", "pair"), None),
        P(("aux", "pair"), None),
        P(),
    )
    return jax.shard_map(
        functools.partial(on_device, mesh.shape["aux"], mesh.shape["pair"]),
        mesh=mesh,
        in_specs=placed,
        out_specs=P(("aux", "pair"), None),
        check_vma=False,
    )
```

time: 458 us -> 94.5 us (0.21)
  matrix products: 234 us -> 0 us
  blocking collectives: 156 us -> 0 us
  local copies, waits for them, and re-layouts: 51.4 us -> 12.8 us
  Pallas kernels: 0 us -> 37.5 us
  waiting for transfers between devices: 0.02 us -> 23.9 us
  starting transfers between devices: 0.01 us -> 15.4 us
  between operations: 13.5 us -> 0.17 us
    dot_general x17 -> x0, matrix products: 234 us -> none  [the longest x8 134 us: one_target(): jnp.einsum('qlad,lbd->qab', half_step, virt_row, preferred_element_type=j...]
    all_gather x3 -> x0, blocking collectives: 156 us -> none  [the longest x1 70.7 us: on_device(): lax.all_gather(g_occ, ('aux', 'pair'), axis=0, tiled=True)]
    pallas_call x0 -> x4, Pallas kernels: none -> 37.5 us  [the longest x2 16.5 us: transform(): pl.pallas_call(functools.partial(transform_kernel, count), grid=(nl // gr...]
    unnamed x3 -> x18, local copies, waits for them, and re-layouts: 27.9 us -> 2.53 us
    ppermute x0 -> x13, waiting for transfers between devices: none -> 23.9 us  [swap(): return lax.ppermute(value, axis, [(i, i ^ offset) for i in range(size)])]
    while x1 -> x0, local copies, waits for them, and re-layouts: 17.8 us -> none  [project_slab(): stacked = lax.map(one_target, (occ_tables, virt_tables))]
    ppermute x0 -> x13, starting transfers between devices: none -> 15.4 us  [swap(): return lax.ppermute(value, axis, [(i, i ^ offset) for i in range(size)])]
    add x0 -> x6, local copies, waits for them, and re-layouts: none -> 4.68 us  [the longest x1 1.31 us: make_tables(): n_rows[:, None, None] * BLK + 0 * lo[None, :, None] + inner[None, None, :]]
  transfers between devices with their start and end apart: 1 -> 13, of which waited for: 0 -> 6; matrix products, arithmetic and copies ran while one was open for 59% -> 12% of each run, Pallas kernels for 0% -> 23%
where the time goes in v1:
time: 94.5 us; the launch traced here: 94.1 us
  Pallas kernels  37.5 us (40%)
  waiting for transfers between devices  23.9 us (25%)
  starting transfers between devices  15.4 us (16%)
  local copies, waits for them, and re-layouts  12.8 us (14%)
  other arithmetic  4.31 us (5%)
    ppermute x13, waiting for transfers between devices, swap(): return lax.ppermute(value, axis, [(i, i ^ offset) for i in range(size)])  23.9 us
    pallas_call x2, Pallas kernels, transform(): pl.pallas_call(functools.partial(transform_kernel, count), grid=(nl // gr...  16.5 us
    pallas_call x1, Pallas kernels, contract(): pl.pallas_call(functools.partial(contract_kernel, len(pieces), nl), grid=...  15.5 us
    ppermute x13, starting transfers between devices, swap(): return lax.ppermute(value, axis, [(i, i ^ offset) for i in range(size)])  15.4 us
    pallas_call x1, Pallas kernels, make_tables(): pl.pallas_call(functools.partial(tables_kernel, g_blocks, None), out_shap...  5.5 us
    unnamed x18, local copies, waits for them, and re-layouts  2.53 us
  transfers between devices with their start and end apart: 13, of which 6 were waited for; matrix products, arithmetic and copies ran while one was open for 12% of the time, Pallas kernels for 23%

profile of v1, /device:TPU:0, one launch (start us, length us, event | category | flops | bytes accessed | tf_op | source)
XLA Modules:
  0.0 94.1 jit_solution(14790130159596993563)
XLA Ops:
  0.7 1.0 %reshape.384 = bf16[8,2,32,128]{3,2,1,0:T(8,128)(2,1)S(1)} reshape(bf16[8,2,4096]{2,1,0:T(2,128)(2,1)} %param.8) | data formatting | bytes 262144 | tf_op jit(solution)/shard_map/reshape | solution.py:186
  2.5 5.1 %collective-permute-start.2 = (bf16[640,128]{1,0:T(8,128)(2,1)S(1)}, bf16[640,128]{1,0:T(8,128)(2,1)S(1)}, u32[]{:S(2)}, u32[]{:S(2)}) collective-permute-start(bf16[640,128]{1,0:T(8,128)(2,1)S(1)} %constant_dynamic-update-slice_fusion.2), channel_id=1, source_target_pairs={{0,3},{1,2},{2,1},{3,0},{4,7},{5,6},{6,5},{7,4},{8,11},{9,10},{10,... | collective-permute-start | bytes 491528 | tf_op jit(solution)/shard_map/ppermute | solution.py:19
  11.6 1.2 %collective-permute-done.2 = bf16[640,128]{1,0:T(8,128)(2,1)S(1)} collective-permute-done((bf16[640,128]{1,0:T(8,128)(2,1)S(1)}, bf16[640,128]{1,0:T(8,128)(2,1)S(1)}, u32[]{:S(2)}, u32[]{:S(2)}) %collective-permute-start.2) | collective-permute-done | bytes 163872 | tf_op jit(solution)/shard_map/ppermute | solution.py:19
  12.8 8.8 %collective-permute-done.1 = bf16[640,128]{1,0:T(8,128)(2,1)S(1)} collective-permute-done((bf16[640,128]{1,0:T(8,128)(2,1)S(1)}, bf16[640,128]{1,0:T(8,128)(2,1)S(1)}, u32[]{:S(2)}, u32[]{:S(2)}) %collective-permute-start.1) | collective-permute-done | bytes 163872 | tf_op jit(solution)/shard_map/ppermute | solution.py:19
  21.6 2.5 %collective-permute-start.6 = (bf16[4,128,128]{2,1,0:T(8,128)(2,1)S(1)}, bf16[4,128,128]{2,1,0:T(8,128)(2,1)S(1)}, u32[]{:S(2)}, u32[]{:S(2)}) collective-permute-start(bf16[4,128,128]{2,1,0:T(8,128)(2,1)S(1)} %get-tuple-element.10), channel_id=1, source_target_pairs={{0,24},{4,28},{8,16},{12,20},{16,8},{20,12},{24,0},{28,4},{1,25},{... | collective-permute-start | bytes 393224 | tf_op jit(solution)/shard_map/ppermute | solution.py:19
  25.3 1.6 %collective-permute-start.3 = (bf16[8,256,128]{2,1,0:T(8,128)(2,1)S(1)}, bf16[8,256,128]{2,1,0:T(8,128)(2,1)S(1)}, u32[]{:S(2)}, u32[]{:S(2)}) collective-permute-start(bf16[8,256,128]{2,1,0:T(8,128)(2,1)S(1)} %pad_maximum_fusion.refs_0_), channel_id=1, source_target_pairs={{0,8},{4,12},{8,0},{12,4},{16,24},{20,28},{24,16},{28,20},{1,9},{5... | collective-permute-start | bytes 1572872 | tf_op jit(solution)/shard_map/ppermute | solution.py:19
  26.8 1.5 %collective-permute-start.8 = (bf16[8,256,128]{2,1,0:T(8,128)(2,1)S(1)}, bf16[8,256,128]{2,1,0:T(8,128)(2,1)S(1)}, u32[]{:S(2)}, u32[]{:S(2)}) collective-permute-start(bf16[8,256,128]{2,1,0:T(8,128)(2,1)S(1)} %pad_maximum_fusion.refs_0_), channel_id=1, source_target_pairs={{0,16},{4,20},{8,24},{12,28},{16,0},{20,4},{24,8},{28,12},{1,17},{... | collective-permute-start | bytes 1572872 | tf_op jit(solution)/shard_map/ppermute | solution.py:19
  28.4 2.5 %collective-permute-done.5 = bf16[4,128,128]{2,1,0:T(8,128)(2,1)S(1)} collective-permute-done((bf16[4,128,128]{2,1,0:T(8,128)(2,1)S(1)}, bf16[4,128,128]{2,1,0:T(8,128)(2,1)S(1)}, u32[]{:S(2)}, u32[]{:S(2)}) %collective-permute-start.5) | collective-permute-done | bytes 131104 | tf_op jit(solution)/shard_map/ppermute | solution.py:19
  30.9 0.8 collective-permute-done.4
  31.9 9.3 %collective-permute-done.8.refs_0_ = bf16[8,256,128]{2,1,0:T(8,128)(2,1)S(1)} collective-permute-done((bf16[8,256,128]{2,1,0:T(8,128)(2,1)S(1)}, bf16[8,256,128]{2,1,0:T(8,128)(2,1)S(1)}, u32[]{:S(2)}, u32[]{:S(2)}) %collective-permute-start.8) | collective-permute-done | bytes 524320 | tf_op jit(solution)/shard_map/ppermute | solution.py:19
  41.2 1.6 %collective-permute-start.10 = (bf16[8,128,128]{2,1,0:T(8,128)(2,1)S(1)}, bf16[8,128,128]{2,1,0:T(8,128)(2,1)S(1)}, u32[]{:S(2)}, u32[]{:S(2)}) collective-permute-start(bf16[8,128,128]{2,1,0:T(8,128)(2,1)S(1)} %slice.71), channel_id=1, source_target_pairs={{0,8},{4,12},{8,0},{12,4},{16,24},{20,28},{24,16},{28,20},{1,9},{5... | collective-permute-start | bytes 786440 | tf_op jit(solution)/shard_map/ppermute | solution.py:19
  42.8 0.9 collective-permute-start.9
  44.4 1.0 %add.291.refs_3_ = s32[512,1]{1,0:T(8,128)} reshape(s32[2,8,32]{2,1,0:T(8,128)S(1)} %iota_add_fusion.4) | data formatting | bytes 4096 | tf_op jit(solution)/shard_map/add | solution.py:71
  45.4 1.0 %add.292.refs_4_ = s32[512,1]{1,0:T(8,128)} reshape(s32[8,2,32]{2,1,0:T(2,128)S(1)} %iota_add_fusion.3) | data formatting | bytes 4096 | tf_op jit(solution)/shard_map/add | solution.py:72
  46.3 1.3 %add.293.refs_5_ = s32[1024,1]{1,0:T(8,128)} reshape(s32[8,2,64]{2,1,0:T(2,128)S(1)} %iota_add_fusion.2) | data formatting | bytes 8192 | tf_op jit(solution)/shard_map/add | solution.py:73
  49.2 5.5 %tables.1 = (bf16[8,128,256]{2,1,0:T(8,128)(2,1)}, bf16[1024,1024]{1,0:T(8,128)(2,1)}) custom-call(bf16[4,4,128,128]{3,2,1,0:T(8,128)(2,1)} %copy-done.1, bf16[4,4,128,128]{3,2,1,0:T(8,128)(2,1)} %copy-done.6, s32[1,512]{1,0:T(1,128)} %add.257.refs_2_, s32[512,1]{1,0:T(8,128)} %add.291.refs_3_, s32[512,1]{1,0:T(8,128)} %add.292.refs_4_, ...), custom_call_target="tpu_custom_call" | custom-call | tf_op jit(solution)/shard_map/tables/pallas_call | solution.py:75
  54.7 8.4 %transform.2 = bf16[8,16,4096]{2,1,0:T(8,128)(2,1)} custom-call(bf16[8,256,128]{2,1,0:T(8,128)(2,1)} %copy-done, bf16[8,256,128]{2,1,0:T(8,128)(2,1)} %copy-done.3, bf16[1024,1024]{1,0:T(8,128)(2,1)} %get-tuple-element.7.refs_2_, bf16[8,128,256]{2,1,0:T(8,128)(2,1)} %get-tuple-element.8.refs_3_), custom_call_target="tpu_custom_call" | custom-call | tf_op jit(solution)/shard_map/transform/pallas_call | solution.py:121
  63.1 1.8 %pad_maximum_fusion.2.refs_1_ = bf16[8,256,128]{2,1,0:T(8,128)(2,1)} fusion(bf16[8,128,128]{2,1,0:T(8,128)(2,1)S(1)} %collective-permute-done.10, bf16[8,128,128]{2,1,0:T(8,128)(2,1)} %collective-permute-done.9), kind=kLoop, calls=%fused_computation.4 | loop fusion | flops 1048576 | bytes 1048576 | tf_op jit(solution)/shard_map/concatenate | solution.py:200
  64.9 8.2 %transform.3 = bf16[8,16,4096]{2,1,0:T(8,128)(2,1)} custom-call(bf16[8,256,128]{2,1,0:T(8,128)(2,1)} %copy-done.2, bf16[8,256,128]{2,1,0:T(8,128)(2,1)} %pad_maximum_fusion.2.refs_1_, bf16[1024,1024]{1,0:T(8,128)(2,1)} %get-tuple-element.7.refs_2_, bf16[8,128,256]{2,1,0:T(8,128)(2,1)} %get-tuple-element.8.refs_3_), custom_call_target="tpu_custom_call" | custom-call | tf_op jit(solution)/shard_map/transform/pallas_call | solution.py:121
  73.8 0.8 fusion.refs_5_
  74.7 1.4 %collective-permute-done.12 = bf16[8,16,4096]{2,1,0:T(8,128)(2,1)S(1)} collective-permute-done((bf16[8,16,4096]{2,1,0:T(8,128)(2,1)}, bf16[8,16,4096]{2,1,0:T(8,128)(2,1)S(1)}, u32[]{:S(2)}, u32[]{:S(2)}) %collective-permute-start.12) | collective-permute-done | bytes 1048608 | tf_op jit(solution)/shard_map/ppermute | solution.py:19
  76.1 1.0 %copy-done.5 = bf16[8,16,4096]{2,1,0:T(8,128)(2,1)} copy-done((bf16[8,16,4096]{2,1,0:T(8,128)(2,1)}, bf16[8,16,4096]{2,1,0:T(8,128)(2,1)S(1)}, u32[]{:S(2)}) %copy-start.5) | copy-done | bytes 1048600
  77.0 15.5 %contract.1 = f32[256,64]{1,0:T(8,128)} custom-call(bf16[128,4096]{1,0:T(8,128)(2,1)} %bitcast.37, bf16[128,4096]{1,0:T(8,128)(2,1)} %bitcast.38, bf16[128,4096]{1,0:T(8,128)(2,1)} %bitcast.41, bf16[128,4096]{1,0:T(8,128)(2,1)} %bitcast.42, bf16[2048,4096]{1,0:T(8,128)(2,1)} %bitcast.36, f32[512,64]{1,0:T(8,128)} %fusion.refs_5_), custom_call_target="tpu_custom_call" | custom-call | tf_op jit(solution)/shard_map/contract/pallas_call | solution.py:166
  92.5 1.6 %copy.14 = f32[256,64]{0,1:T(8,128)} copy(f32[256,64]{1,0:T(8,128)} %contract.1) | data formatting | bytes 131072 | tf_op jit(solution)/shard_map/contract/pallas_call | solution.py:166
  (76 shorter events, 9.9 us)
Async XLA Ops:
  2.5 10.2 %collective-permute-start.2 = (bf16[640,128]{1,0:T(8,128)(2,1)S(1)}, bf16[640,128]{1,0:T(8,128)(2,1)S(1)}, u32[]{:S(2)}, u32[]{:S(2)}) collective-permute-start(bf16[640,128]{1,0:T(8,128)(2,1)S(1)} %constant_dynamic-update-slice_fusion.2), channel_id=1, source_target_pairs={{0,3},{1,2},{2,1},{3,0},{4,7},{5,6},{6,5},{7,4},{8,11},{9,10},{10,... | collective-permute-start | bytes 491528 | tf_op jit(solution)/shard_map/ppermute | solution.py:19
  7.7 13.9 %collective-permute-start.1 = (bf16[640,128]{1,0:T(8,128)(2,1)S(1)}, bf16[640,128]{1,0:T(8,128)(2,1)S(1)}, u32[]{:S(2)}, u32[]{:S(2)}) collective-permute-start(bf16[640,128]{1,0:T(8,128)(2,1)S(1)} %constant_dynamic-update-slice_fusion.2), channel_id=1, source_target_pairs={{0,2},{1,3},{2,0},{3,1},{4,6},{5,7},{6,4},{7,5},{8,10},{9,11},{10,... | collective-permute-start | bytes 491528 | tf_op jit(solution)/shard_map/ppermute | solution.py:19
  7.7 13.9 %collective-permute-start = (bf16[640,128]{1,0:T(8,128)(2,1)S(1)}, bf16[640,128]{1,0:T(8,128)(2,1)S(1)}, u32[]{:S(2)}, u32[]{:S(2)}) collective-permute-start(bf16[640,128]{1,0:T(8,128)(2,1)S(1)} %constant_dynamic-update-slice_fusion.2), channel_id=1, source_target_pairs={{0,1},{1,0},{2,3},{3,2},{4,5},{5,4},{6,7},{7,6},{8,9},{9,8},{10,11... | collective-permute-start | bytes 491528 | tf_op jit(solution)/shard_map/ppermute | solution.py:19
  21.6 6.8 %collective-permute-start.6 = (bf16[4,128,128]{2,1,0:T(8,128)(2,1)S(1)}, bf16[4,128,128]{2,1,0:T(8,128)(2,1)S(1)}, u32[]{:S(2)}, u32[]{:S(2)}) collective-permute-start(bf16[4,128,128]{2,1,0:T(8,128)(2,1)S(1)} %get-tuple-element.10), channel_id=1, source_target_pairs={{0,24},{4,28},{8,16},{12,20},{16,8},{20,12},{24,0},{28,4},{1,25},{... | collective-permute-start | bytes 393224 | tf_op jit(solution)/shard_map/ppermute | solution.py:19
  24.1 6.8 %collective-permute-start.5 = (bf16[4,128,128]{2,1,0:T(8,128)(2,1)S(1)}, bf16[4,128,128]{2,1,0:T(8,128)(2,1)S(1)}, u32[]{:S(2)}, u32[]{:S(2)}) collective-permute-start(bf16[4,128,128]{2,1,0:T(8,128)(2,1)S(1)} %get-tuple-element.10), channel_id=1, source_target_pairs={{0,16},{4,20},{8,24},{12,28},{16,0},{20,4},{24,8},{28,12},{1,17},{... | collective-permute-start | bytes 393224 | tf_op jit(solution)/shard_map/ppermute | solution.py:19
  24.6 7.1 %collective-permute-start.4 = (bf16[4,128,128]{2,1,0:T(8,128)(2,1)S(1)}, bf16[4,128,128]{2,1,0:T(8,128)(2,1)S(1)}, u32[]{:S(2)}, u32[]{:S(2)}) collective-permute-start(bf16[4,128,128]{2,1,0:T(8,128)(2,1)S(1)} %get-tuple-element.10), channel_id=1, source_target_pairs={{0,8},{4,12},{8,0},{12,4},{16,24},{20,28},{24,16},{28,20},{1,9},{5... | collective-permute-start | bytes 393224 | tf_op jit(solution)/shard_map/ppermute | solution.py:19
  25.3 29.4 %copy-start = (bf16[8,256,128]{2,1,0:T(8,128)(2,1)}, bf16[8,256,128]{2,1,0:T(8,128)(2,1)S(1)}, u32[]{:S(2)}) copy-start(bf16[8,256,128]{2,1,0:T(8,128)(2,1)S(1)} %pad_maximum_fusion.refs_0_) | copy-start | bytes 1572868
  25.3 17.5 %collective-permute-start.3 = (bf16[8,256,128]{2,1,0:T(8,128)(2,1)S(1)}, bf16[8,256,128]{2,1,0:T(8,128)(2,1)S(1)}, u32[]{:S(2)}, u32[]{:S(2)}) collective-permute-start(bf16[8,256,128]{2,1,0:T(8,128)(2,1)S(1)} %pad_maximum_fusion.refs_0_), channel_id=1, source_target_pairs={{0,8},{4,12},{8,0},{12,4},{16,24},{20,28},{24,16},{28,20},{1,9},{5... | collective-permute-start | bytes 1572872 | tf_op jit(solution)/shard_map/ppermute | solution.py:19
  26.8 14.3 %collective-permute-start.8 = (bf16[8,256,128]{2,1,0:T(8,128)(2,1)S(1)}, bf16[8,256,128]{2,1,0:T(8,128)(2,1)S(1)}, u32[]{:S(2)}, u32[]{:S(2)}) collective-permute-start(bf16[8,256,128]{2,1,0:T(8,128)(2,1)S(1)} %pad_maximum_fusion.refs_0_), channel_id=1, source_target_pairs={{0,16},{4,20},{8,24},{12,28},{16,0},{20,4},{24,8},{28,12},{1,17},{... | collective-permute-start | bytes 1572872 | tf_op jit(solution)/shard_map/ppermute | solution.py:19
  31.8 16.6 %copy-start.1 = (bf16[4,4,128,128]{3,2,1,0:T(8,128)(2,1)}, bf16[4,4,128,128]{3,2,1,0:T(8,128)(2,1)S(1)}, u32[]{:S(2)}) copy-start(bf16[4,4,128,128]{3,2,1,0:T(8,128)(2,1)S(1)} %pad_maximum_fusion.1.refs_0_) | copy-start | bytes 1572868
  31.8 16.6 %collective-permute-start.7 = (bf16[4,4,128,128]{3,2,1,0:T(8,128)(2,1)S(1)}, bf16[4,4,128,128]{3,2,1,0:T(8,128)(2,1)S(1)}, u32[]{:S(2)}, u32[]{:S(2)}) collective-permute-start(bf16[4,4,128,128]{3,2,1,0:T(8,128)(2,1)S(1)} %pad_maximum_fusion.1.refs_0_), channel_id=1, source_target_pairs={{0,4},{4,0},{8,12},{12,8},{16,20},{20,16},{24,28},{28,24},{1,5},{5... | collective-permute-start | bytes 1572872 | tf_op jit(solution)/shard_map/ppermute | solution.py:19
  41.2 23.8 %copy-start.2 = (bf16[8,256,128]{2,1,0:T(8,128)(2,1)}, bf16[8,256,128]{2,1,0:T(8,128)(2,1)S(1)}, u32[]{:S(2)}) copy-start(bf16[8,256,128]{2,1,0:T(8,128)(2,1)S(1)} %collective-permute-done.8.refs_0_) | copy-start | bytes 1572868
  41.2 21.9 %collective-permute-start.10 = (bf16[8,128,128]{2,1,0:T(8,128)(2,1)S(1)}, bf16[8,128,128]{2,1,0:T(8,128)(2,1)S(1)}, u32[]{:S(2)}, u32[]{:S(2)}) collective-permute-start(bf16[8,128,128]{2,1,0:T(8,128)(2,1)S(1)} %slice.71), channel_id=1, source_target_pairs={{0,8},{4,12},{8,0},{12,4},{16,24},{20,28},{24,16},{28,20},{1,9},{5... | collective-permute-start | bytes 786440 | tf_op jit(solution)/shard_map/ppermute | solution.py:19
  42.7 12.0 %copy-start.3 = (bf16[8,256,128]{2,1,0:T(8,128)(2,1)}, bf16[8,256,128]{2,1,0:T(8,128)(2,1)S(1)}, u32[]{:S(2)}) copy-start(bf16[8,256,128]{2,1,0:T(8,128)(2,1)S(1)} %collective-permute-done.3.refs_1_) | copy-start | bytes 1572868
  42.8 20.3 %collective-permute-start.9 = (bf16[8,128,128]{2,1,0:T(8,128)(2,1)S(1)}, bf16[8,128,128]{2,1,0:T(8,128)(2,1)}, u32[]{:S(2)}, u32[]{:S(2)}) collective-permute-start(bf16[8,128,128]{2,1,0:T(8,128)(2,1)S(1)} %slice.70), channel_id=1, source_target_pairs={{0,16},{4,20},{8,24},{12,28},{16,0},{20,4},{24,8},{28,12},{1,17},{... | collective-permute-start | bytes 786440 | tf_op jit(solution)/shard_map/ppermute | solution.py:19
  48.4 0.8 copy-start.6
  63.1 11.6 %collective-permute-start.11 = (bf16[8,16,4096]{2,1,0:T(8,128)(2,1)}, bf16[8,16,4096]{2,1,0:T(8,128)(2,1)S(1)}, u32[]{:S(2)}, u32[]{:S(2)}) collective-permute-start(bf16[8,16,4096]{2,1,0:T(8,128)(2,1)} %transform.2), channel_id=1, source_target_pairs={{0,4},{4,0},{8,12},{12,8},{16,20},{20,16},{24,28},{28,24},{1,5},{5... | collective-permute-start | bytes 3145736 | tf_op jit(solution)/shard_map/ppermute | solution.py:19
  73.1 3.0 %collective-permute-start.12 = (bf16[8,16,4096]{2,1,0:T(8,128)(2,1)}, bf16[8,16,4096]{2,1,0:T(8,128)(2,1)S(1)}, u32[]{:S(2)}, u32[]{:S(2)}) collective-permute-start(bf16[8,16,4096]{2,1,0:T(8,128)(2,1)} %transform.3), channel_id=1, source_target_pairs={{0,4},{4,0},{8,12},{12,8},{16,20},{20,16},{24,28},{28,24},{1,5},{5... | collective-permute-start | bytes 3145736 | tf_op jit(solution)/shard_map/ppermute | solution.py:19
  74.7 1.4 %copy-start.4 = (bf16[8,16,4096]{2,1,0:T(8,128)(2,1)}, bf16[8,16,4096]{2,1,0:T(8,128)(2,1)S(1)}, u32[]{:S(2)}) copy-start(bf16[8,16,4096]{2,1,0:T(8,128)(2,1)S(1)} %collective-permute-done.11) | copy-start | bytes 3145732
  76.1 1.0 %copy-start.5 = (bf16[8,16,4096]{2,1,0:T(8,128)(2,1)}, bf16[8,16,4096]{2,1,0:T(8,128)(2,1)S(1)}, u32[]{:S(2)}) copy-start(bf16[8,16,4096]{2,1,0:T(8,128)(2,1)S(1)} %collective-permute-done.12) | copy-start | bytes 3145732

commit v2 on v0

v2 whole, which is shorter than its diff:
```python
import functools

import jax
import jax.numpy as jnp
from jax import lax
from jax.experimental import pallas as pl
from jax.experimental.pallas import tpu as pltpu
from jax.sharding import PartitionSpec as P

BLK = 64
LANES = 128
HALF = BLK * BLK // LANES
F32 = jnp.float32
BF16 = jnp.bfloat16
MIB = 1024 * 1024
NT = (((1,), (1,)), ((), ()))
IN_VMEM = pl.BlockSpec(memory_space=pltpu.VMEM)
IN_PLACE = pl.BlockSpec(memory_space=pl.ANY)
IN_SMEM = pl.BlockSpec(memory_space=pltpu.SMEM)


def swap(value, axis, size, offset):
    return lax.ppermute(value, axis, [(i, i ^ offset) for i in range(size)])


def dot(a, b, dims=(((1,), (0,)), ((), ())), precision=None):
    return lax.dot_general(a, b, dims, preferred_element_type=F32, precision=precision)


def iota(shape, dim):
    return lax.broadcasted_iota(jnp.int32, shape, dim)


def in_hbm(value):
    return pltpu.with_memory_space_constraint(value, pltpu.HBM)


def hot(hit):
    return jnp.where(hit, 1.0, 0.0).astype(BF16)


def tables_body(nz, k_local, me, pair, g_refs, occ_out, virt_out, occ_g, virt_g, pick, cols, wide):
    strip = g_refs[0].shape[1] // 8
    nao = occ_g.shape[0]
    nl = occ_out.shape[0]
    nk = virt_out.shape[0] // LANES
    place = 0
    for ref in g_refs:
        for z in range(ref.shape[0]):
            for group in range(4):
                base = group * 2 * strip
                lanes = slice(group * LANES, (group + 1) * LANES)
                occ_g[place : place + strip, lanes] = ref[z, base : base + strip, :]
                virt_g[place : place + strip, lanes] = ref[z, base + strip : base + 2 * strip, :]
            place += strip
    at = iota((1, nao), 1)
    block = at // (nz * strip)
    half = nao // (nz * strip) // 2
    offset = 2 * (block % half) + block // half
    held = (((me[0] ^ offset) * nz) + (me[1] ^ (at // strip) % nz)) * strip + at % strip
    lane = iota((1, nao), 1)
    k_of = [(me[1] ^ (k // k_local)) * k_local + k % k_local for k in range(nk)]

    for k in range(nk):
        for lo in range(2):
            row = pair[0, k_of[k]] * BLK + 2 * iota((HALF, 1), 0) + lo
            pick[(lo * nk + k) * HALF : (lo * nk + k + 1) * HALF, :] = hot(row == held)
    picked = dot(pick[...], occ_g[...]).astype(BF16)
    for l in range(nl):
        for lo in range(2):
            col = pair[0, l] * BLK + 2 * iota((HALF, 1), 0) + lo
            cols[(2 * l + lo) * HALF : (2 * l + lo + 1) * HALF, :] = hot(col == lane)
    table = dot(cols[...], picked, NT).astype(BF16)
    side = nk * HALF
    for l in range(nl):
        for lo in range(2):
            occ_out[l, lo * BLK : (lo + 1) * BLK, :] = table[l * BLK : (l + 1) * BLK, lo * side : (lo + 1) * side]

    for k in range(nk):
        row = pair[1, k_of[k]] * BLK + iota((BLK, 1), 0)
        pick[k * BLK : (k + 1) * BLK, :] = hot(row == held)
    picked = dot(pick[...], virt_g[...]).astype(BF16)
    for l in range(nl):
        col = pair[1, l] * BLK + iota((1, LANES), 1) % BLK
        wide[:, l * LANES : (l + 1) * LANES] = hot(iota((nao, 1), 0) == col)
    full = dot(picked, wide[...])
    for k in range(nk):
        part = full[k * BLK : (k + 1) * BLK, :]
        low = (iota(part.shape, 1) // BLK) % 2 == 0
        virt_out[k * LANES : k * LANES + BLK, :] = jnp.where(low, part, 0.0).astype(BF16)
        virt_out[k * LANES + BLK : (k + 1) * LANES, :] = jnp.where(low, 0.0, part).astype(BF16)


def tables_kernel(count, nz, k_local, me, pair, *refs):
    tables_body(nz, k_local, me, pair, refs[:count], *refs[count:])


def tables_shapes(nao, nl):
    out = (
        jax.ShapeDtypeStruct((nl, 2 * BLK, nl * HALF), BF16),
        jax.ShapeDtypeStruct((nl * LANES, nl * LANES), BF16),
    )
    scratch = [
        pltpu.VMEM((nao, nao), BF16),
        pltpu.VMEM((nao, nao), BF16),
        pltpu.VMEM((nl * BLK, nao), BF16),
        pltpu.VMEM((nl * BLK, nao), BF16),
        pltpu.VMEM((nao, nl * LANES), BF16),
    ]
    return out, scratch


def make_tables(g_blocks, me, pair_index, nz, k_local):
    nl = pair_index.shape[1]
    nao = len(g_blocks) * g_blocks[0].shape[0] * (g_blocks[0].shape[1] // 8)
    out, scratch = tables_shapes(nao, nl)
    return pl.pallas_call(
        functools.partial(tables_kernel, len(g_blocks), nz, k_local),
        in_specs=[IN_SMEM, IN_SMEM] + [IN_VMEM] * len(g_blocks),
        out_specs=[IN_VMEM, IN_VMEM],
        out_shape=out,
        scratch_shapes=scratch,
        compiler_params=pltpu.CompilerParams(vmem_limit_bytes=24 * MIB),
        name="tables",
    )(me, pair_index, *g_blocks)


def transform_body(blocks, rows, virt, occ, out, done, x_buf, z_buf):
    nl = occ.shape[0]
    count = len(blocks)
    per = rows // HALF
    for e in range(count):
        k = 0
        for ref, length in blocks[e]:
            for j in range(length):
                held = ref[j] if len(ref.shape) == 3 else ref[j * rows : (j + 1) * rows, :]
                for l in range(0, nl, 2):
                    weights = virt[k * LANES : (k + 1) * LANES, l * LANES : (l + 2) * LANES]
                    x = dot(held, weights).astype(BF16)
                    for i in range(2):
                        for p in range(per):
                            at = (e * per + p) * LANES
                            x_buf[l + i, k * HALF : (k + 1) * HALF, at : at + LANES] = x[
                                p * HALF : (p + 1) * HALF, i * LANES : (i + 1) * LANES
                            ]
                k += 1
    low = iota((HALF, LANES), 1) < BLK
    for l in range(nl):
        y = dot(occ[l], x_buf[l])
        for p in range(count * per):
            part = y[:, p * LANES : (p + 1) * LANES]
            t0, t2, t1, t3 = (part[i * HALF : (i + 1) * HALF] for i in range(4))
            z = jnp.where(low, t0, t3) + pltpu.roll(jnp.where(low, t2, t1), BLK, 1)
            z_buf[p, :, :] = z.astype(BF16)
        turned = jnp.swapaxes(z_buf[...], 0, 1)
        for c in range(HALF):
            out[l, done : done + count * per, c * LANES : (c + 1) * LANES] = turned[c]


def runs_of(layout, refs):
    refs = iter(refs)
    return [[(next(refs), length) for length in block] for block in layout]


def transform_kernel(layout, rows, *refs):
    total = sum(map(len, layout))
    virt, occ = refs[total : total + 2]
    out, x_buf, z_buf = refs[-3:]
    done = 0
    for before in refs[total + 2 : -3]:
        done = before.shape[1]
        out[:, :done, :] = before[...]
    transform_body(runs_of(layout, refs[:total]), rows, virt, occ, out, done, x_buf, z_buf)


def whole_block(value):
    return pl.BlockSpec(value.shape, lambda i: (0,) * len(value.shape))


def transform(blocks, rows, occ, virt, before=()):
    nl = occ.shape[0]
    layout = [[length for _, length in block] for block in blocks]
    flat = [run for block in blocks for run, _ in block]
    ps = len(blocks) * rows // HALF
    held = ps + sum(b.shape[1] for b in before)
    group = nl if nl <= 8 else 4
    return pl.pallas_call(
        functools.partial(transform_kernel, layout, rows),
        grid=(nl // group,),
        in_specs=[whole_block(run) for run in flat]
        + [
            pl.BlockSpec((nl * LANES, group * LANES), lambda i: (0, i)),
            pl.BlockSpec((group, 2 * BLK, nl * HALF), lambda i: (i, 0, 0)),
        ]
        + [pl.BlockSpec((group,) + b.shape[1:], lambda i: (i, 0, 0)) for b in before],
        out_specs=pl.BlockSpec((group, held, BLK * BLK), lambda i: (i, 0, 0)),
        out_shape=jax.ShapeDtypeStruct((nl, held, BLK * BLK), BF16),
        scratch_shapes=[
            pltpu.VMEM((group, nl * HALF, ps * LANES), BF16),
            pltpu.VMEM((ps, HALF, LANES), BF16),
        ],
        compiler_params=pltpu.CompilerParams(vmem_limit_bytes=36 * MIB),
        name="transform",
    )(*flat, virt, occ, *before)


def prepare_kernel(layout, rows, count, after, nz, k_local, me, pair, *refs):
    g_refs, refs = refs[:count], refs[count:]
    total = sum(map(len, layout))
    runs, refs = refs[:total], refs[total + after :]
    occ, virt, out = refs[:3]
    tables_body(nz, k_local, me, pair, g_refs, occ, virt, *refs[3:8])
    transform_body(runs_of(layout, runs), rows, virt, occ, out, 0, *refs[8:])


def prepare(g_blocks, blocks, rows, me, pair_index, nz, k_local, after):
    nl = pair_index.shape[1]
    nao = len(g_blocks) * g_blocks[0].shape[0] * (g_blocks[0].shape[1] // 8)
    out, scratch = tables_shapes(nao, nl)
    layout = [[length for _, length in block] for block in blocks]
    flat = [run for block in blocks for run, _ in block]
    ps = len(blocks) * rows // HALF
    return pl.pallas_call(
        functools.partial(prepare_kernel, layout, rows, len(g_blocks), len(after), nz, k_local),
        in_specs=[IN_SMEM, IN_SMEM] + [IN_VMEM] * (len(g_blocks) + len(flat)) + [IN_PLACE] * len(after),
        out_specs=[IN_VMEM] * 3,
        out_shape=out + (jax.ShapeDtypeStruct((nl, ps, BLK * BLK), BF16),),
        scratch_shapes=scratch
        + [pltpu.VMEM((nl, nl * HALF, ps * LANES), BF16), pltpu.VMEM((ps, HALF, LANES), BF16)],
        compiler_params=pltpu.CompilerParams(vmem_limit_bytes=44 * MIB),
        name="prepare",
    )(me, pair_index, *g_blocks, *flat, *map(in_hbm, after))


def reorder_kernel(slab, out):
    q, nl, tile = slab.shape
    n = q * nl
    row, col = iota((n, n), 0), iota((n, n), 1)
    order = hot((row % q) * nl + row // q == col)
    step = 512
    for t in range(0, tile, step):
        moved = dot(order, slab[:, :, t : t + step].reshape(n, step)).astype(BF16)
        for l in range(nl):
            out[l, :, t : t + step] = moved[l * q : (l + 1) * q]


def reorder(slab, part, parts):
    count, nl, tile = slab.shape
    q = 256 // nl
    steps = count // parts // q
    return pl.pallas_call(
        reorder_kernel,
        grid=(steps,),
        in_specs=[pl.BlockSpec((q, nl, tile), lambda i: (part * steps + i, 0, 0))],
        out_specs=pl.BlockSpec((nl, q, tile), lambda i: (0, i, 0)),
        out_shape=pltpu.HBM((nl, count // parts, tile), BF16),
        compiler_params=pltpu.CompilerParams(vmem_limit_bytes=24 * MIB),
        name="reorder",
    )(in_hbm(slab))


def stack_kernel(split, nz, after, *refs):
    refs, b_out, g_out = refs[: -2 - after], refs[-2], refs[-1]
    column, side = refs[: nz - 1], refs[nz - 1 :]
    k_local = b_out.shape[0] // len(column)
    rows = split // k_local
    for i, ref in enumerate(column):
        for j in range(k_local):
            b_out[i * k_local + j] = ref[j * rows : (j + 1) * rows, :]
    for i, ref in enumerate(side):
        g_out[i] = ref[split:, :]


def stack(column, side, split, k_local, after):
    one = column[0].shape[0] - split
    return pl.pallas_call(
        functools.partial(stack_kernel, split, len(column) + 1, len(after)),
        in_specs=[IN_VMEM] * (len(column) + len(side)) + [IN_PLACE] * len(after),
        out_specs=[IN_VMEM, IN_VMEM],
        out_shape=(
            jax.ShapeDtypeStruct((len(column) * k_local, split // k_local, LANES), BF16),
            jax.ShapeDtypeStruct((len(side), one, LANES), BF16),
        ),
        compiler_params=pltpu.CompilerParams(vmem_limit_bytes=8 * MIB),
        name="stack",
    )(*column, *side, *map(in_hbm, after))


def collect_kernel(split, nz, sides, *refs):
    near, side, far, out = refs[:nz], refs[nz : nz + sides], refs[nz + sides : 2 * nz + sides - 1], refs[-1]
    for z, ref in enumerate(near):
        out[z] = ref[split:, :]
    for e, ref in enumerate(side):
        out[(e + 1) * nz] = ref[split:, :]
        for z, block in enumerate(far):
            out[(e + 1) * nz + z + 1] = block[e]


def collect(own, column, side, far, split, after):
    nz = len(column) + 1
    return pl.pallas_call(
        functools.partial(collect_kernel, split, nz, len(side)),
        in_specs=[IN_VMEM] * (nz + len(side) + len(far)) + [IN_PLACE] * len(after),
        out_specs=IN_VMEM,
        out_shape=jax.ShapeDtypeStruct((nz * (len(side) + 1), own.shape[0] - split, LANES), BF16),
        compiler_params=pltpu.CompilerParams(vmem_limit_bytes=8 * MIB),
        name="collect",
    )(own, *column, *side, *far, *map(in_hbm, after))


def contract_kernel(parts, place, *refs):
    slabs, w_refs, out, total = refs[:parts], refs[parts:-2], refs[-2], refs[-1]
    l = pl.program_id(0)
    weights = jnp.concatenate([w[0] for w in w_refs], axis=0)
    count = slabs[0].shape[1]

    @pl.when(l == 0)
    def _():
        total[...] = jnp.zeros_like(total)

    for i, slab in enumerate(slabs):
        total[i * count : (i + 1) * count, :] += dot(slab[0], weights, NT)

    @pl.when(l == pl.num_programs(0) - 1)
    def _():
        out[...] = dot(place[...], total[...], NT, precision=lax.Precision.HIGHEST)


def contract(slabs, w_pieces, place):
    nl, count, tile = slabs[0].shape
    rows = place.shape[0]
    count *= len(slabs)
    one = lambda value: pl.BlockSpec((1,) + value.shape[1:], lambda i: (i, 0, 0))
    return pl.pallas_call(
        functools.partial(contract_kernel, len(slabs)),
        grid=(nl,),
        in_specs=[whole_block(place)] + [one(s) for s in slabs] + [one(w) for w in w_pieces],
        out_specs=pl.BlockSpec((rows, count), lambda i: (0, 0)),
        out_shape=jax.ShapeDtypeStruct((rows, count), F32),
        scratch_shapes=[pltpu.VMEM((count, rows), F32)],
        compiler_params=pltpu.CompilerParams(vmem_limit_bytes=28 * MIB),
        name="contract",
    )(place, *map(in_hbm, slabs), *w_pieces)


def on_device(na, nz, b_slab, b_rows, g_occ, g_virt, pair_index):
    per, k_local, tile = b_rows.shape
    me_a, me_z = lax.axis_index("aux"), lax.axis_index("pair")
    me = jnp.stack([me_a, me_z]).astype(jnp.int32)
    outer = list(range(0, na, 2))
    rows = per * HALF
    split = k_local * rows

    g_own = jnp.concatenate([g_occ, g_virt], axis=0)
    b_own = jnp.transpose(b_rows.reshape(per, k_local, HALF, LANES), (1, 0, 2, 3)).reshape(-1, LANES)
    own = jnp.concatenate([b_own] + [g_own[:, i : i + LANES] for i in range(0, g_own.shape[1], LANES)], axis=0)

    column = [swap(own, "pair", nz, d) for d in range(1, nz)]
    side = [swap(own, "aux", na, e) for e in outer[1:]]
    slabs = [reorder(b_slab, 0, 2)]
    b_z, g_side = stack(column, side, split, k_local, slabs)

    b_z, b_slab = lax.optimization_barrier((b_z, b_slab))
    slabs.append(reorder(b_slab, 1, 2))
    far = [[(swap(b_z, "aux", na, e), b_z.shape[0])] for e in outer[1 : 3 if len(outer) == 4 else None]]
    g_far = [swap(g_side, "pair", nz, d) for d in range(1, nz)]
    if len(outer) == 4:
        cut = b_z.shape[0] // 2
        low, high = far[0][0][0][:cut], far[1][0][0][cut:]
        far.append([(swap(low, "aux", na, 4), cut), (swap(high, "aux", na, 2), b_z.shape[0] - cut)])
    g_half = collect(own, column, side, g_far, split, slabs[1:])
    g_blocks = [g_half, swap(g_half, "aux", na, 1)]
    blocks = [[(own, k_local), (b_z, b_z.shape[0])]] + [[(b, k_local)] + f for b, f in zip(side, far)]
    if len(outer) == 4:
        occ, virt, first = prepare(g_blocks, blocks[:3], rows, me, pair_index, nz, k_local, slabs)
        pieces = [transform(blocks[3:], rows, occ, virt, [first])]
    else:
        occ, virt = make_tables(g_blocks, me, pair_index, nz, k_local)
        pieces = [transform(blocks[i : i + 2], rows, occ, virt) for i in range(0, len(outer), 2)]
    others = [swap(w, "aux", na, 1) for w in pieces]

    count = na * per
    at = jnp.arange(count, dtype=jnp.int32)
    block = at // per
    target = (me_a ^ (2 * (block % (na // 2)) + block // (na // 2))) * per + at % per
    place = (target[None, :] == at[:, None]).astype(F32)
    return contract(slabs, pieces + others, place).T


def solution(mesh):
    placed = (
        P(("aux", "pair"), None, None),
        P("aux", "pair", None),
        P(("aux", "pair"), None),
        P(("aux", "pair"), None),
        P(),
    )
    return jax.shard_map(
        functools.partial(on_device, mesh.shape["aux"], mesh.shape["pair"]),
        mesh=mesh,
        in_specs=placed,
        out_specs=P(("aux", "pair"), None),
        check_vma=False,
    )
```

time: 458 us -> 67.9 us (0.15)
  matrix products: 234 us -> 0 us
  blocking collectives: 156 us -> 0 us
  local copies, waits for them, and re-layouts: 51.4 us -> 3.21 us
  Pallas kernels: 0 us -> 37.9 us
  starting transfers between devices: 0.01 us -> 21.4 us
  between operations: 13.5 us -> 0.13 us
  waiting for transfers between devices: 0.02 us -> 4.8 us
    dot_general x17 -> x0, matrix products: 234 us -> none  [the longest x8 134 us: one_target(): jnp.einsum('qlad,lbd->qab', half_step, virt_row, preferred_element_type=j...]
    all_gather x3 -> x0, blocking collectives: 156 us -> none  [the longest x1 70.7 us: on_device(): lax.all_gather(g_occ, ('aux', 'pair'), axis=0, tiled=True)]
    pallas_call x0 -> x7, Pallas kernels: none -> 37.9 us  [the longest x2 16.4 us: reorder(): pl.pallas_call(reorder_kernel, grid=(steps,), in_specs=[pl.BlockSpec((q,...]
    unnamed x3 -> x7, local copies, waits for them, and re-layouts: 27.9 us -> 0.76 us
    ppermute x0 -> x15, starting transfers between devices: none -> 21.4 us  [swap(): return lax.ppermute(value, axis, [(i, i ^ offset) for i in range(size)])]
    while x1 -> x0, local copies, waits for them, and re-layouts: 17.8 us -> none  [project_slab(): stacked = lax.map(one_target, (occ_tables, virt_tables))]
    ppermute x0 -> x15, waiting for transfers between devices: none -> 4.8 us  [swap(): return lax.ppermute(value, axis, [(i, i ^ offset) for i in range(size)])]
  transfers between devices with their start and end apart: 1 -> 15, of which waited for: 0 -> 2; matrix products, arithmetic and copies ran while one was open for 59% -> 1% of each run, Pallas kernels for 0% -> 36%
where the time goes in v2:
time: 67.9 us; the launch traced here: 67.5 us
  Pallas kernels  37.9 us (56%)
  starting transfers between devices  21.4 us (32%)
  waiting for transfers between devices  4.8 us (7%)
  local copies, waits for them, and re-layouts  3.21 us (5%)
    ppermute x15, starting transfers between devices, swap(): return lax.ppermute(value, axis, [(i, i ^ offset) for i in range(size)])  21.4 us
    pallas_call x2, Pallas kernels, reorder(): pl.pallas_call(reorder_kernel, grid=(steps,), in_specs=[pl.BlockSpec((q,...  16.4 us
    pallas_call x1, Pallas kernels, contract(): pl.pallas_call(functools.partial(contract_kernel, len(slabs)), grid=(nl,)...  11.2 us
    pallas_call x1, Pallas kernels, prepare(): pl.pallas_call(functools.partial(prepare_kernel, layout, rows, len(g_bloc...  7.8 us
    ppermute x15, waiting for transfers between devices, swap(): return lax.ppermute(value, axis, [(i, i ^ offset) for i in range(size)])  4.8 us
    pallas_call x1, Pallas kernels, transform(): pl.pallas_call(functools.partial(transform_kernel, layout, rows), grid=(n...  2.39 us
  transfers between devices with their start and end apart: 15, of which 2 were waited for; matrix products, arithmetic and copies ran while one was open for 1% of the time, Pallas kernels for 36%

profile of v2, /device:TPU:0, one launch (start us, length us, event | category | flops | bytes accessed | tf_op | source)
XLA Modules:
  0.0 67.5 jit_solution(3598639378105262406)
XLA Ops:
  0.0 0.7 %constant_dynamic-update-slice_fusion.1 = bf16[32,512]{1,0:T(8,128)(2,1)S(1)} fusion(bf16[16,512]{1,0:T(8,128)(2,1)} %param.7), kind=kLoop, calls=%fused_computation.3 | loop fusion | bytes 32768
  0.7 1.0 %reshape.57 = bf16[8,2,32,128]{3,2,1,0:T(8,128)(2,1)S(1)} reshape(bf16[8,2,4096]{2,1,0:T(2,128)(2,1)} %param.6) | data formatting | bytes 262144 | tf_op jit(solution)/shard_map/reshape | solution.py:355
  1.8 0.7 %constant_dynamic-update-slice_fusion = bf16[32,512]{1,0:T(8,128)(2,1)S(1)} fusion(bf16[32,512]{1,0:T(8,128)(2,1)S(1)} %constant_dynamic-update-slice_fusion.1, bf16[16,512]{1,0:T(8,128)(2,1)} %param.8), kind=kLoop, calls=%fused_computation.2 | loop fusion | bytes 32768 | tf_op jit(solution)/shard_map/concatenate | solution.py:354
  2.5 3.0 %collective-permute-start.3 = (bf16[640,128]{1,0:T(8,128)(2,1)S(1)}, bf16[640,128]{1,0:T(8,128)(2,1)S(1)}, u32[]{:S(2)}, u32[]{:S(2)}) collective-permute-start(bf16[640,128]{1,0:T(8,128)(2,1)S(1)} %constant_dynamic-update-slice_fusion.2.refs_0_.refs_2_), channel_id=1, source_target_pairs={{0,8},{4,12},{8,0},{12,4},{16,24},{20,28},{24,16},{28,20},{1,9},{5... | collective-permute-start | bytes 491528 | tf_op jit(solution)/shard_map/ppermute | solution.py:23
  5.5 1.5 %collective-permute-start.4 = (bf16[640,128]{1,0:T(8,128)(2,1)S(1)}, bf16[640,128]{1,0:T(8,128)(2,1)S(1)}, u32[]{:S(2)}, u32[]{:S(2)}) collective-permute-start(bf16[640,128]{1,0:T(8,128)(2,1)S(1)} %constant_dynamic-update-slice_fusion.2.refs_0_.refs_2_), channel_id=1, source_target_pairs={{0,16},{4,20},{8,24},{12,28},{16,0},{20,4},{24,8},{28,12},{1,17},{... | collective-permute-start | bytes 491528 | tf_op jit(solution)/shard_map/ppermute | solution.py:23
  7.1 2.0 %collective-permute-start = (bf16[640,128]{1,0:T(8,128)(2,1)S(1)}, bf16[640,128]{1,0:T(8,128)(2,1)S(1)}, u32[]{:S(2)}, u32[]{:S(2)}) collective-permute-start(bf16[640,128]{1,0:T(8,128)(2,1)S(1)} %constant_dynamic-update-slice_fusion.2.refs_0_.refs_2_), channel_id=1, source_target_pairs={{0,1},{1,0},{2,3},{3,2},{4,5},{5,4},{6,7},{7,6},{8,9},{9,8},{10,11... | collective-permute-start | bytes 491528 | tf_op jit(solution)/shard_map/ppermute | solution.py:23
  9.1 2.6 %collective-permute-start.1 = (bf16[640,128]{1,0:T(8,128)(2,1)S(1)}, bf16[640,128]{1,0:T(8,128)(2,1)S(1)}, u32[]{:S(2)}, u32[]{:S(2)}) collective-permute-start(bf16[640,128]{1,0:T(8,128)(2,1)S(1)} %constant_dynamic-update-slice_fusion.2.refs_0_.refs_2_), channel_id=1, source_target_pairs={{0,2},{1,3},{2,0},{3,1},{4,6},{5,7},{6,4},{7,5},{8,10},{9,11},{10,... | collective-permute-start | bytes 491528 | tf_op jit(solution)/shard_map/ppermute | solution.py:23
  11.7 3.0 %collective-permute-start.2 = (bf16[640,128]{1,0:T(8,128)(2,1)S(1)}, bf16[640,128]{1,0:T(8,128)(2,1)S(1)}, u32[]{:S(2)}, u32[]{:S(2)}) collective-permute-start(bf16[640,128]{1,0:T(8,128)(2,1)S(1)} %constant_dynamic-update-slice_fusion.2.refs_0_.refs_2_), channel_id=1, source_target_pairs={{0,3},{1,2},{2,1},{3,0},{4,7},{5,6},{6,5},{7,4},{8,11},{9,10},{10,... | collective-permute-start | bytes 491528 | tf_op jit(solution)/shard_map/ppermute | solution.py:23
  14.7 8.2 %reorder.2.refs_6_.refs_8_.refs_0_ = bf16[8,128,4096]{2,1,0:T(8,128)(2,1)} custom-call(bf16[256,8,4096]{2,1,0:T(8,128)(2,1)} %slab.2), custom_call_target="tpu_custom_call" | custom-call | tf_op jit(solution)/shard_map/reorder/pallas_call | solution.py:251
  22.9 0.8 %collective-permute-done.1.refs_1_.refs_2_ = bf16[640,128]{1,0:T(8,128)(2,1)S(1)} collective-permute-done((bf16[640,128]{1,0:T(8,128)(2,1)S(1)}, bf16[640,128]{1,0:T(8,128)(2,1)S(1)}, u32[]{:S(2)}, u32[]{:S(2)}) %collective-permute-start.1) | collective-permute-done | bytes 163872 | tf_op jit(solution)/shard_map/ppermute | solution.py:23
  23.7 2.4 %collective-permute-start.10 = (bf16[3,128,128]{2,1,0:T(8,128)(2,1)S(1)}, bf16[3,128,128]{2,1,0:T(8,128)(2,1)S(1)}, u32[]{:S(2)}, u32[]{:S(2)}) collective-permute-start(bf16[3,128,128]{2,1,0:T(8,128)(2,1)S(1)} %get-tuple-element.15), channel_id=1, source_target_pairs={{0,1},{1,0},{2,3},{3,2},{4,5},{5,4},{6,7},{7,6},{8,9},{9,8},{10,11... | collective-permute-start | bytes 294920 | tf_op jit(solution)/shard_map/ppermute | solution.py:23
  26.1 1.1 %collective-permute-start.11 = (bf16[3,128,128]{2,1,0:T(8,128)(2,1)S(1)}, bf16[3,128,128]{2,1,0:T(8,128)(2,1)S(1)}, u32[]{:S(2)}, u32[]{:S(2)}) collective-permute-start(bf16[3,128,128]{2,1,0:T(8,128)(2,1)S(1)} %get-tuple-element.15), channel_id=1, source_target_pairs={{0,2},{1,3},{2,0},{3,1},{4,6},{5,7},{6,4},{7,5},{8,10},{9,11},{10,... | collective-permute-start | bytes 294920 | tf_op jit(solution)/shard_map/ppermute | solution.py:23
  27.2 1.4 %collective-permute-start.12 = (bf16[3,128,128]{2,1,0:T(8,128)(2,1)S(1)}, bf16[3,128,128]{2,1,0:T(8,128)(2,1)S(1)}, u32[]{:S(2)}, u32[]{:S(2)}) collective-permute-start(bf16[3,128,128]{2,1,0:T(8,128)(2,1)S(1)} %get-tuple-element.15), channel_id=1, source_target_pairs={{0,3},{1,2},{2,1},{3,0},{4,7},{5,6},{6,5},{7,4},{8,11},{9,10},{10,... | collective-permute-start | bytes 294920 | tf_op jit(solution)/shard_map/ppermute | solution.py:23
  28.6 1.5 %collective-permute-start.6 = (bf16[6,256,128]{2,1,0:T(8,128)(2,1)S(1)}, bf16[6,256,128]{2,1,0:T(8,128)(2,1)S(1)}, u32[]{:S(2)}, u32[]{:S(2)}) collective-permute-start(bf16[6,256,128]{2,1,0:T(8,128)(2,1)S(1)} %get-tuple-element.14.refs_3_), channel_id=1, source_target_pairs={{0,8},{4,12},{8,0},{12,4},{16,24},{20,28},{24,16},{28,20},{1,9},{5... | collective-permute-start | bytes 1179656 | tf_op jit(solution)/shard_map/ppermute | solution.py:23
  30.0 1.5 %collective-permute-start.8 = (bf16[6,256,128]{2,1,0:T(8,128)(2,1)S(1)}, bf16[6,256,128]{2,1,0:T(8,128)(2,1)S(1)}, u32[]{:S(2)}, u32[]{:S(2)}) collective-permute-start(bf16[6,256,128]{2,1,0:T(8,128)(2,1)S(1)} %get-tuple-element.14.refs_3_), channel_id=1, source_target_pairs={{0,16},{4,20},{8,24},{12,28},{16,0},{20,4},{24,8},{28,12},{1,17},{... | collective-permute-start | bytes 1179656 | tf_op jit(solution)/shard_map/ppermute | solution.py:23
  31.6 8.2 %reorder.3.refs_10_.refs_9_.refs_1_ = bf16[8,128,4096]{2,1,0:T(8,128)(2,1)} custom-call(bf16[256,8,4096]{2,1,0:T(8,128)(2,1)} %slab.2), custom_call_target="tpu_custom_call" | custom-call | tf_op jit(solution)/shard_map/reorder/pallas_call | solution.py:251
  39.9 0.6 collective-permute-start.7
  40.5 0.7 %slice.29 = bf16[3,256,128]{2,1,0:T(8,128)(2,1)} slice(bf16[6,256,128]{2,1,0:T(8,128)(2,1)S(1)} %collective-permute-done.8.refs_7_), slice={[3:6], [0:256], [0:128]} | slice | bytes 393216 | tf_op jit(solution)/shard_map/slice | solution.py:369
  41.2 0.5 collective-permute-start.9
  41.8 7.8 %prepare.1 = (bf16[8,128,256]{2,1,0:T(8,128)(2,1)S(1)}, bf16[1024,1024]{1,0:T(8,128)(2,1)S(1)}, bf16[8,24,4096]{2,1,0:T(8,128)(2,1)S(1)}) custom-call(s32[2]{0:T(128)S(1)} %pad_add_fusion.me, s32[2,8]{1,0:T(2,128)S(1)} %copy-done, bf16[16,128,128]{2,1,0:T(8,128)(2,1)S(1)} %collect.1.refs_0_, bf16[16,128,128]{2,1,0:T(8,128)(2,1)S(1)} %collective-permute-done.13.refs_1_, ...), custom_call_target="tpu_custom_call" | custom-call | tf_op jit(solution)/shard_map/prepare/pallas_call | solution.py:223
  49.6 2.4 %transform.1.refs_2_ = bf16[8,32,4096]{2,1,0:T(8,128)(2,1)S(1)} custom-call(bf16[640,128]{1,0:T(8,128)(2,1)S(1)} %collective-permute-done.5.refs_5_.refs_6_.refs_0_, bf16[3,256,128]{2,1,0:T(8,128)(2,1)S(1)} %collective-permute-done.7.refs_1_, bf16[3,256,128]{2,1,0:T(8,128)(2,1)S(1)} %collective-permute-done.9.refs_2_, ...), custom_call_target="tpu_custom_call" | custom-call | tf_op jit(solution)/shard_map/transform/pallas_call | solution.py:187
  52.0 0.2 collective-permute-start.14
  52.3 4.0 %collective-permute-done.14.refs_3_ = bf16[8,32,4096]{2,1,0:T(8,128)(2,1)S(1)} collective-permute-done((bf16[8,32,4096]{2,1,0:T(8,128)(2,1)S(1)}, bf16[8,32,4096]{2,1,0:T(8,128)(2,1)S(1)}, u32[]{:S(2)}, u32[]{:S(2)}) %collective-permute-start.14) | collective-permute-done | bytes 2097184 | tf_op jit(solution)/shard_map/ppermute | solution.py:23
  56.3 11.2 %contract.1 = f32[64,256]{1,0:T(8,128)} custom-call(f32[64,64]{1,0:T(8,128)S(1)} %fusion.place, bf16[8,128,4096]{2,1,0:T(8,128)(2,1)} %reorder.2.refs_6_.refs_8_.refs_0_, bf16[8,128,4096]{2,1,0:T(8,128)(2,1)} %reorder.3.refs_10_.refs_9_.refs_1_, bf16[8,32,4096]{2,1,0:T(8,128)(2,1)S(1)} %transform.1.refs_2_, ...), custom_call_target="tpu_custom_call" | custom-call | tf_op jit(solution)/shard_map/contract/pallas_call | solution.py:334
  (29 shorter events, 0.4 us)
Async XLA Ops:
  2.5 9.2 %collective-permute-start.3 = (bf16[640,128]{1,0:T(8,128)(2,1)S(1)}, bf16[640,128]{1,0:T(8,128)(2,1)S(1)}, u32[]{:S(2)}, u32[]{:S(2)}) collective-permute-start(bf16[640,128]{1,0:T(8,128)(2,1)S(1)} %constant_dynamic-update-slice_fusion.2.refs_0_.refs_2_), channel_id=1, source_target_pairs={{0,8},{4,12},{8,0},{12,4},{16,24},{20,28},{24,16},{28,20},{1,9},{5... | collective-permute-start | bytes 491528 | tf_op jit(solution)/shard_map/ppermute | solution.py:23
  5.5 17.4 %collective-permute-start.4 = (bf16[640,128]{1,0:T(8,128)(2,1)S(1)}, bf16[640,128]{1,0:T(8,128)(2,1)S(1)}, u32[]{:S(2)}, u32[]{:S(2)}) collective-permute-start(bf16[640,128]{1,0:T(8,128)(2,1)S(1)} %constant_dynamic-update-slice_fusion.2.refs_0_.refs_2_), channel_id=1, source_target_pairs={{0,16},{4,20},{8,24},{12,28},{16,0},{20,4},{24,8},{28,12},{1,17},{... | collective-permute-start | bytes 491528 | tf_op jit(solution)/shard_map/ppermute | solution.py:23
  7.1 15.8 %collective-permute-start.5 = (bf16[640,128]{1,0:T(8,128)(2,1)S(1)}, bf16[640,128]{1,0:T(8,128)(2,1)S(1)}, u32[]{:S(2)}, u32[]{:S(2)}) collective-permute-start(bf16[640,128]{1,0:T(8,128)(2,1)S(1)} %constant_dynamic-update-slice_fusion.2.refs_0_.refs_2_), channel_id=1, source_target_pairs={{0,24},{4,28},{8,16},{12,20},{16,8},{20,12},{24,0},{28,4},{1,25},{... | collective-permute-start | bytes 491528 | tf_op jit(solution)/shard_map/ppermute | solution.py:23
  7.1 15.8 %collective-permute-start = (bf16[640,128]{1,0:T(8,128)(2,1)S(1)}, bf16[640,128]{1,0:T(8,128)(2,1)S(1)}, u32[]{:S(2)}, u32[]{:S(2)}) collective-permute-start(bf16[640,128]{1,0:T(8,128)(2,1)S(1)} %constant_dynamic-update-slice_fusion.2.refs_0_.refs_2_), channel_id=1, source_target_pairs={{0,1},{1,0},{2,3},{3,2},{4,5},{5,4},{6,7},{7,6},{8,9},{9,8},{10,11... | collective-permute-start | bytes 491528 | tf_op jit(solution)/shard_map/ppermute | solution.py:23
  9.1 14.5 %collective-permute-start.1 = (bf16[640,128]{1,0:T(8,128)(2,1)S(1)}, bf16[640,128]{1,0:T(8,128)(2,1)S(1)}, u32[]{:S(2)}, u32[]{:S(2)}) collective-permute-start(bf16[640,128]{1,0:T(8,128)(2,1)S(1)} %constant_dynamic-update-slice_fusion.2.refs_0_.refs_2_), channel_id=1, source_target_pairs={{0,2},{1,3},{2,0},{3,1},{4,6},{5,7},{6,4},{7,5},{8,10},{9,11},{10,... | collective-permute-start | bytes 491528 | tf_op jit(solution)/shard_map/ppermute | solution.py:23
  11.7 12.0 %collective-permute-start.2 = (bf16[640,128]{1,0:T(8,128)(2,1)S(1)}, bf16[640,128]{1,0:T(8,128)(2,1)S(1)}, u32[]{:S(2)}, u32[]{:S(2)}) collective-permute-start(bf16[640,128]{1,0:T(8,128)(2,1)S(1)} %constant_dynamic-update-slice_fusion.2.refs_0_.refs_2_), channel_id=1, source_target_pairs={{0,3},{1,2},{2,1},{3,0},{4,7},{5,6},{6,5},{7,4},{8,11},{9,10},{10,... | collective-permute-start | bytes 491528 | tf_op jit(solution)/shard_map/ppermute | solution.py:23
  23.7 16.1 %collective-permute-start.10 = (bf16[3,128,128]{2,1,0:T(8,128)(2,1)S(1)}, bf16[3,128,128]{2,1,0:T(8,128)(2,1)S(1)}, u32[]{:S(2)}, u32[]{:S(2)}) collective-permute-start(bf16[3,128,128]{2,1,0:T(8,128)(2,1)S(1)} %get-tuple-element.15), channel_id=1, source_target_pairs={{0,1},{1,0},{2,3},{3,2},{4,5},{5,4},{6,7},{7,6},{8,9},{9,8},{10,11... | collective-permute-start | bytes 294920 | tf_op jit(solution)/shard_map/ppermute | solution.py:23
  26.1 13.7 %collective-permute-start.11 = (bf16[3,128,128]{2,1,0:T(8,128)(2,1)S(1)}, bf16[3,128,128]{2,1,0:T(8,128)(2,1)S(1)}, u32[]{:S(2)}, u32[]{:S(2)}) collective-permute-start(bf16[3,128,128]{2,1,0:T(8,128)(2,1)S(1)} %get-tuple-element.15), channel_id=1, source_target_pairs={{0,2},{1,3},{2,0},{3,1},{4,6},{5,7},{6,4},{7,5},{8,10},{9,11},{10,... | collective-permute-start | bytes 294920 | tf_op jit(solution)/shard_map/ppermute | solution.py:23
  27.2 12.6 %collective-permute-start.12 = (bf16[3,128,128]{2,1,0:T(8,128)(2,1)S(1)}, bf16[3,128,128]{2,1,0:T(8,128)(2,1)S(1)}, u32[]{:S(2)}, u32[]{:S(2)}) collective-permute-start(bf16[3,128,128]{2,1,0:T(8,128)(2,1)S(1)} %get-tuple-element.15), channel_id=1, source_target_pairs={{0,3},{1,2},{2,1},{3,0},{4,7},{5,6},{6,5},{7,4},{8,11},{9,10},{10,... | collective-permute-start | bytes 294920 | tf_op jit(solution)/shard_map/ppermute | solution.py:23
  28.6 11.3 %collective-permute-start.6 = (bf16[6,256,128]{2,1,0:T(8,128)(2,1)S(1)}, bf16[6,256,128]{2,1,0:T(8,128)(2,1)S(1)}, u32[]{:S(2)}, u32[]{:S(2)}) collective-permute-start(bf16[6,256,128]{2,1,0:T(8,128)(2,1)S(1)} %get-tuple-element.14.refs_3_), channel_id=1, source_target_pairs={{0,8},{4,12},{8,0},{12,4},{16,24},{20,28},{24,16},{28,20},{1,9},{5... | collective-permute-start | bytes 1179656 | tf_op jit(solution)/shard_map/ppermute | solution.py:23
  30.0 10.5 %collective-permute-start.8 = (bf16[6,256,128]{2,1,0:T(8,128)(2,1)S(1)}, bf16[6,256,128]{2,1,0:T(8,128)(2,1)S(1)}, u32[]{:S(2)}, u32[]{:S(2)}) collective-permute-start(bf16[6,256,128]{2,1,0:T(8,128)(2,1)S(1)} %get-tuple-element.14.refs_3_), channel_id=1, source_target_pairs={{0,16},{4,20},{8,24},{12,28},{16,0},{20,4},{24,8},{28,12},{1,17},{... | collective-permute-start | bytes 1179656 | tf_op jit(solution)/shard_map/ppermute | solution.py:23
  39.7 2.1 %copy-start = (s32[2,8]{1,0:T(2,128)S(1)}, s32[2,8]{1,0:T(2,128)}, u32[]{:S(2)}) copy-start(s32[2,8]{1,0:T(2,128)} %pair.1) | copy-start | bytes 196
  39.8 2.0 %collective-permute-start.13 = (bf16[16,128,128]{2,1,0:T(8,128)(2,1)S(1)}, bf16[16,128,128]{2,1,0:T(8,128)(2,1)S(1)}, u32[]{:S(2)}, u32[]{:S(2)}) collective-permute-start(bf16[16,128,128]{2,1,0:T(8,128)(2,1)S(1)} %collect.1.refs_0_), channel_id=1, source_target_pairs={{0,4},{4,0},{8,12},{12,8},{16,20},{20,16},{24,28},{28,24},{1,5},{5... | collective-permute-start | bytes 1572872 | tf_op jit(solution)/shard_map/ppermute | solution.py:23
  39.9 9.7 %collective-permute-start.7 = (bf16[3,256,128]{2,1,0:T(8,128)(2,1)S(1)}, bf16[3,256,128]{2,1,0:T(8,128)(2,1)S(1)}, u32[]{:S(2)}, u32[]{:S(2)}) collective-permute-start(bf16[3,256,128]{2,1,0:T(8,128)(2,1)S(1)} %slice.28), channel_id=1, source_target_pairs={{0,16},{4,20},{8,24},{12,28},{16,0},{20,4},{24,8},{28,12},{1,17},{... | collective-permute-start | bytes 589832 | tf_op jit(solution)/shard_map/ppermute | solution.py:23
  41.2 8.4 %collective-permute-start.9 = (bf16[3,256,128]{2,1,0:T(8,128)(2,1)}, bf16[3,256,128]{2,1,0:T(8,128)(2,1)S(1)}, u32[]{:S(2)}, u32[]{:S(2)}) collective-permute-start(bf16[3,256,128]{2,1,0:T(8,128)(2,1)} %slice.29), channel_id=1, source_target_pairs={{0,8},{4,12},{8,0},{12,4},{16,24},{20,28},{24,16},{28,20},{1,9},{5... | collective-permute-start | bytes 589832 | tf_op jit(solution)/shard_map/ppermute | solution.py:23
  52.0 4.2 %collective-permute-start.14 = (bf16[8,32,4096]{2,1,0:T(8,128)(2,1)S(1)}, bf16[8,32,4096]{2,1,0:T(8,128)(2,1)S(1)}, u32[]{:S(2)}, u32[]{:S(2)}) collective-permute-start(bf16[8,32,4096]{2,1,0:T(8,128)(2,1)S(1)} %transform.1.refs_2_), channel_id=1, source_target_pairs={{0,4},{4,0},{8,12},{12,8},{16,20},{20,16},{24,28},{28,24},{1,5},{5... | collective-permute-start | bytes 6291464 | tf_op jit(solution)/shard_map/ppermute | solution.py:23

commit v3 on v2

--- a/solution.py
+++ b/solution.py
@@ -33,6 +33,10 @@
 
 def in_hbm(value):
     return pltpu.with_memory_space_constraint(value, pltpu.HBM)
+
+
+def in_vmem(value):
+    return pltpu.with_memory_space_constraint(value, pltpu.VMEM)
 
 
 def hot(hit):
@@ -199,7 +203,7 @@
             pltpu.VMEM((group, nl * HALF, ps * LANES), BF16),
             pltpu.VMEM((ps, HALF, LANES), BF16),
         ],
-        compiler_params=pltpu.CompilerParams(vmem_limit_bytes=36 * MIB),
+        compiler_params=pltpu.CompilerParams(vmem_limit_bytes=(18 if nl <= 8 else 36) * MIB),
         name="transform",
     )(*flat, virt, occ, *before)
 
@@ -227,13 +231,14 @@
         out_shape=out + (jax.ShapeDtypeStruct((nl, ps, BLK * BLK), BF16),),
         scratch_shapes=scratch
         + [pltpu.VMEM((nl, nl * HALF, ps * LANES), BF16), pltpu.VMEM((ps, HALF, LANES), BF16)],
-        compiler_params=pltpu.CompilerParams(vmem_limit_bytes=44 * MIB),
+        compiler_params=pltpu.CompilerParams(vmem_limit_bytes=27 * MIB),
         name="prepare",
-    )(me, pair_index, *g_blocks, *flat, *map(in_hbm, after))
+    )(me, pair_index, *g_blocks, *flat, *after)
 
 
 def reorder_kernel(slab, out):
     q, nl, tile = slab.shape
+    at = 0 if out.shape[1] == q else pl.multiple_of(pl.program_id(0) * q, q)
     n = q * nl
     row, col = iota((n, n), 0), iota((n, n), 1)
     order = hot((row % q) * nl + row // q == col)
@@ -241,22 +246,58 @@
     for t in range(0, tile, step):
         moved = dot(order, slab[:, :, t : t + step].reshape(n, step)).astype(BF16)
         for l in range(nl):
-            out[l, :, t : t + step] = moved[l * q : (l + 1) * q]
-
-
-def reorder(slab, part, parts):
+            out[l, pl.ds(at, q), t : t + step] = moved[l * q : (l + 1) * q]
+
+
+def reorder(slab, first, last, parts, space):
     count, nl, tile = slab.shape
     q = 256 // nl
-    steps = count // parts // q
+    skip = count * first // parts // q
+    steps = count * last // parts // q - skip
     return pl.pallas_call(
         reorder_kernel,
         grid=(steps,),
-        in_specs=[pl.BlockSpec((q, nl, tile), lambda i: (part * steps + i, 0, 0))],
-        out_specs=pl.BlockSpec((nl, q, tile), lambda i: (0, i, 0)),
-        out_shape=pltpu.HBM((nl, count // parts, tile), BF16),
+        in_specs=[pl.BlockSpec((q, nl, tile), lambda i: (skip + i, 0, 0))],
+        out_specs=IN_VMEM if space == pltpu.VMEM else pl.BlockSpec((nl, q, tile), lambda i: (0, i, 0)),
+        out_shape=space((nl, steps * q, tile), BF16),
         compiler_params=pltpu.CompilerParams(vmem_limit_bytes=24 * MIB),
         name="reorder",
     )(in_hbm(slab))
+
+
+def pack_kernel(b_in, occ_in, virt_in, out, b_rows, g_occ, g_virt, sems):
+    moves = [
+        pltpu.make_async_copy(source, to, sems.at[i])
+        for i, (source, to) in enumerate(((b_in, b_rows), (occ_in, g_occ), (virt_in, g_virt)))
+    ]
+    for move in moves:
+        move.start()
+    for move in moves:
+        move.wait()
+    per, k_local, _ = b_rows.shape
+    for k in range(k_local):
+        held = b_rows[:, k, :].astype(F32)
+        for p in range(per):
+            out[(k * per + p) * HALF : (k * per + p + 1) * HALF, :] = held[p].reshape(HALF, LANES).astype(BF16)
+    at = k_local * per * HALF
+    strip = g_occ.shape[0]
+    for i in range(0, g_occ.shape[1], LANES):
+        for ref in (g_occ, g_virt):
+            out[at : at + strip, :] = ref[:, i : i + LANES]
+            at += strip
+
+
+def pack(b_rows, g_occ, g_virt):
+    total = (b_rows.size + 2 * g_occ.size) // LANES
+    return pl.pallas_call(
+        pack_kernel,
+        in_specs=[IN_PLACE] * 3,
+        out_specs=IN_VMEM,
+        out_shape=jax.ShapeDtypeStruct((total, LANES), BF16),
+        scratch_shapes=[pltpu.VMEM(x.shape, BF16) for x in (b_rows, g_occ, g_virt)] + [pltpu.SemaphoreType.DMA((3,))],
+        compiler_params=pltpu.CompilerParams(vmem_limit_bytes=8 * MIB),
+        name="pack",
+    )(in_hbm(b_rows), in_hbm(g_occ), in_hbm(g_virt))
 
 
 def stack_kernel(split, nz, after, *refs):
@@ -283,7 +324,7 @@
         ),
         compiler_params=pltpu.CompilerParams(vmem_limit_bytes=8 * MIB),
         name="stack",
-    )(*column, *side, *map(in_hbm, after))
+    )(*column, *side, *after)
 
 
 def collect_kernel(split, nz, sides, *refs):
@@ -305,42 +346,31 @@
         out_shape=jax.ShapeDtypeStruct((nz * (len(side) + 1), own.shape[0] - split, LANES), BF16),
         compiler_params=pltpu.CompilerParams(vmem_limit_bytes=8 * MIB),
         name="collect",
-    )(own, *column, *side, *far, *map(in_hbm, after))
+    )(own, *column, *side, *far, *after)
 
 
 def contract_kernel(parts, place, *refs):
-    slabs, w_refs, out, total = refs[:parts], refs[parts:-2], refs[-2], refs[-1]
-    l = pl.program_id(0)
-    weights = jnp.concatenate([w[0] for w in w_refs], axis=0)
-    count = slabs[0].shape[1]
-
-    @pl.when(l == 0)
-    def _():
-        total[...] = jnp.zeros_like(total)
-
-    for i, slab in enumerate(slabs):
-        total[i * count : (i + 1) * count, :] += dot(slab[0], weights, NT)
-
-    @pl.when(l == pl.num_programs(0) - 1)
-    def _():
-        out[...] = dot(place[...], total[...], NT, precision=lax.Precision.HIGHEST)
+    slabs, w_refs, out = refs[:parts], refs[parts:-1], refs[-1]
+    total = [None] * parts
+    for l in range(slabs[0].shape[0]):
+        weights = jnp.concatenate([w[l] for w in w_refs], axis=0)
+        for i, slab in enumerate(slabs):
+            part = dot(slab[l], weights, NT)
+            total[i] = part if total[i] is None else total[i] + part
+    total = jnp.concatenate(total, axis=0)
+    out[...] = dot(place[...], total, NT, precision=lax.Precision.HIGHEST)
 
 
 def contract(slabs, w_pieces, place):
-    nl, count, tile = slabs[0].shape
-    rows = place.shape[0]
-    count *= len(slabs)
-    one = lambda value: pl.BlockSpec((1,) + value.shape[1:], lambda i: (i, 0, 0))
-    return pl.pallas_call(
-        functools.partial(contract_kernel, len(slabs)),
-        grid=(nl,),
-        in_specs=[whole_block(place)] + [one(s) for s in slabs] + [one(w) for w in w_pieces],
-        out_specs=pl.BlockSpec((rows, count), lambda i: (0, 0)),
-        out_shape=jax.ShapeDtypeStruct((rows, count), F32),
-        scratch_shapes=[pltpu.VMEM((count, rows), F32)],
+    parts = len(slabs)
+    return pl.pallas_call(
+        functools.partial(contract_kernel, parts),
+        in_specs=[IN_VMEM] * (1 + parts + len(w_pieces)),
+        out_specs=IN_VMEM,
+        out_shape=jax.ShapeDtypeStruct((place.shape[0], sum(slab.shape[1] for slab in slabs)), F32),
         compiler_params=pltpu.CompilerParams(vmem_limit_bytes=28 * MIB),
         name="contract",
-    )(place, *map(in_hbm, slabs), *w_pieces)
+    )(place, *map(in_vmem, slabs), *w_pieces)
 
 
 def on_device(na, nz, b_slab, b_rows, g_occ, g_virt, pair_index):
@@ -351,32 +381,32 @@
     rows = per * HALF
     split = k_local * rows
 
-    g_own = jnp.concatenate([g_occ, g_virt], axis=0)
-    b_own = jnp.transpose(b_rows.reshape(per, k_local, HALF, LANES), (1, 0, 2, 3)).reshape(-1, LANES)
-    own = jnp.concatenate([b_own] + [g_own[:, i : i + LANES] for i in range(0, g_own.shape[1], LANES)], axis=0)
-
+    own = pack(b_rows, g_occ, g_virt)
+
+    side = [swap(own, "aux", na, e) for e in outer[1:]]
     column = [swap(own, "pair", nz, d) for d in range(1, nz)]
-    side = [swap(own, "aux", na, e) for e in outer[1:]]
-    slabs = [reorder(b_slab, 0, 2)]
-    b_z, g_side = stack(column, side, split, k_local, slabs)
+    slabs = [reorder(b_slab, 0, 2, 4, pltpu.HBM)]
+    b_z, g_side = stack(column, side, split, k_local, [in_hbm(slabs[0])])
 
     b_z, b_slab = lax.optimization_barrier((b_z, b_slab))
-    slabs.append(reorder(b_slab, 1, 2))
+    slabs.append(reorder(b_slab, 2, 3, 4, pltpu.HBM))
+    g_far = [swap(g_side, "pair", nz, d) for d in range(1, nz)]
     far = [[(swap(b_z, "aux", na, e), b_z.shape[0])] for e in outer[1 : 3 if len(outer) == 4 else None]]
-    g_far = [swap(g_side, "pair", nz, d) for d in range(1, nz)]
     if len(outer) == 4:
         cut = b_z.shape[0] // 2
         low, high = far[0][0][0][:cut], far[1][0][0][cut:]
         far.append([(swap(low, "aux", na, 4), cut), (swap(high, "aux", na, 2), b_z.shape[0] - cut)])
-    g_half = collect(own, column, side, g_far, split, slabs[1:])
+    close = [block[0][0] for block in far[:2]]
+    g_half = collect(own, column, side, g_far, split, [in_hbm(slabs[1])] + (close if len(outer) == 4 else []))
     g_blocks = [g_half, swap(g_half, "aux", na, 1)]
     blocks = [[(own, k_local), (b_z, b_z.shape[0])]] + [[(b, k_local)] + f for b, f in zip(side, far)]
     if len(outer) == 4:
-        occ, virt, first = prepare(g_blocks, blocks[:3], rows, me, pair_index, nz, k_local, slabs)
+        occ, virt, first = prepare(g_blocks, blocks[:3], rows, me, pair_index, nz, k_local, [])
         pieces = [transform(blocks[3:], rows, occ, virt, [first])]
     else:
         occ, virt = make_tables(g_blocks, me, pair_index, nz, k_local)
         pieces = [transform(blocks[i : i + 2], rows, occ, virt) for i in range(0, len(outer), 2)]
+    pieces[-1], b_slab = lax.optimization_barrier((pieces[-1], b_slab))
     others = [swap(w, "aux", na, 1) for w in pieces]
 
     count = na * per
@@ -384,6 +414,7 @@
     block = at // per
     target = (me_a ^ (2 * (block % (na // 2)) + block // (na // 2))) * per + at % per
     place = (target[None, :] == at[:, None]).astype(F32)
+    slabs.append(reorder(b_slab, 3, 4, 4, pltpu.VMEM))
     return contract(slabs, pieces + others, place).T
 
 

time: 67.9 us -> 58.6 us (0.86)
  Pallas kernels: 37.9 us -> 32.7 us
  starting transfers between devices: 21.4 us -> 19.4 us
  local copies, waits for them, and re-layouts: 3.21 us -> 1.45 us
    pallas_call x1 -> x2, Pallas kernels: 11.2 us -> 6.47 us  [the longest x1 5.5 us: contract(): pl.pallas_call(functools.partial(contract_kernel, parts), in_specs=[IN_VM...]
    ppermute x15, starting transfers between devices: 21.4 us -> 19.4 us  [swap(): return lax.ppermute(value, axis, [(i, i ^ offset) for i in range(size)])]
    reshape x2 -> x0, local copies, waits for them, and re-layouts: 1.02 us -> none  [on_device(): b_rows.reshape(per, k_local, HALF, LANES)]
    concatenate x2 -> x0, local copies, waits for them, and re-layouts: 0.73 us -> none  [the longest x1 0.72 us: on_device(): g_own = jnp.concatenate([g_occ, g_virt], axis=0)]
    pallas_call x2 -> x3, Pallas kernels: 16.4 us -> 16 us  [reorder(): pl.pallas_call(reorder_kernel, grid=(steps,), in_specs=[pl.BlockSpec((q,...]
  transfers between devices with their start and end apart: 15 -> 15, of which waited for: 2 -> 4; matrix products, arithmetic and copies ran while one was open for 1% -> 1% of each run, Pallas kernels for 36% -> 41%
where the time goes in v3:
time: 58.6 us; the launch traced here: 58.5 us
  Pallas kernels  32.7 us (56%)
  starting transfers between devices  19.4 us (33%)
  waiting for transfers between devices  4.72 us (8%)
  local copies, waits for them, and re-layouts  1.45 us (2%)
    ppermute x15, starting transfers between devices, swap(): return lax.ppermute(value, axis, [(i, i ^ offset) for i in range(size)])  19.4 us
    pallas_call x3, Pallas kernels, reorder(): pl.pallas_call(reorder_kernel, grid=(steps,), in_specs=[pl.BlockSpec((q,...  16 us
    pallas_call x1, Pallas kernels, prepare(): pl.pallas_call(functools.partial(prepare_kernel, layout, rows, len(g_bloc...  7.78 us
    pallas_call x1, Pallas kernels, contract(): pl.pallas_call(functools.partial(contract_kernel, parts), in_specs=[IN_VM...  5.5 us
    ppermute x15, waiting for transfers between devices, swap(): return lax.ppermute(value, axis, [(i, i ^ offset) for i in range(size)])  4.72 us
    pallas_call x1, Pallas kernels, transform(): pl.pallas_call(functools.partial(transform_kernel, layout, rows), grid=(n...  2.37 us
  transfers between devices with their start and end apart: 15, of which 4 were waited for; matrix products, arithmetic and copies ran while one was open for 1% of the time, Pallas kernels for 41%

profile of v3, /device:TPU:0, one launch (start us, length us, event | category | flops | bytes accessed | tf_op | source)
XLA Modules:
  0.0 58.5 jit_solution(16161525381591718628)
XLA Ops:
  0.0 1.0 %pack.1.refs_0_.refs_2_ = bf16[640,128]{1,0:T(8,128)(2,1)S(1)} custom-call(bf16[8,2,4096]{2,1,0:T(2,128)(2,1)} %b_in.1, bf16[16,512]{1,0:T(8,128)(2,1)} %occ_in.1, bf16[16,512]{1,0:T(8,128)(2,1)} %virt_in.1), custom_call_target="tpu_custom_call" | custom-call | tf_op jit(solution)/shard_map/pack/pallas_call | solution.py:292
  1.0 4.0 %collective-permute-start.5 = (bf16[640,128]{1,0:T(8,128)(2,1)S(1)}, bf16[640,128]{1,0:T(8,128)(2,1)S(1)}, u32[]{:S(2)}, u32[]{:S(2)}) collective-permute-start(bf16[640,128]{1,0:T(8,128)(2,1)S(1)} %pack.1.refs_0_.refs_2_), channel_id=1, source_target_pairs={{0,24},{4,28},{8,16},{12,20},{16,8},{20,12},{24,0},{28,4},{1,25},{... | collective-permute-start | bytes 491528 | tf_op jit(solution)/shard_map/ppermute | solution.py:23
  4.9 0.5 collective-permute-start.4
  5.6 4.0 %collective-permute-start.2 = (bf16[640,128]{1,0:T(8,128)(2,1)S(1)}, bf16[640,128]{1,0:T(8,128)(2,1)S(1)}, u32[]{:S(2)}, u32[]{:S(2)}) collective-permute-start(bf16[640,128]{1,0:T(8,128)(2,1)S(1)} %pack.1.refs_0_.refs_2_), channel_id=1, source_target_pairs={{0,3},{1,2},{2,1},{3,0},{4,7},{5,6},{6,5},{7,4},{8,11},{9,10},{10,... | collective-permute-start | bytes 491528 | tf_op jit(solution)/shard_map/ppermute | solution.py:23
  9.6 0.4 collective-permute-done.5.refs_5_.refs_6_.refs_0_
  10.0 2.0 %collective-permute-start = (bf16[640,128]{1,0:T(8,128)(2,1)S(1)}, bf16[640,128]{1,0:T(8,128)(2,1)S(1)}, u32[]{:S(2)}, u32[]{:S(2)}) collective-permute-start(bf16[640,128]{1,0:T(8,128)(2,1)S(1)} %pack.1.refs_0_.refs_2_), channel_id=1, source_target_pairs={{0,1},{1,0},{2,3},{3,2},{4,5},{5,4},{6,7},{7,6},{8,9},{9,8},{10,11... | collective-permute-start | bytes 491528 | tf_op jit(solution)/shard_map/ppermute | solution.py:23
  11.9 8.2 %reorder.3.refs_6_.refs_0_ = bf16[8,128,4096]{2,1,0:T(8,128)(2,1)} custom-call(bf16[256,8,4096]{2,1,0:T(8,128)(2,1)} %slab.3), custom_call_target="tpu_custom_call" | custom-call | tf_op jit(solution)/shard_map/reorder/pallas_call | solution.py:257
  20.1 2.5 %collective-permute-done.1.refs_1_.refs_2_ = bf16[640,128]{1,0:T(8,128)(2,1)S(1)} collective-permute-done((bf16[640,128]{1,0:T(8,128)(2,1)S(1)}, bf16[640,128]{1,0:T(8,128)(2,1)S(1)}, u32[]{:S(2)}, u32[]{:S(2)}) %collective-permute-start.1) | collective-permute-done | bytes 163872 | tf_op jit(solution)/shard_map/ppermute | solution.py:23
  22.7 1.6 %collective-permute-start.8 = (bf16[6,256,128]{2,1,0:T(8,128)(2,1)S(1)}, bf16[6,256,128]{2,1,0:T(8,128)(2,1)S(1)}, u32[]{:S(2)}, u32[]{:S(2)}) collective-permute-start(bf16[6,256,128]{2,1,0:T(8,128)(2,1)S(1)} %get-tuple-element.16.refs_3_), channel_id=1, source_target_pairs={{0,16},{4,20},{8,24},{12,28},{16,0},{20,4},{24,8},{28,12},{1,17},{... | collective-permute-start | bytes 1179656 | tf_op jit(solution)/shard_map/ppermute | solution.py:23
  24.2 1.5 %collective-permute-start.6 = (bf16[6,256,128]{2,1,0:T(8,128)(2,1)S(1)}, bf16[6,256,128]{2,1,0:T(8,128)(2,1)S(1)}, u32[]{:S(2)}, u32[]{:S(2)}) collective-permute-start(bf16[6,256,128]{2,1,0:T(8,128)(2,1)S(1)} %get-tuple-element.16.refs_3_), channel_id=1, source_target_pairs={{0,8},{4,12},{8,0},{12,4},{16,24},{20,28},{24,16},{28,20},{1,9},{5... | collective-permute-start | bytes 1179656 | tf_op jit(solution)/shard_map/ppermute | solution.py:23
  25.7 2.5 %collective-permute-start.12 = (bf16[3,128,128]{2,1,0:T(8,128)(2,1)S(1)}, bf16[3,128,128]{2,1,0:T(8,128)(2,1)S(1)}, u32[]{:S(2)}, u32[]{:S(2)}) collective-permute-start(bf16[3,128,128]{2,1,0:T(8,128)(2,1)S(1)} %get-tuple-element.17), channel_id=1, source_target_pairs={{0,3},{1,2},{2,1},{3,0},{4,7},{5,6},{6,5},{7,4},{8,11},{9,10},{10,... | collective-permute-start | bytes 294920 | tf_op jit(solution)/shard_map/ppermute | solution.py:23
  28.2 1.9 %collective-permute-start.10 = (bf16[3,128,128]{2,1,0:T(8,128)(2,1)S(1)}, bf16[3,128,128]{2,1,0:T(8,128)(2,1)S(1)}, u32[]{:S(2)}, u32[]{:S(2)}) collective-permute-start(bf16[3,128,128]{2,1,0:T(8,128)(2,1)S(1)} %get-tuple-element.17), channel_id=1, source_target_pairs={{0,1},{1,0},{2,3},{3,2},{4,5},{5,4},{6,7},{7,6},{8,9},{9,8},{10,11... | collective-permute-start | bytes 294920 | tf_op jit(solution)/shard_map/ppermute | solution.py:23
  30.1 4.4 %reorder.4.refs_10_.refs_1_ = bf16[8,64,4096]{2,1,0:T(8,128)(2,1)} custom-call(bf16[256,8,4096]{2,1,0:T(8,128)(2,1)} %slab.3), custom_call_target="tpu_custom_call" | custom-call | tf_op jit(solution)/shard_map/reorder/pallas_call | solution.py:257
  34.5 1.2 %collective-permute-done.11.refs_8_ = bf16[3,128,128]{2,1,0:T(8,128)(2,1)S(1)} collective-permute-done((bf16[3,128,128]{2,1,0:T(8,128)(2,1)S(1)}, bf16[3,128,128]{2,1,0:T(8,128)(2,1)S(1)}, u32[]{:S(2)}, u32[]{:S(2)}) %collective-permute-start.11) | collective-permute-done | bytes 98336 | tf_op jit(solution)/shard_map/ppermute | solution.py:23
  35.9 0.6 %collective-permute-start.9 = (bf16[3,256,128]{2,1,0:T(8,128)(2,1)S(1)}, bf16[3,256,128]{2,1,0:T(8,128)(2,1)S(1)}, u32[]{:S(2)}, u32[]{:S(2)}) collective-permute-start(bf16[3,256,128]{2,1,0:T(8,128)(2,1)S(1)} %slice.9), channel_id=1, source_target_pairs={{0,8},{4,12},{8,0},{12,4},{16,24},{20,28},{24,16},{28,20},{1,9},{5... | collective-permute-start | bytes 589832 | tf_op jit(solution)/shard_map/ppermute | solution.py:23
  36.5 0.7 %slice.8 = bf16[3,256,128]{2,1,0:T(8,128)(2,1)} slice(bf16[6,256,128]{2,1,0:T(8,128)(2,1)S(1)} %collective-permute-done.6.refs_11_.refs_5_), slice={[0:3], [0:256], [0:128]} | slice | bytes 393216 | tf_op jit(solution)/shard_map/slice | solution.py:397
  37.2 0.5 collective-permute-start.7
  37.8 7.8 %prepare.1 = (bf16[8,128,256]{2,1,0:T(8,128)(2,1)S(1)}, bf16[1024,1024]{1,0:T(8,128)(2,1)S(1)}, bf16[8,24,4096]{2,1,0:T(8,128)(2,1)S(1)}) custom-call(s32[2]{0:T(128)S(1)} %pad_add_fusion.me, s32[2,8]{1,0:T(2,128)S(1)} %copy-done.1, bf16[16,128,128]{2,1,0:T(8,128)(2,1)S(1)} %collect.1.refs_0_, bf16[16,128,128]{2,1,0:T(8,128)(2,1)S(1)} %collective-permute-done.13.refs_1_, ...), custom_call_target="tpu_custom_call" | custom-call | tf_op jit(solution)/shard_map/prepare/pallas_call | solution.py:227
  45.6 2.4 %transform.1.refs_3_ = bf16[8,32,4096]{2,1,0:T(8,128)(2,1)S(1)} custom-call(bf16[640,128]{1,0:T(8,128)(2,1)S(1)} %collective-permute-done.5.refs_5_.refs_6_.refs_0_, bf16[3,256,128]{2,1,0:T(8,128)(2,1)S(1)} %collective-permute-done.7.refs_1_, bf16[3,256,128]{2,1,0:T(8,128)(2,1)S(1)} %collective-permute-done.9.refs_2_, ...), custom_call_target="tpu_custom_call" | custom-call | tf_op jit(solution)/shard_map/transform/pallas_call | solution.py:191
  48.0 0.2 collective-permute-start.14
  48.3 3.4 %reorder.5.refs_2_ = bf16[8,64,4096]{2,1,0:T(8,128)(2,1)S(1)} custom-call(bf16[256,8,4096]{2,1,0:T(8,128)(2,1)} %slab.3), custom_call_target="tpu_custom_call" | custom-call | tf_op jit(solution)/shard_map/reorder/pallas_call | solution.py:257
  51.7 0.6 %collective-permute-done.14.refs_4_ = bf16[8,32,4096]{2,1,0:T(8,128)(2,1)S(1)} collective-permute-done((bf16[8,32,4096]{2,1,0:T(8,128)(2,1)S(1)}, bf16[8,32,4096]{2,1,0:T(8,128)(2,1)S(1)}, u32[]{:S(2)}, u32[]{:S(2)}) %collective-permute-start.14) | collective-permute-done | bytes 2097184 | tf_op jit(solution)/shard_map/ppermute | solution.py:23
  52.3 0.7 %copy-done = bf16[8,64,4096]{2,1,0:T(8,128)(2,1)S(1)} copy-done((bf16[8,64,4096]{2,1,0:T(8,128)(2,1)S(1)}, bf16[8,64,4096]{2,1,0:T(8,128)(2,1)}, u32[]{:S(2)}) %copy-start) | copy-done | bytes 4194328
  53.0 5.5 %contract.1 = f32[64,256]{1,0:T(8,128)} custom-call(f32[64,64]{1,0:T(8,128)S(1)} %fusion.place, bf16[8,128,4096]{2,1,0:T(8,128)(2,1)S(1)} %bitcast.4, bf16[8,64,4096]{2,1,0:T(8,128)(2,1)S(1)} %copy-done, bf16[8,64,4096]{2,1,0:T(8,128)(2,1)S(1)} %reorder.5.refs_2_, bf16[8,32,4096]{2,1,0:T(8,128)(2,1)S(1)} %transform.1.refs_3_, ...), custom_call_target="tpu_custom_call" | custom-call | tf_op jit(solution)/shard_map/contract/pallas_call | solution.py:366
  (29 shorter events, 0.4 us)
Async XLA Ops:
  1.0 9.0 %collective-permute-start.5 = (bf16[640,128]{1,0:T(8,128)(2,1)S(1)}, bf16[640,128]{1,0:T(8,128)(2,1)S(1)}, u32[]{:S(2)}, u32[]{:S(2)}) collective-permute-start(bf16[640,128]{1,0:T(8,128)(2,1)S(1)} %pack.1.refs_0_.refs_2_), channel_id=1, source_target_pairs={{0,24},{4,28},{8,16},{12,20},{16,8},{20,12},{24,0},{28,4},{1,25},{... | collective-permute-start | bytes 491528 | tf_op jit(solution)/shard_map/ppermute | solution.py:23
  4.9 15.2 %collective-permute-start.4 = (bf16[640,128]{1,0:T(8,128)(2,1)S(1)}, bf16[640,128]{1,0:T(8,128)(2,1)S(1)}, u32[]{:S(2)}, u32[]{:S(2)}) collective-permute-start(bf16[640,128]{1,0:T(8,128)(2,1)S(1)} %pack.1.refs_0_.refs_2_), channel_id=1, source_target_pairs={{0,16},{4,20},{8,24},{12,28},{16,0},{20,4},{24,8},{28,12},{1,17},{... | collective-permute-start | bytes 491528 | tf_op jit(solution)/shard_map/ppermute | solution.py:23
  5.4 14.7 %collective-permute-start.3 = (bf16[640,128]{1,0:T(8,128)(2,1)S(1)}, bf16[640,128]{1,0:T(8,128)(2,1)S(1)}, u32[]{:S(2)}, u32[]{:S(2)}) collective-permute-start(bf16[640,128]{1,0:T(8,128)(2,1)S(1)} %pack.1.refs_0_.refs_2_), channel_id=1, source_target_pairs={{0,8},{4,12},{8,0},{12,4},{16,24},{20,28},{24,16},{28,20},{1,9},{5... | collective-permute-start | bytes 491528 | tf_op jit(solution)/shard_map/ppermute | solution.py:23
  5.6 14.6 %collective-permute-start.2 = (bf16[640,128]{1,0:T(8,128)(2,1)S(1)}, bf16[640,128]{1,0:T(8,128)(2,1)S(1)}, u32[]{:S(2)}, u32[]{:S(2)}) collective-permute-start(bf16[640,128]{1,0:T(8,128)(2,1)S(1)} %pack.1.refs_0_.refs_2_), channel_id=1, source_target_pairs={{0,3},{1,2},{2,1},{3,0},{4,7},{5,6},{6,5},{7,4},{8,11},{9,10},{10,... | collective-permute-start | bytes 491528 | tf_op jit(solution)/shard_map/ppermute | solution.py:23
  9.6 13.0 %collective-permute-start.1 = (bf16[640,128]{1,0:T(8,128)(2,1)S(1)}, bf16[640,128]{1,0:T(8,128)(2,1)S(1)}, u32[]{:S(2)}, u32[]{:S(2)}) collective-permute-start(bf16[640,128]{1,0:T(8,128)(2,1)S(1)} %pack.1.refs_0_.refs_2_), channel_id=1, source_target_pairs={{0,2},{1,3},{2,0},{3,1},{4,6},{5,7},{6,4},{7,5},{8,10},{9,11},{10,... | collective-permute-start | bytes 491528 | tf_op jit(solution)/shard_map/ppermute | solution.py:23
  10.0 12.7 %collective-permute-start = (bf16[640,128]{1,0:T(8,128)(2,1)S(1)}, bf16[640,128]{1,0:T(8,128)(2,1)S(1)}, u32[]{:S(2)}, u32[]{:S(2)}) collective-permute-start(bf16[640,128]{1,0:T(8,128)(2,1)S(1)} %pack.1.refs_0_.refs_2_), channel_id=1, source_target_pairs={{0,1},{1,0},{2,3},{3,2},{4,5},{5,4},{6,7},{7,6},{8,9},{9,8},{10,11... | collective-permute-start | bytes 491528 | tf_op jit(solution)/shard_map/ppermute | solution.py:23
  22.7 13.1 %collective-permute-start.8 = (bf16[6,256,128]{2,1,0:T(8,128)(2,1)S(1)}, bf16[6,256,128]{2,1,0:T(8,128)(2,1)S(1)}, u32[]{:S(2)}, u32[]{:S(2)}) collective-permute-start(bf16[6,256,128]{2,1,0:T(8,128)(2,1)S(1)} %get-tuple-element.16.refs_3_), channel_id=1, source_target_pairs={{0,16},{4,20},{8,24},{12,28},{16,0},{20,4},{24,8},{28,12},{1,17},{... | collective-permute-start | bytes 1179656 | tf_op jit(solution)/shard_map/ppermute | solution.py:23
  24.2 11.5 %collective-permute-start.6 = (bf16[6,256,128]{2,1,0:T(8,128)(2,1)S(1)}, bf16[6,256,128]{2,1,0:T(8,128)(2,1)S(1)}, u32[]{:S(2)}, u32[]{:S(2)}) collective-permute-start(bf16[6,256,128]{2,1,0:T(8,128)(2,1)S(1)} %get-tuple-element.16.refs_3_), channel_id=1, source_target_pairs={{0,8},{4,12},{8,0},{12,4},{16,24},{20,28},{24,16},{28,20},{1,9},{5... | collective-permute-start | bytes 1179656 | tf_op jit(solution)/shard_map/ppermute | solution.py:23
  25.7 8.8 %collective-permute-start.12 = (bf16[3,128,128]{2,1,0:T(8,128)(2,1)S(1)}, bf16[3,128,128]{2,1,0:T(8,128)(2,1)S(1)}, u32[]{:S(2)}, u32[]{:S(2)}) collective-permute-start(bf16[3,128,128]{2,1,0:T(8,128)(2,1)S(1)} %get-tuple-element.17), channel_id=1, source_target_pairs={{0,3},{1,2},{2,1},{3,0},{4,7},{5,6},{6,5},{7,4},{8,11},{9,10},{10,... | collective-permute-start | bytes 294920 | tf_op jit(solution)/shard_map/ppermute | solution.py:23
  28.2 7.6 %collective-permute-start.11 = (bf16[3,128,128]{2,1,0:T(8,128)(2,1)S(1)}, bf16[3,128,128]{2,1,0:T(8,128)(2,1)S(1)}, u32[]{:S(2)}, u32[]{:S(2)}) collective-permute-start(bf16[3,128,128]{2,1,0:T(8,128)(2,1)S(1)} %get-tuple-element.17), channel_id=1, source_target_pairs={{0,2},{1,3},{2,0},{3,1},{4,6},{5,7},{6,4},{7,5},{8,10},{9,11},{10,... | collective-permute-start | bytes 294920 | tf_op jit(solution)/shard_map/ppermute | solution.py:23
  28.2 7.6 %collective-permute-start.10 = (bf16[3,128,128]{2,1,0:T(8,128)(2,1)S(1)}, bf16[3,128,128]{2,1,0:T(8,128)(2,1)S(1)}, u32[]{:S(2)}, u32[]{:S(2)}) collective-permute-start(bf16[3,128,128]{2,1,0:T(8,128)(2,1)S(1)} %get-tuple-element.17), channel_id=1, source_target_pairs={{0,1},{1,0},{2,3},{3,2},{4,5},{5,4},{6,7},{7,6},{8,9},{9,8},{10,11... | collective-permute-start | bytes 294920 | tf_op jit(solution)/shard_map/ppermute | solution.py:23
  34.5 3.3 %copy-start.1 = (s32[2,8]{1,0:T(2,128)S(1)}, s32[2,8]{1,0:T(2,128)}, u32[]{:S(2)}) copy-start(s32[2,8]{1,0:T(2,128)} %pair.1) | copy-start | bytes 196
  35.8 2.0 %collective-permute-start.13 = (bf16[16,128,128]{2,1,0:T(8,128)(2,1)S(1)}, bf16[16,128,128]{2,1,0:T(8,128)(2,1)S(1)}, u32[]{:S(2)}, u32[]{:S(2)}) collective-permute-start(bf16[16,128,128]{2,1,0:T(8,128)(2,1)S(1)} %collect.1.refs_0_), channel_id=1, source_target_pairs={{0,4},{4,0},{8,12},{12,8},{16,20},{20,16},{24,28},{28,24},{1,5},{5... | collective-permute-start | bytes 1572872 | tf_op jit(solution)/shard_map/ppermute | solution.py:23
  35.9 9.7 %collective-permute-start.9 = (bf16[3,256,128]{2,1,0:T(8,128)(2,1)S(1)}, bf16[3,256,128]{2,1,0:T(8,128)(2,1)S(1)}, u32[]{:S(2)}, u32[]{:S(2)}) collective-permute-start(bf16[3,256,128]{2,1,0:T(8,128)(2,1)S(1)} %slice.9), channel_id=1, source_target_pairs={{0,8},{4,12},{8,0},{12,4},{16,24},{20,28},{24,16},{28,20},{1,9},{5... | collective-permute-start | bytes 589832 | tf_op jit(solution)/shard_map/ppermute | solution.py:23
  37.2 8.4 %collective-permute-start.7 = (bf16[3,256,128]{2,1,0:T(8,128)(2,1)}, bf16[3,256,128]{2,1,0:T(8,128)(2,1)S(1)}, u32[]{:S(2)}, u32[]{:S(2)}) collective-permute-start(bf16[3,256,128]{2,1,0:T(8,128)(2,1)} %slice.8), channel_id=1, source_target_pairs={{0,16},{4,20},{8,24},{12,28},{16,0},{20,4},{24,8},{28,12},{1,17},{... | collective-permute-start | bytes 589832 | tf_op jit(solution)/shard_map/ppermute | solution.py:23
  45.6 6.6 %slice-start = ((s8[8388608]{0:T(1024)(128)(4,1)}), s8[4194304]{0:T(1024)(128)(4,1)S(1)}, s32[]{:S(2)}) async-start(s8[8388608]{0:T(1024)(128)(4,1)} %bitcast.3), calls=%async_computation | async-start | bytes 8388608
  48.0 4.2 %collective-permute-start.14 = (bf16[8,32,4096]{2,1,0:T(8,128)(2,1)S(1)}, bf16[8,32,4096]{2,1,0:T(8,128)(2,1)S(1)}, u32[]{:S(2)}, u32[]{:S(2)}) collective-permute-start(bf16[8,32,4096]{2,1,0:T(8,128)(2,1)S(1)} %transform.1.refs_3_), channel_id=1, source_target_pairs={{0,4},{4,0},{8,12},{12,8},{16,20},{20,16},{24,28},{28,24},{1,5},{5... | collective-permute-start | bytes 6291464 | tf_op jit(solution)/shard_map/ppermute | solution.py:23
  48.2 4.0 %slice-start.1 = ((s8[8388608]{0:T(1024)(128)(4,1)}), s8[4194304]{0:T(1024)(128)(4,1)S(1)}, s32[]{:S(2)}) async-start(s8[8388608]{0:T(1024)(128)(4,1)} %bitcast.3), calls=%async_computation.1 | async-start | bytes 8388608
  48.3 4.7 %copy-start = (bf16[8,64,4096]{2,1,0:T(8,128)(2,1)S(1)}, bf16[8,64,4096]{2,1,0:T(8,128)(2,1)}, u32[]{:S(2)}) copy-start(bf16[8,64,4096]{2,1,0:T(8,128)(2,1)} %reorder.4.refs_10_.refs_1_) | copy-start | bytes 12582916

commit v4 on v3

--- a/solution.py
+++ b/solution.py
@@ -13,6 +13,7 @@
 F32 = jnp.float32
 BF16 = jnp.bfloat16
 MIB = 1024 * 1024
+PAD = 16
 NT = (((1,), (1,)), ((), ()))
 IN_VMEM = pl.BlockSpec(memory_space=pltpu.VMEM)
 IN_PLACE = pl.BlockSpec(memory_space=pl.ANY)
@@ -51,11 +52,16 @@
     place = 0
     for ref in g_refs:
         for z in range(ref.shape[0]):
+            at = place
+            if strip % 16 == 0:
+                e, c = divmod(place // (nz * strip), nao // (nz * strip) // 2)
+                at = ((me[0] ^ (2 * c + e)) * nz + (me[1] ^ (z % nz))) * strip
+                at = pl.multiple_of(at, strip)
             for group in range(4):
                 base = group * 2 * strip
                 lanes = slice(group * LANES, (group + 1) * LANES)
                 occ_g[place : place + strip, lanes] = ref[z, base : base + strip, :]
-                virt_g[place : place + strip, lanes] = ref[z, base + strip : base + 2 * strip, :]
+                virt_g[pl.ds(at, strip), lanes] = ref[z, base + strip : base + 2 * strip, :]
             place += strip
     at = iota((1, nao), 1)
     block = at // (nz * strip)
@@ -80,6 +86,22 @@
         for lo in range(2):
             occ_out[l, lo * BLK : (lo + 1) * BLK, :] = table[l * BLK : (l + 1) * BLK, lo * side : (lo + 1) * side]
 
+    side = iota((1, LANES), 1) // BLK
+    low = jnp.bitwise_and(iota((1, nl * LANES), 1), BLK) == 0
+    keep = [hot(low), hot(jnp.logical_not(low))]
+    if strip % 16 == 0:
+        for l in range(nl):
+            block = pair[1, l]
+            group = pl.multiple_of((block // 2) * LANES, LANES)
+            part = virt_g[:, pl.ds(group, LANES)].astype(F32)
+            wide[:, l * LANES : (l + 1) * LANES] = jnp.where(
+                side == block % 2, part, pltpu.roll(part, BLK, 1)
+            ).astype(BF16)
+        for k in range(nk):
+            part = wide[pl.ds(pl.multiple_of(pair[1, k_of[k]] * BLK, BLK), BLK), :]
+            for lo in range(2):
+                virt_out[k * LANES + lo * BLK : k * LANES + (lo + 1) * BLK, :] = part * keep[lo]
+        return
     for k in range(nk):
         row = pair[1, k_of[k]] * BLK + iota((BLK, 1), 0)
         pick[k * BLK : (k + 1) * BLK, :] = hot(row == held)
@@ -90,7 +112,7 @@
     full = dot(picked, wide[...])
     for k in range(nk):
         part = full[k * BLK : (k + 1) * BLK, :]
-        low = (iota(part.shape, 1) // BLK) % 2 == 0
+        low = jnp.bitwise_and(iota(part.shape, 1), BLK) == 0
         virt_out[k * LANES : k * LANES + BLK, :] = jnp.where(low, part, 0.0).astype(BF16)
         virt_out[k * LANES + BLK : (k + 1) * LANES, :] = jnp.where(low, 0.0, part).astype(BF16)
 
@@ -133,21 +155,24 @@
     nl = occ.shape[0]
     count = len(blocks)
     per = rows // HALF
-    for e in range(count):
-        k = 0
-        for ref, length in blocks[e]:
-            for j in range(length):
-                held = ref[j] if len(ref.shape) == 3 else ref[j * rows : (j + 1) * rows, :]
-                for l in range(0, nl, 2):
-                    weights = virt[k * LANES : (k + 1) * LANES, l * LANES : (l + 2) * LANES]
-                    x = dot(held, weights).astype(BF16)
-                    for i in range(2):
-                        for p in range(per):
-                            at = (e * per + p) * LANES
-                            x_buf[l + i, k * HALF : (k + 1) * HALF, at : at + LANES] = x[
-                                p * HALF : (p + 1) * HALF, i * LANES : (i + 1) * LANES
-                            ]
-                k += 1
+    held = []
+    for block in blocks:
+        held.append([])
+        for ref, length in block:
+            held[-1] += [(ref, j) for j in range(length)]
+    for k in range(len(held[0])):
+        block_rows = [
+            ref[j] if len(ref.shape) == 3 else ref[j * rows : (j + 1) * rows, :] for ref, j in (h[k] for h in held)
+        ]
+        block_rows = jnp.concatenate(block_rows, axis=0) if count > 1 else block_rows[0]
+        for l in range(0, nl, 2):
+            weights = virt[k * LANES : (k + 1) * LANES, l * LANES : (l + 2) * LANES]
+            x = dot(block_rows, weights).astype(BF16)
+            for i in range(2):
+                for p in range(count * per):
+                    x_buf[l + i, k * HALF : (k + 1) * HALF, p * LANES : (p + 1) * LANES] = x[
+                        p * HALF : (p + 1) * HALF, i * LANES : (i + 1) * LANES
+                    ]
     low = iota((HALF, LANES), 1) < BLK
     for l in range(nl):
         y = dot(occ[l], x_buf[l])
@@ -236,15 +261,19 @@
     )(me, pair_index, *g_blocks, *flat, *after)
 
 
-def reorder_kernel(slab, out):
+def reorder_kernel(slab, out, order):
     q, nl, tile = slab.shape
+    n = q * nl
+
+    @pl.when(pl.program_id(0) == 0)
+    def _():
+        for l in range(nl):
+            order[l * q : (l + 1) * q, :] = hot(iota((q, n), 1) == iota((q, n), 0) * nl + l)
+
     at = 0 if out.shape[1] == q else pl.multiple_of(pl.program_id(0) * q, q)
-    n = q * nl
-    row, col = iota((n, n), 0), iota((n, n), 1)
-    order = hot((row % q) * nl + row // q == col)
     step = 512
     for t in range(0, tile, step):
-        moved = dot(order, slab[:, :, t : t + step].reshape(n, step)).astype(BF16)
+        moved = dot(order[...], slab[:, :, t : t + step].reshape(n, step)).astype(BF16)
         for l in range(nl):
             out[l, pl.ds(at, q), t : t + step] = moved[l * q : (l + 1) * q]
 
@@ -260,12 +289,13 @@
         in_specs=[pl.BlockSpec((q, nl, tile), lambda i: (skip + i, 0, 0))],
         out_specs=IN_VMEM if space == pltpu.VMEM else pl.BlockSpec((nl, q, tile), lambda i: (0, i, 0)),
         out_shape=space((nl, steps * q, tile), BF16),
-        compiler_params=pltpu.CompilerParams(vmem_limit_bytes=24 * MIB),
+        scratch_shapes=[pltpu.VMEM((q * nl, q * nl), BF16)],
+        compiler_params=pltpu.CompilerParams(vmem_limit_bytes=16 * MIB),
         name="reorder",
     )(in_hbm(slab))
 
 
-def pack_kernel(b_in, occ_in, virt_in, out, b_rows, g_occ, g_virt, sems):
+def pack_kernel(b_in, occ_in, virt_in, out, padded, b_rows, g_occ, g_virt, sems):
     moves = [
         pltpu.make_async_copy(source, to, sems.at[i])
         for i, (source, to) in enumerate(((b_in, b_rows), (occ_in, g_occ), (virt_in, g_virt)))
@@ -285,6 +315,8 @@
         for ref in (g_occ, g_virt):
             out[at : at + strip, :] = ref[:, i : i + LANES]
             at += strip
+    padded[:at, :] = out[...]
+    padded[at:, :] = jnp.zeros_like(padded[at:, :])
 
 
 def pack(b_rows, g_occ, g_virt):
@@ -292,8 +324,8 @@
     return pl.pallas_call(
         pack_kernel,
         in_specs=[IN_PLACE] * 3,
-        out_specs=IN_VMEM,
-        out_shape=jax.ShapeDtypeStruct((total, LANES), BF16),
+        out_specs=[IN_VMEM, IN_VMEM],
+        out_shape=(jax.ShapeDtypeStruct((total, LANES), BF16), jax.ShapeDtypeStruct((total + PAD, LANES), BF16)),
         scratch_shapes=[pltpu.VMEM(x.shape, BF16) for x in (b_rows, g_occ, g_virt)] + [pltpu.SemaphoreType.DMA((3,))],
         compiler_params=pltpu.CompilerParams(vmem_limit_bytes=8 * MIB),
         name="pack",
@@ -313,7 +345,7 @@
 
 
 def stack(column, side, split, k_local, after):
-    one = column[0].shape[0] - split
+    one = side[0].shape[0] - split
     return pl.pallas_call(
         functools.partial(stack_kernel, split, len(column) + 1, len(after)),
         in_specs=[IN_VMEM] * (len(column) + len(side)) + [IN_PLACE] * len(after),
@@ -330,7 +362,7 @@
 def collect_kernel(split, nz, sides, *refs):
     near, side, far, out = refs[:nz], refs[nz : nz + sides], refs[nz + sides : 2 * nz + sides - 1], refs[-1]
     for z, ref in enumerate(near):
-        out[z] = ref[split:, :]
+        out[z] = ref[split : split + out.shape[1], :]
     for e, ref in enumerate(side):
         out[(e + 1) * nz] = ref[split:, :]
         for z, block in enumerate(far):
@@ -381,10 +413,10 @@
     rows = per * HALF
     split = k_local * rows
 
-    own = pack(b_rows, g_occ, g_virt)
+    own, padded = pack(b_rows, g_occ, g_virt)
 
     side = [swap(own, "aux", na, e) for e in outer[1:]]
-    column = [swap(own, "pair", nz, d) for d in range(1, nz)]
+    column = [swap(padded, "pair", nz, d) for d in range(1, nz)]
     slabs = [reorder(b_slab, 0, 2, 4, pltpu.HBM)]
     b_z, g_side = stack(column, side, split, k_local, [in_hbm(slabs[0])])
 

time: 58.6 us -> 57.9 us (0.988)
  starting transfers between devices: 19.4 us -> 18.5 us
  waiting for transfers between devices: 4.72 us -> 5.33 us
    ppermute x15, starting transfers between devices: 19.4 us -> 18.5 us  [swap(): return lax.ppermute(value, axis, [(i, i ^ offset) for i in range(size)])]
    ppermute x15, waiting for transfers between devices: 4.72 us -> 5.33 us  [swap(): return lax.ppermute(value, axis, [(i, i ^ offset) for i in range(size)])]
    pallas_call x1, Pallas kernels: 7.78 us -> 7.17 us  [prepare(): pl.pallas_call(functools.partial(prepare_kernel, layout, rows, len(g_bloc...]
  transfers between devices with their start and end apart: 15 -> 15, of which waited for: 4 -> 3; matrix products, arithmetic and copies ran while one was open for 1% -> 1% of each run, Pallas kernels for 41% -> 40%
where the time goes in v4:
time: 57.9 us; the launch traced here: 57.7 us
  Pallas kernels  32.2 us (56%)
  starting transfers between devices  18.5 us (32%)
  waiting for transfers between devices  5.33 us (9%)
  local copies, waits for them, and re-layouts  1.34 us (2%)
    ppermute x15, starting transfers between devices, swap(): return lax.ppermute(value, axis, [(i, i ^ offset) for i in range(size)])  18.5 us
    pallas_call x3, Pallas kernels, reorder(): pl.pallas_call(reorder_kernel, grid=(steps,), in_specs=[pl.BlockSpec((q,...  16.1 us
    pallas_call x1, Pallas kernels, prepare(): pl.pallas_call(functools.partial(prepare_kernel, layout, rows, len(g_bloc...  7.17 us
    pallas_call x1, Pallas kernels, contract(): pl.pallas_call(functools.partial(contract_kernel, parts), in_specs=[IN_VM...  5.51 us
    ppermute x15, waiting for transfers between devices, swap(): return lax.ppermute(value, axis, [(i, i ^ offset) for i in range(size)])  5.33 us
    pallas_call x1, Pallas kernels, transform(): pl.pallas_call(functools.partial(transform_kernel, layout, rows), grid=(n...  2.37 us
  transfers between devices with their start and end apart: 15, of which 3 were waited for; matrix products, arithmetic and copies ran while one was open for 1% of the time, Pallas kernels for 40%

profile of v4, /device:TPU:0, one launch (start us, length us, event | category | flops | bytes accessed | tf_op | source)
XLA Modules:
  0.0 57.7 jit_solution(11815388317321037423)
XLA Ops:
  0.0 1.0 %pack.1 = (bf16[640,128]{1,0:T(8,128)(2,1)S(1)}, bf16[656,128]{1,0:T(8,128)(2,1)S(1)}) custom-call(bf16[8,2,4096]{2,1,0:T(2,128)(2,1)} %b_in.1, bf16[16,512]{1,0:T(8,128)(2,1)} %occ_in.1, bf16[16,512]{1,0:T(8,128)(2,1)} %virt_in.1), custom_call_target="tpu_custom_call" | custom-call | tf_op jit(solution)/shard_map/pack/pallas_call | solution.py:324
  1.0 4.0 %collective-permute-start.5 = (bf16[640,128]{1,0:T(8,128)(2,1)S(1)}, bf16[640,128]{1,0:T(8,128)(2,1)S(1)}, u32[]{:S(2)}, u32[]{:S(2)}) collective-permute-start(bf16[640,128]{1,0:T(8,128)(2,1)S(1)} %get-tuple-element.17.refs_0_.refs_2_), channel_id=1, source_target_pairs={{0,24},{4,28},{8,16},{12,20},{16,8},{20,12},{24,0},{28,4},{1,25},{... | collective-permute-start | bytes 491528 | tf_op jit(solution)/shard_map/ppermute | solution.py:24
  5.0 3.6 %collective-permute-start.2 = (bf16[656,128]{1,0:T(8,128)(2,1)S(1)}, bf16[656,128]{1,0:T(8,128)(2,1)S(1)}, u32[]{:S(2)}, u32[]{:S(2)}) collective-permute-start(bf16[656,128]{1,0:T(8,128)(2,1)S(1)} %get-tuple-element.16), channel_id=1, source_target_pairs={{0,3},{1,2},{2,1},{3,0},{4,7},{5,6},{6,5},{7,4},{8,11},{9,10},{10,... | collective-permute-start | bytes 503816 | tf_op jit(solution)/shard_map/ppermute | solution.py:24
  8.6 0.8 %collective-permute-start = (bf16[656,128]{1,0:T(8,128)(2,1)S(1)}, bf16[656,128]{1,0:T(8,128)(2,1)S(1)}, u32[]{:S(2)}, u32[]{:S(2)}) collective-permute-start(bf16[656,128]{1,0:T(8,128)(2,1)S(1)} %get-tuple-element.16), channel_id=1, source_target_pairs={{0,1},{1,0},{2,3},{3,2},{4,5},{5,4},{6,7},{7,6},{8,9},{9,8},{10,11... | collective-permute-start | bytes 503816 | tf_op jit(solution)/shard_map/ppermute | solution.py:24
  9.3 0.5 collective-permute-start.4
  9.9 1.0 %collective-permute-start.3 = (bf16[640,128]{1,0:T(8,128)(2,1)S(1)}, bf16[640,128]{1,0:T(8,128)(2,1)S(1)}, u32[]{:S(2)}, u32[]{:S(2)}) collective-permute-start(bf16[640,128]{1,0:T(8,128)(2,1)S(1)} %get-tuple-element.17.refs_0_.refs_2_), channel_id=1, source_target_pairs={{0,8},{4,12},{8,0},{12,4},{16,24},{20,28},{24,16},{28,20},{1,9},{5... | collective-permute-start | bytes 491528 | tf_op jit(solution)/shard_map/ppermute | solution.py:24
  10.8 8.3 %reorder.3.refs_6_.refs_0_ = bf16[8,128,4096]{2,1,0:T(8,128)(2,1)} custom-call(bf16[256,8,4096]{2,1,0:T(8,128)(2,1)} %slab.3), custom_call_target="tpu_custom_call" | custom-call | tf_op jit(solution)/shard_map/reorder/pallas_call | solution.py:286
  19.1 3.4 %collective-permute-done.1.refs_1_.refs_2_ = bf16[656,128]{1,0:T(8,128)(2,1)S(1)} collective-permute-done((bf16[656,128]{1,0:T(8,128)(2,1)S(1)}, bf16[656,128]{1,0:T(8,128)(2,1)S(1)}, u32[]{:S(2)}, u32[]{:S(2)}) %collective-permute-start.1) | collective-permute-done | bytes 167968 | tf_op jit(solution)/shard_map/ppermute | solution.py:24
  22.6 0.6 collective-permute-start.8
  23.1 0.5 collective-permute-start.6
  23.7 2.5 %collective-permute-start.12 = (bf16[3,128,128]{2,1,0:T(8,128)(2,1)S(1)}, bf16[3,128,128]{2,1,0:T(8,128)(2,1)S(1)}, u32[]{:S(2)}, u32[]{:S(2)}) collective-permute-start(bf16[3,128,128]{2,1,0:T(8,128)(2,1)S(1)} %get-tuple-element.21), channel_id=1, source_target_pairs={{0,3},{1,2},{2,1},{3,0},{4,7},{5,6},{6,5},{7,4},{8,11},{9,10},{10,... | collective-permute-start | bytes 294920 | tf_op jit(solution)/shard_map/ppermute | solution.py:24
  26.1 1.9 %collective-permute-start.10 = (bf16[3,128,128]{2,1,0:T(8,128)(2,1)S(1)}, bf16[3,128,128]{2,1,0:T(8,128)(2,1)S(1)}, u32[]{:S(2)}, u32[]{:S(2)}) collective-permute-start(bf16[3,128,128]{2,1,0:T(8,128)(2,1)S(1)} %get-tuple-element.21), channel_id=1, source_target_pairs={{0,1},{1,0},{2,3},{3,2},{4,5},{5,4},{6,7},{7,6},{8,9},{9,8},{10,11... | collective-permute-start | bytes 294920 | tf_op jit(solution)/shard_map/ppermute | solution.py:24
  28.1 4.4 %reorder.4.refs_10_.refs_1_ = bf16[8,64,4096]{2,1,0:T(8,128)(2,1)} custom-call(bf16[256,8,4096]{2,1,0:T(8,128)(2,1)} %slab.3), custom_call_target="tpu_custom_call" | custom-call | tf_op jit(solution)/shard_map/reorder/pallas_call | solution.py:286
  32.5 1.2 %collective-permute-done.11.refs_8_ = bf16[3,128,128]{2,1,0:T(8,128)(2,1)S(1)} collective-permute-done((bf16[3,128,128]{2,1,0:T(8,128)(2,1)S(1)}, bf16[3,128,128]{2,1,0:T(8,128)(2,1)S(1)}, u32[]{:S(2)}, u32[]{:S(2)}) %collective-permute-start.11) | collective-permute-done | bytes 98336 | tf_op jit(solution)/shard_map/ppermute | solution.py:24
  33.9 1.6 %collective-permute-start.9 = (bf16[3,256,128]{2,1,0:T(8,128)(2,1)S(1)}, bf16[3,256,128]{2,1,0:T(8,128)(2,1)S(1)}, u32[]{:S(2)}, u32[]{:S(2)}) collective-permute-start(bf16[3,256,128]{2,1,0:T(8,128)(2,1)S(1)} %slice.9), channel_id=1, source_target_pairs={{0,8},{4,12},{8,0},{12,4},{16,24},{20,28},{24,16},{28,20},{1,9},{5... | collective-permute-start | bytes 589832 | tf_op jit(solution)/shard_map/ppermute | solution.py:24
  35.4 0.7 %slice.8 = bf16[3,256,128]{2,1,0:T(8,128)(2,1)} slice(bf16[6,256,128]{2,1,0:T(8,128)(2,1)S(1)} %collective-permute-done.6.refs_11_.refs_5_), slice={[0:3], [0:256], [0:128]} | slice | bytes 393216 | tf_op jit(solution)/shard_map/slice | solution.py:429
  36.1 1.5 %collective-permute-start.7 = (bf16[3,256,128]{2,1,0:T(8,128)(2,1)}, bf16[3,256,128]{2,1,0:T(8,128)(2,1)S(1)}, u32[]{:S(2)}, u32[]{:S(2)}) collective-permute-start(bf16[3,256,128]{2,1,0:T(8,128)(2,1)} %slice.8), channel_id=1, source_target_pairs={{0,16},{4,20},{8,24},{12,28},{16,0},{20,4},{24,8},{28,12},{1,17},{... | collective-permute-start | bytes 589832 | tf_op jit(solution)/shard_map/ppermute | solution.py:24
  37.6 0.1 pad_add_fusion.me
  37.7 7.2 %prepare.1 = (bf16[8,128,256]{2,1,0:T(8,128)(2,1)S(1)}, bf16[1024,1024]{1,0:T(8,128)(2,1)S(1)}, bf16[8,24,4096]{2,1,0:T(8,128)(2,1)S(1)}) custom-call(s32[2]{0:T(128)S(1)} %pad_add_fusion.me, s32[2,8]{1,0:T(2,128)S(1)} %copy-done.1, bf16[16,128,128]{2,1,0:T(8,128)(2,1)S(1)} %collect.1.refs_0_, bf16[16,128,128]{2,1,0:T(8,128)(2,1)S(1)} %collective-permute-done.13.refs_1_, ...), custom_call_target="tpu_custom_call" | custom-call | tf_op jit(solution)/shard_map/prepare/pallas_call | solution.py:252
  44.9 2.4 %transform.1.refs_3_ = bf16[8,32,4096]{2,1,0:T(8,128)(2,1)S(1)} custom-call(bf16[640,128]{1,0:T(8,128)(2,1)S(1)} %collective-permute-done.5.refs_5_.refs_6_.refs_0_, bf16[3,256,128]{2,1,0:T(8,128)(2,1)S(1)} %collective-permute-done.7.refs_1_, bf16[3,256,128]{2,1,0:T(8,128)(2,1)S(1)} %collective-permute-done.9.refs_2_, ...), custom_call_target="tpu_custom_call" | custom-call | tf_op jit(solution)/shard_map/transform/pallas_call | solution.py:216
  47.4 3.4 %reorder.5.refs_2_ = bf16[8,64,4096]{2,1,0:T(8,128)(2,1)S(1)} custom-call(bf16[256,8,4096]{2,1,0:T(8,128)(2,1)} %slab.3), custom_call_target="tpu_custom_call" | custom-call | tf_op jit(solution)/shard_map/reorder/pallas_call | solution.py:286
  50.9 0.7 %collective-permute-done.14.refs_4_ = bf16[8,32,4096]{2,1,0:T(8,128)(2,1)S(1)} collective-permute-done((bf16[8,32,4096]{2,1,0:T(8,128)(2,1)S(1)}, bf16[8,32,4096]{2,1,0:T(8,128)(2,1)S(1)}, u32[]{:S(2)}, u32[]{:S(2)}) %collective-permute-start.14) | collective-permute-done | bytes 2097184 | tf_op jit(solution)/shard_map/ppermute | solution.py:24
  51.5 0.6 %copy-done = bf16[8,64,4096]{2,1,0:T(8,128)(2,1)S(1)} copy-done((bf16[8,64,4096]{2,1,0:T(8,128)(2,1)S(1)}, bf16[8,64,4096]{2,1,0:T(8,128)(2,1)}, u32[]{:S(2)}) %copy-start) | copy-done | bytes 4194328
  52.1 5.5 %contract.1 = f32[64,256]{1,0:T(8,128)} custom-call(f32[64,64]{1,0:T(8,128)S(1)} %fusion.place, bf16[8,128,4096]{2,1,0:T(8,128)(2,1)S(1)} %bitcast.4, bf16[8,64,4096]{2,1,0:T(8,128)(2,1)S(1)} %copy-done, bf16[8,64,4096]{2,1,0:T(8,128)(2,1)S(1)} %reorder.5.refs_2_, bf16[8,32,4096]{2,1,0:T(8,128)(2,1)S(1)} %transform.1.refs_3_, ...), custom_call_target="tpu_custom_call" | custom-call | tf_op jit(solution)/shard_map/contract/pallas_call | solution.py:398
  (29 shorter events, 0.3 us)
Async XLA Ops:
  1.0 8.9 %collective-permute-start.5 = (bf16[640,128]{1,0:T(8,128)(2,1)S(1)}, bf16[640,128]{1,0:T(8,128)(2,1)S(1)}, u32[]{:S(2)}, u32[]{:S(2)}) collective-permute-start(bf16[640,128]{1,0:T(8,128)(2,1)S(1)} %get-tuple-element.17.refs_0_.refs_2_), channel_id=1, source_target_pairs={{0,24},{4,28},{8,16},{12,20},{16,8},{20,12},{24,0},{28,4},{1,25},{... | collective-permute-start | bytes 491528 | tf_op jit(solution)/shard_map/ppermute | solution.py:24
  5.0 14.2 %collective-permute-start.2 = (bf16[656,128]{1,0:T(8,128)(2,1)S(1)}, bf16[656,128]{1,0:T(8,128)(2,1)S(1)}, u32[]{:S(2)}, u32[]{:S(2)}) collective-permute-start(bf16[656,128]{1,0:T(8,128)(2,1)S(1)} %get-tuple-element.16), channel_id=1, source_target_pairs={{0,3},{1,2},{2,1},{3,0},{4,7},{5,6},{6,5},{7,4},{8,11},{9,10},{10,... | collective-permute-start | bytes 503816 | tf_op jit(solution)/shard_map/ppermute | solution.py:24
  8.6 14.0 %collective-permute-start.1 = (bf16[656,128]{1,0:T(8,128)(2,1)S(1)}, bf16[656,128]{1,0:T(8,128)(2,1)S(1)}, u32[]{:S(2)}, u32[]{:S(2)}) collective-permute-start(bf16[656,128]{1,0:T(8,128)(2,1)S(1)} %get-tuple-element.16), channel_id=1, source_target_pairs={{0,2},{1,3},{2,0},{3,1},{4,6},{5,7},{6,4},{7,5},{8,10},{9,11},{10,... | collective-permute-start | bytes 503816 | tf_op jit(solution)/shard_map/ppermute | solution.py:24
  8.6 14.0 %collective-permute-start = (bf16[656,128]{1,0:T(8,128)(2,1)S(1)}, bf16[656,128]{1,0:T(8,128)(2,1)S(1)}, u32[]{:S(2)}, u32[]{:S(2)}) collective-permute-start(bf16[656,128]{1,0:T(8,128)(2,1)S(1)} %get-tuple-element.16), channel_id=1, source_target_pairs={{0,1},{1,0},{2,3},{3,2},{4,5},{5,4},{6,7},{7,6},{8,9},{9,8},{10,11... | collective-permute-start | bytes 503816 | tf_op jit(solution)/shard_map/ppermute | solution.py:24
  9.3 9.8 %collective-permute-start.4 = (bf16[640,128]{1,0:T(8,128)(2,1)S(1)}, bf16[640,128]{1,0:T(8,128)(2,1)S(1)}, u32[]{:S(2)}, u32[]{:S(2)}) collective-permute-start(bf16[640,128]{1,0:T(8,128)(2,1)S(1)} %get-tuple-element.17.refs_0_.refs_2_), channel_id=1, source_target_pairs={{0,16},{4,20},{8,24},{12,28},{16,0},{20,4},{24,8},{28,12},{1,17},{... | collective-permute-start | bytes 491528 | tf_op jit(solution)/shard_map/ppermute | solution.py:24
  9.9 9.2 %collective-permute-start.3 = (bf16[640,128]{1,0:T(8,128)(2,1)S(1)}, bf16[640,128]{1,0:T(8,128)(2,1)S(1)}, u32[]{:S(2)}, u32[]{:S(2)}) collective-permute-start(bf16[640,128]{1,0:T(8,128)(2,1)S(1)} %get-tuple-element.17.refs_0_.refs_2_), channel_id=1, source_target_pairs={{0,8},{4,12},{8,0},{12,4},{16,24},{20,28},{24,16},{28,20},{1,9},{5... | collective-permute-start | bytes 491528 | tf_op jit(solution)/shard_map/ppermute | solution.py:24
  22.6 11.1 %collective-permute-start.8 = (bf16[6,256,128]{2,1,0:T(8,128)(2,1)S(1)}, bf16[6,256,128]{2,1,0:T(8,128)(2,1)S(1)}, u32[]{:S(2)}, u32[]{:S(2)}) collective-permute-start(bf16[6,256,128]{2,1,0:T(8,128)(2,1)S(1)} %get-tuple-element.20.refs_3_), channel_id=1, source_target_pairs={{0,16},{4,20},{8,24},{12,28},{16,0},{20,4},{24,8},{28,12},{1,17},{... | collective-permute-start | bytes 1179656 | tf_op jit(solution)/shard_map/ppermute | solution.py:24
  23.1 10.6 %collective-permute-start.6 = (bf16[6,256,128]{2,1,0:T(8,128)(2,1)S(1)}, bf16[6,256,128]{2,1,0:T(8,128)(2,1)S(1)}, u32[]{:S(2)}, u32[]{:S(2)}) collective-permute-start(bf16[6,256,128]{2,1,0:T(8,128)(2,1)S(1)} %get-tuple-element.20.refs_3_), channel_id=1, source_target_pairs={{0,8},{4,12},{8,0},{12,4},{16,24},{20,28},{24,16},{28,20},{1,9},{5... | collective-permute-start | bytes 1179656 | tf_op jit(solution)/shard_map/ppermute | solution.py:24
  23.7 8.8 %collective-permute-start.12 = (bf16[3,128,128]{2,1,0:T(8,128)(2,1)S(1)}, bf16[3,128,128]{2,1,0:T(8,128)(2,1)S(1)}, u32[]{:S(2)}, u32[]{:S(2)}) collective-permute-start(bf16[3,128,128]{2,1,0:T(8,128)(2,1)S(1)} %get-tuple-element.21), channel_id=1, source_target_pairs={{0,3},{1,2},{2,1},{3,0},{4,7},{5,6},{6,5},{7,4},{8,11},{9,10},{10,... | collective-permute-start | bytes 294920 | tf_op jit(solution)/shard_map/ppermute | solution.py:24
  26.1 7.6 %collective-permute-start.11 = (bf16[3,128,128]{2,1,0:T(8,128)(2,1)S(1)}, bf16[3,128,128]{2,1,0:T(8,128)(2,1)S(1)}, u32[]{:S(2)}, u32[]{:S(2)}) collective-permute-start(bf16[3,128,128]{2,1,0:T(8,128)(2,1)S(1)} %get-tuple-element.21), channel_id=1, source_target_pairs={{0,2},{1,3},{2,0},{3,1},{4,6},{5,7},{6,4},{7,5},{8,10},{9,11},{10,... | collective-permute-start | bytes 294920 | tf_op jit(solution)/shard_map/ppermute | solution.py:24
  26.1 7.6 %collective-permute-start.10 = (bf16[3,128,128]{2,1,0:T(8,128)(2,1)S(1)}, bf16[3,128,128]{2,1,0:T(8,128)(2,1)S(1)}, u32[]{:S(2)}, u32[]{:S(2)}) collective-permute-start(bf16[3,128,128]{2,1,0:T(8,128)(2,1)S(1)} %get-tuple-element.21), channel_id=1, source_target_pairs={{0,1},{1,0},{2,3},{3,2},{4,5},{5,4},{6,7},{7,6},{8,9},{9,8},{10,11... | collective-permute-start | bytes 294920 | tf_op jit(solution)/shard_map/ppermute | solution.py:24
  32.5 5.3 %copy-start.1 = (s32[2,8]{1,0:T(2,128)S(1)}, s32[2,8]{1,0:T(2,128)}, u32[]{:S(2)}) copy-start(s32[2,8]{1,0:T(2,128)} %pair.1) | copy-start | bytes 196
  33.8 4.0 %collective-permute-start.13 = (bf16[16,128,128]{2,1,0:T(8,128)(2,1)S(1)}, bf16[16,128,128]{2,1,0:T(8,128)(2,1)S(1)}, u32[]{:S(2)}, u32[]{:S(2)}) collective-permute-start(bf16[16,128,128]{2,1,0:T(8,128)(2,1)S(1)} %collect.1.refs_0_), channel_id=1, source_target_pairs={{0,4},{4,0},{8,12},{12,8},{16,20},{20,16},{24,28},{28,24},{1,5},{5... | collective-permute-start | bytes 1572872 | tf_op jit(solution)/shard_map/ppermute | solution.py:24
  33.9 11.0 %collective-permute-start.9 = (bf16[3,256,128]{2,1,0:T(8,128)(2,1)S(1)}, bf16[3,256,128]{2,1,0:T(8,128)(2,1)S(1)}, u32[]{:S(2)}, u32[]{:S(2)}) collective-permute-start(bf16[3,256,128]{2,1,0:T(8,128)(2,1)S(1)} %slice.9), channel_id=1, source_target_pairs={{0,8},{4,12},{8,0},{12,4},{16,24},{20,28},{24,16},{28,20},{1,9},{5... | collective-permute-start | bytes 589832 | tf_op jit(solution)/shard_map/ppermute | solution.py:24
  36.1 8.8 %collective-permute-start.7 = (bf16[3,256,128]{2,1,0:T(8,128)(2,1)}, bf16[3,256,128]{2,1,0:T(8,128)(2,1)S(1)}, u32[]{:S(2)}, u32[]{:S(2)}) collective-permute-start(bf16[3,256,128]{2,1,0:T(8,128)(2,1)} %slice.8), channel_id=1, source_target_pairs={{0,16},{4,20},{8,24},{12,28},{16,0},{20,4},{24,8},{28,12},{1,17},{... | collective-permute-start | bytes 589832 | tf_op jit(solution)/shard_map/ppermute | solution.py:24
  44.9 6.6 %slice-start = ((s8[8388608]{0:T(1024)(128)(4,1)}), s8[4194304]{0:T(1024)(128)(4,1)S(1)}, s32[]{:S(2)}) async-start(s8[8388608]{0:T(1024)(128)(4,1)} %bitcast.3), calls=%async_computation | async-start | bytes 8388608
  47.3 4.2 %collective-permute-start.14 = (bf16[8,32,4096]{2,1,0:T(8,128)(2,1)S(1)}, bf16[8,32,4096]{2,1,0:T(8,128)(2,1)S(1)}, u32[]{:S(2)}, u32[]{:S(2)}) collective-permute-start(bf16[8,32,4096]{2,1,0:T(8,128)(2,1)S(1)} %transform.1.refs_3_), channel_id=1, source_target_pairs={{0,4},{4,0},{8,12},{12,8},{16,20},{20,16},{24,28},{28,24},{1,5},{5... | collective-permute-start | bytes 6291464 | tf_op jit(solution)/shard_map/ppermute | solution.py:24
  47.4 4.1 %slice-start.1 = ((s8[8388608]{0:T(1024)(128)(4,1)}), s8[4194304]{0:T(1024)(128)(4,1)S(1)}, s32[]{:S(2)}) async-start(s8[8388608]{0:T(1024)(128)(4,1)} %bitcast.3), calls=%async_computation.1 | async-start | bytes 8388608
  47.4 4.7 %copy-start = (bf16[8,64,4096]{2,1,0:T(8,128)(2,1)S(1)}, bf16[8,64,4096]{2,1,0:T(8,128)(2,1)}, u32[]{:S(2)}) copy-start(bf16[8,64,4096]{2,1,0:T(8,128)(2,1)} %reorder.4.refs_10_.refs_1_) | copy-start | bytes 12582916

commit v5 on v4

--- a/solution.py
+++ b/solution.py
@@ -415,7 +415,9 @@
 
     own, padded = pack(b_rows, g_occ, g_virt)
 
-    side = [swap(own, "aux", na, e) for e in outer[1:]]
+    side = [swap(own, "aux", na, e) for e in outer[2:]]
+    side[0], late = lax.optimization_barrier((side[0], own))
+    side = [swap(late, "aux", na, outer[1])] + side
     column = [swap(padded, "pair", nz, d) for d in range(1, nz)]
     slabs = [reorder(b_slab, 0, 2, 4, pltpu.HBM)]
     b_z, g_side = stack(column, side, split, k_local, [in_hbm(slabs[0])])

time: 57.9 us -> 56.9 us (0.983)
  starting transfers between devices: 18.5 us -> 17.9 us
    ppermute x15, starting transfers between devices: 18.5 us -> 17.9 us  [swap(): return lax.ppermute(value, axis, [(i, i ^ offset) for i in range(size)])]
  transfers between devices with their start and end apart: 15 -> 15, of which waited for: 3 -> 3; matrix products, arithmetic and copies ran while one was open for 1% -> 1% of each run, Pallas kernels for 40% -> 41%
where the time goes in v5:
time: 56.9 us; the launch traced here: 56.8 us
  Pallas kernels  32.2 us (57%)
  starting transfers between devices  17.9 us (31%)
  waiting for transfers between devices  5.08 us (9%)
  local copies, waits for them, and re-layouts  1.34 us (2%)
    ppermute x15, starting transfers between devices, swap(): return lax.ppermute(value, axis, [(i, i ^ offset) for i in range(size)])  17.9 us
    pallas_call x3, Pallas kernels, reorder(): pl.pallas_call(reorder_kernel, grid=(steps,), in_specs=[pl.BlockSpec((q,...  16.1 us
    pallas_call x1, Pallas kernels, prepare(): pl.pallas_call(functools.partial(prepare_kernel, layout, rows, len(g_bloc...  7.18 us
    pallas_call x1, Pallas kernels, contract(): pl.pallas_call(functools.partial(contract_kernel, parts), in_specs=[IN_VM...  5.51 us
    ppermute x15, waiting for transfers between devices, swap(): return lax.ppermute(value, axis, [(i, i ^ offset) for i in range(size)])  5.08 us
    pallas_call x1, Pallas kernels, transform(): pl.pallas_call(functools.partial(transform_kernel, layout, rows), grid=(n...  2.38 us
  transfers between devices with their start and end apart: 15, of which 3 were waited for; matrix products, arithmetic and copies ran while one was open for 1% of the time, Pallas kernels for 41%

profile of v5, /device:TPU:0, one launch (start us, length us, event | category | flops | bytes accessed | tf_op | source)
XLA Modules:
  0.0 56.8 jit_solution(11652254470610875312)
XLA Ops:
  0.0 1.0 %pack.1 = (bf16[640,128]{1,0:T(8,128)(2,1)S(1)}, bf16[656,128]{1,0:T(8,128)(2,1)S(1)}) custom-call(bf16[8,2,4096]{2,1,0:T(2,128)(2,1)} %b_in.1, bf16[16,512]{1,0:T(8,128)(2,1)} %occ_in.1, bf16[16,512]{1,0:T(8,128)(2,1)} %virt_in.1), custom_call_target="tpu_custom_call" | custom-call | tf_op jit(solution)/shard_map/pack/pallas_call | solution.py:324
  1.0 3.0 %collective-permute-start.3 = (bf16[640,128]{1,0:T(8,128)(2,1)S(1)}, bf16[640,128]{1,0:T(8,128)(2,1)S(1)}, u32[]{:S(2)}, u32[]{:S(2)}) collective-permute-start(bf16[640,128]{1,0:T(8,128)(2,1)S(1)} %get-tuple-element.20.refs_0_.refs_2_), channel_id=1, source_target_pairs={{0,16},{4,20},{8,24},{12,28},{16,0},{20,4},{24,8},{28,12},{1,17},{... | collective-permute-start | bytes 491528 | tf_op jit(solution)/shard_map/ppermute | solution.py:24
  4.0 3.6 %collective-permute-start.2 = (bf16[656,128]{1,0:T(8,128)(2,1)S(1)}, bf16[656,128]{1,0:T(8,128)(2,1)S(1)}, u32[]{:S(2)}, u32[]{:S(2)}) collective-permute-start(bf16[656,128]{1,0:T(8,128)(2,1)S(1)} %get-tuple-element.18), channel_id=1, source_target_pairs={{0,3},{1,2},{2,1},{3,0},{4,7},{5,6},{6,5},{7,4},{8,11},{9,10},{10,... | collective-permute-start | bytes 503816 | tf_op jit(solution)/shard_map/ppermute | solution.py:24
  7.6 0.8 %collective-permute-start = (bf16[656,128]{1,0:T(8,128)(2,1)S(1)}, bf16[656,128]{1,0:T(8,128)(2,1)S(1)}, u32[]{:S(2)}, u32[]{:S(2)}) collective-permute-start(bf16[656,128]{1,0:T(8,128)(2,1)S(1)} %get-tuple-element.18), channel_id=1, source_target_pairs={{0,1},{1,0},{2,3},{3,2},{4,5},{5,4},{6,7},{7,6},{8,9},{9,8},{10,11... | collective-permute-start | bytes 503816 | tf_op jit(solution)/shard_map/ppermute | solution.py:24
  8.4 1.4 %collective-permute-start.5 = (bf16[640,128]{1,0:T(8,128)(2,1)S(1)}, bf16[640,128]{1,0:T(8,128)(2,1)S(1)}, u32[]{:S(2)}, u32[]{:S(2)}) collective-permute-start(bf16[640,128]{1,0:T(8,128)(2,1)S(1)} %get-tuple-element.20.refs_0_.refs_2_), channel_id=1, source_target_pairs={{0,24},{4,28},{8,16},{12,20},{16,8},{20,12},{24,0},{28,4},{1,25},{... | collective-permute-start | bytes 491528 | tf_op jit(solution)/shard_map/ppermute | solution.py:24
  9.9 0.3 collective-permute-start.4
  10.2 8.3 %reorder.3.refs_6_.refs_0_ = bf16[8,128,4096]{2,1,0:T(8,128)(2,1)} custom-call(bf16[256,8,4096]{2,1,0:T(8,128)(2,1)} %slab.3), custom_call_target="tpu_custom_call" | custom-call | tf_op jit(solution)/shard_map/reorder/pallas_call | solution.py:286
  18.4 3.1 %collective-permute-done.1.refs_1_.refs_2_ = bf16[656,128]{1,0:T(8,128)(2,1)S(1)} collective-permute-done((bf16[656,128]{1,0:T(8,128)(2,1)S(1)}, bf16[656,128]{1,0:T(8,128)(2,1)S(1)}, u32[]{:S(2)}, u32[]{:S(2)}) %collective-permute-start.1) | collective-permute-done | bytes 167968 | tf_op jit(solution)/shard_map/ppermute | solution.py:24
  21.6 0.6 %collective-permute-start.8 = (bf16[6,256,128]{2,1,0:T(8,128)(2,1)S(1)}, bf16[6,256,128]{2,1,0:T(8,128)(2,1)S(1)}, u32[]{:S(2)}, u32[]{:S(2)}) collective-permute-start(bf16[6,256,128]{2,1,0:T(8,128)(2,1)S(1)} %get-tuple-element.24.refs_3_), channel_id=1, source_target_pairs={{0,16},{4,20},{8,24},{12,28},{16,0},{20,4},{24,8},{28,12},{1,17},{... | collective-permute-start | bytes 1179656 | tf_op jit(solution)/shard_map/ppermute | solution.py:24
  22.2 1.5 %collective-permute-start.6 = (bf16[6,256,128]{2,1,0:T(8,128)(2,1)S(1)}, bf16[6,256,128]{2,1,0:T(8,128)(2,1)S(1)}, u32[]{:S(2)}, u32[]{:S(2)}) collective-permute-start(bf16[6,256,128]{2,1,0:T(8,128)(2,1)S(1)} %get-tuple-element.24.refs_3_), channel_id=1, source_target_pairs={{0,8},{4,12},{8,0},{12,4},{16,24},{20,28},{24,16},{28,20},{1,9},{5... | collective-permute-start | bytes 1179656 | tf_op jit(solution)/shard_map/ppermute | solution.py:24
  23.7 2.5 %collective-permute-start.12 = (bf16[3,128,128]{2,1,0:T(8,128)(2,1)S(1)}, bf16[3,128,128]{2,1,0:T(8,128)(2,1)S(1)}, u32[]{:S(2)}, u32[]{:S(2)}) collective-permute-start(bf16[3,128,128]{2,1,0:T(8,128)(2,1)S(1)} %get-tuple-element.25), channel_id=1, source_target_pairs={{0,3},{1,2},{2,1},{3,0},{4,7},{5,6},{6,5},{7,4},{8,11},{9,10},{10,... | collective-permute-start | bytes 294920 | tf_op jit(solution)/shard_map/ppermute | solution.py:24
  26.2 1.9 %collective-permute-start.10 = (bf16[3,128,128]{2,1,0:T(8,128)(2,1)S(1)}, bf16[3,128,128]{2,1,0:T(8,128)(2,1)S(1)}, u32[]{:S(2)}, u32[]{:S(2)}) collective-permute-start(bf16[3,128,128]{2,1,0:T(8,128)(2,1)S(1)} %get-tuple-element.25), channel_id=1, source_target_pairs={{0,1},{1,0},{2,3},{3,2},{4,5},{5,4},{6,7},{7,6},{8,9},{9,8},{10,11... | collective-permute-start | bytes 294920 | tf_op jit(solution)/shard_map/ppermute | solution.py:24
  28.1 4.4 %reorder.4.refs_10_.refs_1_ = bf16[8,64,4096]{2,1,0:T(8,128)(2,1)} custom-call(bf16[256,8,4096]{2,1,0:T(8,128)(2,1)} %slab.3), custom_call_target="tpu_custom_call" | custom-call | tf_op jit(solution)/shard_map/reorder/pallas_call | solution.py:286
  32.5 1.2 %collective-permute-done.11.refs_8_ = bf16[3,128,128]{2,1,0:T(8,128)(2,1)S(1)} collective-permute-done((bf16[3,128,128]{2,1,0:T(8,128)(2,1)S(1)}, bf16[3,128,128]{2,1,0:T(8,128)(2,1)S(1)}, u32[]{:S(2)}, u32[]{:S(2)}) %collective-permute-start.11) | collective-permute-done | bytes 98336 | tf_op jit(solution)/shard_map/ppermute | solution.py:24
  33.9 0.6 %collective-permute-start.9 = (bf16[3,256,128]{2,1,0:T(8,128)(2,1)S(1)}, bf16[3,256,128]{2,1,0:T(8,128)(2,1)S(1)}, u32[]{:S(2)}, u32[]{:S(2)}) collective-permute-start(bf16[3,256,128]{2,1,0:T(8,128)(2,1)S(1)} %slice.9), channel_id=1, source_target_pairs={{0,8},{4,12},{8,0},{12,4},{16,24},{20,28},{24,16},{28,20},{1,9},{5... | collective-permute-start | bytes 589832 | tf_op jit(solution)/shard_map/ppermute | solution.py:24
  34.5 0.7 %slice.8 = bf16[3,256,128]{2,1,0:T(8,128)(2,1)} slice(bf16[6,256,128]{2,1,0:T(8,128)(2,1)S(1)} %collective-permute-done.6.refs_11_.refs_5_), slice={[0:3], [0:256], [0:128]} | slice | bytes 393216 | tf_op jit(solution)/shard_map/slice | solution.py:431
  35.2 1.5 %collective-permute-start.7 = (bf16[3,256,128]{2,1,0:T(8,128)(2,1)}, bf16[3,256,128]{2,1,0:T(8,128)(2,1)S(1)}, u32[]{:S(2)}, u32[]{:S(2)}) collective-permute-start(bf16[3,256,128]{2,1,0:T(8,128)(2,1)} %slice.8), channel_id=1, source_target_pairs={{0,16},{4,20},{8,24},{12,28},{16,0},{20,4},{24,8},{28,12},{1,17},{... | collective-permute-start | bytes 589832 | tf_op jit(solution)/shard_map/ppermute | solution.py:24
  36.7 0.1 pad_add_fusion.me
  36.8 7.2 %prepare.1 = (bf16[8,128,256]{2,1,0:T(8,128)(2,1)S(1)}, bf16[1024,1024]{1,0:T(8,128)(2,1)S(1)}, bf16[8,24,4096]{2,1,0:T(8,128)(2,1)S(1)}) custom-call(s32[2]{0:T(128)S(1)} %pad_add_fusion.me, s32[2,8]{1,0:T(2,128)S(1)} %copy-done.1, bf16[16,128,128]{2,1,0:T(8,128)(2,1)S(1)} %collect.1.refs_0_, bf16[16,128,128]{2,1,0:T(8,128)(2,1)S(1)} %collective-permute-done.13.refs_1_, ...), custom_call_target="tpu_custom_call" | custom-call | tf_op jit(solution)/shard_map/prepare/pallas_call | solution.py:252
  44.0 2.4 %transform.1.refs_3_ = bf16[8,32,4096]{2,1,0:T(8,128)(2,1)S(1)} custom-call(bf16[640,128]{1,0:T(8,128)(2,1)S(1)} %collective-permute-done.5.refs_5_.refs_6_.refs_0_, bf16[3,256,128]{2,1,0:T(8,128)(2,1)S(1)} %collective-permute-done.7.refs_1_, bf16[3,256,128]{2,1,0:T(8,128)(2,1)S(1)} %collective-permute-done.9.refs_2_, ...), custom_call_target="tpu_custom_call" | custom-call | tf_op jit(solution)/shard_map/transform/pallas_call | solution.py:216
  46.5 3.4 %reorder.5.refs_2_ = bf16[8,64,4096]{2,1,0:T(8,128)(2,1)S(1)} custom-call(bf16[256,8,4096]{2,1,0:T(8,128)(2,1)} %slab.3), custom_call_target="tpu_custom_call" | custom-call | tf_op jit(solution)/shard_map/reorder/pallas_call | solution.py:286
  50.0 0.7 %collective-permute-done.14.refs_4_ = bf16[8,32,4096]{2,1,0:T(8,128)(2,1)S(1)} collective-permute-done((bf16[8,32,4096]{2,1,0:T(8,128)(2,1)S(1)}, bf16[8,32,4096]{2,1,0:T(8,128)(2,1)S(1)}, u32[]{:S(2)}, u32[]{:S(2)}) %collective-permute-start.14) | collective-permute-done | bytes 2097184 | tf_op jit(solution)/shard_map/ppermute | solution.py:24
  50.6 0.6 %copy-done = bf16[8,64,4096]{2,1,0:T(8,128)(2,1)S(1)} copy-done((bf16[8,64,4096]{2,1,0:T(8,128)(2,1)S(1)}, bf16[8,64,4096]{2,1,0:T(8,128)(2,1)}, u32[]{:S(2)}) %copy-start) | copy-done | bytes 4194328
  51.2 5.5 %contract.1 = f32[64,256]{1,0:T(8,128)} custom-call(f32[64,64]{1,0:T(8,128)S(1)} %fusion.place, bf16[8,128,4096]{2,1,0:T(8,128)(2,1)S(1)} %bitcast.4, bf16[8,64,4096]{2,1,0:T(8,128)(2,1)S(1)} %copy-done, bf16[8,64,4096]{2,1,0:T(8,128)(2,1)S(1)} %reorder.5.refs_2_, bf16[8,32,4096]{2,1,0:T(8,128)(2,1)S(1)} %transform.1.refs_3_, ...), custom_call_target="tpu_custom_call" | custom-call | tf_op jit(solution)/shard_map/contract/pallas_call | solution.py:398
  (29 shorter events, 0.3 us)
Async XLA Ops:
  1.0 8.9 %collective-permute-start.3 = (bf16[640,128]{1,0:T(8,128)(2,1)S(1)}, bf16[640,128]{1,0:T(8,128)(2,1)S(1)}, u32[]{:S(2)}, u32[]{:S(2)}) collective-permute-start(bf16[640,128]{1,0:T(8,128)(2,1)S(1)} %get-tuple-element.20.refs_0_.refs_2_), channel_id=1, source_target_pairs={{0,16},{4,20},{8,24},{12,28},{16,0},{20,4},{24,8},{28,12},{1,17},{... | collective-permute-start | bytes 491528 | tf_op jit(solution)/shard_map/ppermute | solution.py:24
  4.0 14.4 %collective-permute-start.2 = (bf16[656,128]{1,0:T(8,128)(2,1)S(1)}, bf16[656,128]{1,0:T(8,128)(2,1)S(1)}, u32[]{:S(2)}, u32[]{:S(2)}) collective-permute-start(bf16[656,128]{1,0:T(8,128)(2,1)S(1)} %get-tuple-element.18), channel_id=1, source_target_pairs={{0,3},{1,2},{2,1},{3,0},{4,7},{5,6},{6,5},{7,4},{8,11},{9,10},{10,... | collective-permute-start | bytes 503816 | tf_op jit(solution)/shard_map/ppermute | solution.py:24
  7.6 14.0 %collective-permute-start.1 = (bf16[656,128]{1,0:T(8,128)(2,1)S(1)}, bf16[656,128]{1,0:T(8,128)(2,1)S(1)}, u32[]{:S(2)}, u32[]{:S(2)}) collective-permute-start(bf16[656,128]{1,0:T(8,128)(2,1)S(1)} %get-tuple-element.18), channel_id=1, source_target_pairs={{0,2},{1,3},{2,0},{3,1},{4,6},{5,7},{6,4},{7,5},{8,10},{9,11},{10,... | collective-permute-start | bytes 503816 | tf_op jit(solution)/shard_map/ppermute | solution.py:24
  7.6 14.0 %collective-permute-start = (bf16[656,128]{1,0:T(8,128)(2,1)S(1)}, bf16[656,128]{1,0:T(8,128)(2,1)S(1)}, u32[]{:S(2)}, u32[]{:S(2)}) collective-permute-start(bf16[656,128]{1,0:T(8,128)(2,1)S(1)} %get-tuple-element.18), channel_id=1, source_target_pairs={{0,1},{1,0},{2,3},{3,2},{4,5},{5,4},{6,7},{7,6},{8,9},{9,8},{10,11... | collective-permute-start | bytes 503816 | tf_op jit(solution)/shard_map/ppermute | solution.py:24
  8.4 10.0 %collective-permute-start.5 = (bf16[640,128]{1,0:T(8,128)(2,1)S(1)}, bf16[640,128]{1,0:T(8,128)(2,1)S(1)}, u32[]{:S(2)}, u32[]{:S(2)}) collective-permute-start(bf16[640,128]{1,0:T(8,128)(2,1)S(1)} %get-tuple-element.20.refs_0_.refs_2_), channel_id=1, source_target_pairs={{0,24},{4,28},{8,16},{12,20},{16,8},{20,12},{24,0},{28,4},{1,25},{... | collective-permute-start | bytes 491528 | tf_op jit(solution)/shard_map/ppermute | solution.py:24
  9.9 11.7 %collective-permute-start.4 = (bf16[640,128]{1,0:T(8,128)(2,1)S(1)}, bf16[640,128]{1,0:T(8,128)(2,1)S(1)}, u32[]{:S(2)}, u32[]{:S(2)}) collective-permute-start(bf16[640,128]{1,0:T(8,128)(2,1)S(1)} %get-tuple-element.20.refs_0_.refs_2_), channel_id=1, source_target_pairs={{0,8},{4,12},{8,0},{12,4},{16,24},{20,28},{24,16},{28,20},{1,9},{5... | collective-permute-start | bytes 491528 | tf_op jit(solution)/shard_map/ppermute | solution.py:24
  21.6 12.1 %collective-permute-start.8 = (bf16[6,256,128]{2,1,0:T(8,128)(2,1)S(1)}, bf16[6,256,128]{2,1,0:T(8,128)(2,1)S(1)}, u32[]{:S(2)}, u32[]{:S(2)}) collective-permute-start(bf16[6,256,128]{2,1,0:T(8,128)(2,1)S(1)} %get-tuple-element.24.refs_3_), channel_id=1, source_target_pairs={{0,16},{4,20},{8,24},{12,28},{16,0},{20,4},{24,8},{28,12},{1,17},{... | collective-permute-start | bytes 1179656 | tf_op jit(solution)/shard_map/ppermute | solution.py:24
  22.2 11.5 %collective-permute-start.6 = (bf16[6,256,128]{2,1,0:T(8,128)(2,1)S(1)}, bf16[6,256,128]{2,1,0:T(8,128)(2,1)S(1)}, u32[]{:S(2)}, u32[]{:S(2)}) collective-permute-start(bf16[6,256,128]{2,1,0:T(8,128)(2,1)S(1)} %get-tuple-element.24.refs_3_), channel_id=1, source_target_pairs={{0,8},{4,12},{8,0},{12,4},{16,24},{20,28},{24,16},{28,20},{1,9},{5... | collective-permute-start | bytes 1179656 | tf_op jit(solution)/shard_map/ppermute | solution.py:24
  23.7 8.8 %collective-permute-start.12 = (bf16[3,128,128]{2,1,0:T(8,128)(2,1)S(1)}, bf16[3,128,128]{2,1,0:T(8,128)(2,1)S(1)}, u32[]{:S(2)}, u32[]{:S(2)}) collective-permute-start(bf16[3,128,128]{2,1,0:T(8,128)(2,1)S(1)} %get-tuple-element.25), channel_id=1, source_target_pairs={{0,3},{1,2},{2,1},{3,0},{4,7},{5,6},{6,5},{7,4},{8,11},{9,10},{10,... | collective-permute-start | bytes 294920 | tf_op jit(solution)/shard_map/ppermute | solution.py:24
  26.2 7.6 %collective-permute-start.11 = (bf16[3,128,128]{2,1,0:T(8,128)(2,1)S(1)}, bf16[3,128,128]{2,1,0:T(8,128)(2,1)S(1)}, u32[]{:S(2)}, u32[]{:S(2)}) collective-permute-start(bf16[3,128,128]{2,1,0:T(8,128)(2,1)S(1)} %get-tuple-element.25), channel_id=1, source_target_pairs={{0,2},{1,3},{2,0},{3,1},{4,6},{5,7},{6,4},{7,5},{8,10},{9,11},{10,... | collective-permute-start | bytes 294920 | tf_op jit(solution)/shard_map/ppermute | solution.py:24
  26.2 7.6 %collective-permute-start.10 = (bf16[3,128,128]{2,1,0:T(8,128)(2,1)S(1)}, bf16[3,128,128]{2,1,0:T(8,128)(2,1)S(1)}, u32[]{:S(2)}, u32[]{:S(2)}) collective-permute-start(bf16[3,128,128]{2,1,0:T(8,128)(2,1)S(1)} %get-tuple-element.25), channel_id=1, source_target_pairs={{0,1},{1,0},{2,3},{3,2},{4,5},{5,4},{6,7},{7,6},{8,9},{9,8},{10,11... | collective-permute-start | bytes 294920 | tf_op jit(solution)/shard_map/ppermute | solution.py:24
  32.5 4.3 %copy-start.1 = (s32[2,8]{1,0:T(2,128)S(1)}, s32[2,8]{1,0:T(2,128)}, u32[]{:S(2)}) copy-start(s32[2,8]{1,0:T(2,128)} %pair.1) | copy-start | bytes 196
  33.8 3.0 %collective-permute-start.13 = (bf16[16,128,128]{2,1,0:T(8,128)(2,1)S(1)}, bf16[16,128,128]{2,1,0:T(8,128)(2,1)S(1)}, u32[]{:S(2)}, u32[]{:S(2)}) collective-permute-start(bf16[16,128,128]{2,1,0:T(8,128)(2,1)S(1)} %collect.1.refs_0_), channel_id=1, source_target_pairs={{0,4},{4,0},{8,12},{12,8},{16,20},{20,16},{24,28},{28,24},{1,5},{5... | collective-permute-start | bytes 1572872 | tf_op jit(solution)/shard_map/ppermute | solution.py:24
  33.9 10.1 %collective-permute-start.9 = (bf16[3,256,128]{2,1,0:T(8,128)(2,1)S(1)}, bf16[3,256,128]{2,1,0:T(8,128)(2,1)S(1)}, u32[]{:S(2)}, u32[]{:S(2)}) collective-permute-start(bf16[3,256,128]{2,1,0:T(8,128)(2,1)S(1)} %slice.9), channel_id=1, source_target_pairs={{0,8},{4,12},{8,0},{12,4},{16,24},{20,28},{24,16},{28,20},{1,9},{5... | collective-permute-start | bytes 589832 | tf_op jit(solution)/shard_map/ppermute | solution.py:24
  35.2 8.8 %collective-permute-start.7 = (bf16[3,256,128]{2,1,0:T(8,128)(2,1)}, bf16[3,256,128]{2,1,0:T(8,128)(2,1)S(1)}, u32[]{:S(2)}, u32[]{:S(2)}) collective-permute-start(bf16[3,256,128]{2,1,0:T(8,128)(2,1)} %slice.8), channel_id=1, source_target_pairs={{0,16},{4,20},{8,24},{12,28},{16,0},{20,4},{24,8},{28,12},{1,17},{... | collective-permute-start | bytes 589832 | tf_op jit(solution)/shard_map/ppermute | solution.py:24
  44.0 6.6 %slice-start = ((s8[8388608]{0:T(1024)(128)(4,1)}), s8[4194304]{0:T(1024)(128)(4,1)S(1)}, s32[]{:S(2)}) async-start(s8[8388608]{0:T(1024)(128)(4,1)} %bitcast.3), calls=%async_computation | async-start | bytes 8388608
  46.4 4.2 %collective-permute-start.14 = (bf16[8,32,4096]{2,1,0:T(8,128)(2,1)S(1)}, bf16[8,32,4096]{2,1,0:T(8,128)(2,1)S(1)}, u32[]{:S(2)}, u32[]{:S(2)}) collective-permute-start(bf16[8,32,4096]{2,1,0:T(8,128)(2,1)S(1)} %transform.1.refs_3_), channel_id=1, source_target_pairs={{0,4},{4,0},{8,12},{12,8},{16,20},{20,16},{24,28},{28,24},{1,5},{5... | collective-permute-start | bytes 6291464 | tf_op jit(solution)/shard_map/ppermute | solution.py:24
  46.5 4.1 %slice-start.1 = ((s8[8388608]{0:T(1024)(128)(4,1)}), s8[4194304]{0:T(1024)(128)(4,1)S(1)}, s32[]{:S(2)}) async-start(s8[8388608]{0:T(1024)(128)(4,1)} %bitcast.3), calls=%async_computation.1 | async-start | bytes 8388608
  46.5 4.7 %copy-start = (bf16[8,64,4096]{2,1,0:T(8,128)(2,1)S(1)}, bf16[8,64,4096]{2,1,0:T(8,128)(2,1)}, u32[]{:S(2)}) copy-start(bf16[8,64,4096]{2,1,0:T(8,128)(2,1)} %reorder.4.refs_10_.refs_1_) | copy-start | bytes 12582916
